TPU v7x, 32 devices: a whole 2x2x4 slice. The times are simulated.
32 devices in a mesh: head: 2 (over y), seq: 4 (over z), dp: 4 (over x, core).
Axes of the slice: x: 2, y: 2, z: 4, core: 2. Of those that a mesh axis runs over, the one named last changes fastest.
Arguments:
- teacher_query: bfloat16 [4, 512, 3072], P('dp', 'seq', 'head'), may hold values from -6 to 6
- teacher_key: bfloat16 [4, 512, 3072], P('dp', 'seq', 'head'), may hold values from -6 to 6
- student_query: bfloat16 [4, 512, 512], P('dp', 'seq'), may hold values from -6 to 6
- student_key: bfloat16 [4, 512, 512], P('dp', 'seq'), may hold values from -6 to 6
- head_mix: float32 [24, 8], P('head'), may hold values from 0.02 to 0.25
Outputs:
- grad_query: float32 [4, 512, 512], P('dp', 'seq', 'head')
- grad_key: float32 [4, 512, 512], P('dp', 'seq', 'head')
- grad_mix: float32 [24, 8], P('head')
- head_loss: float32 [24], P('head')
All inputs are finite; a program needn't handle non-finite values.
Results may differ from a plain program's by a relative error of at most 0.0012.
Values may be sent and summed in bfloat16 or wider, within the bound.
No kernel may reach another device: no remote copies, remote signals or barrier semaphores. Data moves between devices by JAX's collectives and lax.ppermute only.
A program may use at most 64 MiB of HBM per device.

v0:
```python
import functools
import math

import jax
import jax.numpy as jnp
from jax import lax
from jax.experimental import pallas as pl
from jax.experimental.pallas import tpu as pltpu
from jax.sharding import PartitionSpec as P

HEADS_T = 24
HD_T = 128
HEADS_S = 8
HD_S = 64
LOG2E = math.log2(math.e)
LN2 = math.log(2.0)
LIFT_BLOCK = 32
BACK_BLOCK = 16
VMEM_LIMIT = 8 * 1024 * 1024

F32 = jnp.float32
BF16 = jnp.bfloat16


def dot(lhs, rhs, dims=((1,), (0,))):
    return lax.dot_general(lhs, rhs, (dims, ((), ())), preferred_element_type=F32)


def split(value):
    high = value.astype(BF16)
    low = (value - high.astype(F32)).astype(BF16)
    return high, low


def expand_kernel(mix_ref, mix_tr_ref, lift_hi, lift_lo, back_hi, back_lo):
    def kron(values, size):
        rows, columns = values.shape
        lane = lax.broadcasted_iota(jnp.int32, (rows, columns * size), 1)
        spread = jnp.zeros((rows, columns * size), F32)
        for index in range(columns):
            inside = (lane >= index * size) & (lane < (index + 1) * size)
            spread = jnp.where(inside, values[:, index : index + 1], spread)
        full = (rows, size, columns * size)
        sub = lax.broadcasted_iota(jnp.int32, full, 1)
        within = lax.broadcasted_iota(jnp.int32, full, 2) & (size - 1)
        picked = jnp.where(sub == within, spread[:, None, :], 0.0)
        return picked.reshape(rows * size, columns * size)

    scaled = mix_ref[...] * (HD_S ** (-0.5) * LOG2E)
    lift_hi[...], lift_lo[...] = split(kron(scaled, LIFT_BLOCK))
    back_hi[...], back_lo[...] = split(kron(mix_tr_ref[...], BACK_BLOCK))


def expand_mix(head_mix):
    heads = head_mix.shape[0]
    lift = jax.ShapeDtypeStruct((heads * LIFT_BLOCK, HEADS_S * LIFT_BLOCK), BF16)
    back = jax.ShapeDtypeStruct((HEADS_S * BACK_BLOCK, heads * BACK_BLOCK), BF16)
    return pl.pallas_call(
        expand_kernel,
        out_shape=(lift, lift, back, back),
        compiler_params=pltpu.CompilerParams(vmem_limit_bytes=VMEM_LIMIT // 2),
        name="expand",
    )(head_mix, head_mix.T)


def stacked(refs, columns):
    parts = [ref[0, :, columns] for ref in refs]
    return parts[0] if len(parts) == 1 else jnp.concatenate(parts, axis=0)


def maps_kernel(row_parts, key_parts, heads, carried, *refs):
    refs = list(refs)
    query_t = [refs.pop(0) for _ in range(row_parts)]
    key_t = [refs.pop(0) for _ in range(key_parts)]
    query_s = [refs.pop(0) for _ in range(row_parts)]
    key_s = [refs.pop(0) for _ in range(key_parts)]
    before = refs.pop(0) if carried else None
    lift_hi, lift_lo, exp_t, exp_l, stu_hi, stu_lo, top, kl, lse, *turned, lifted = refs
    keys = stu_hi.shape[1]
    rows = stu_hi.shape[2]
    for index in range(HEADS_S):
        columns = slice(index * HD_S, (index + 1) * HD_S)
        student = dot(stacked(key_s, columns), stacked(query_s, columns), ((1,), (1,)))
        stu_hi[index], stu_lo[index] = split(student)
    for start in range(0, keys, LIFT_BLOCK):
        block = slice(start, start + LIFT_BLOCK)
        high = stu_hi[:, block, :].reshape(HEADS_S * LIFT_BLOCK, rows)
        low = stu_lo[:, block, :].reshape(HEADS_S * LIFT_BLOCK, rows)
        total = dot(lift_hi[...], high) + (dot(lift_hi[...], low) + dot(lift_lo[...], high))
        lifted[:, block, :] = total.reshape(heads, LIFT_BLOCK, rows)
    for head in range(heads):
        columns = slice(head * HD_T, (head + 1) * HD_T)
        teacher = dot(stacked(key_t, columns), stacked(query_t, columns), ((1,), (1,)))
        teacher = teacher * (HD_T ** (-0.5) * LOG2E)
        top_t = jnp.max(teacher, axis=0, keepdims=True)
        prob_t = jnp.exp2(teacher - top_t)
        exp_t[head] = prob_t
        mixed = lifted[head]
        kl[head : head + 1, :] = jnp.sum(prob_t * (teacher - mixed), axis=0, keepdims=True)
        top_l = jnp.max(mixed, axis=0, keepdims=True)
        prob_l = jnp.exp2(mixed - top_l)
        exp_l[head] = prob_l
        top[0, head : head + 1, :] = top_t
        top[1, head : head + 1, :] = top_l
        for which, best, prob in ((0, top_t, prob_t), (1, top_l, prob_l)):
            total = jnp.sum(prob, axis=0, keepdims=True)
            if carried:
                earlier = before[which, head : head + 1, :]
                higher = jnp.maximum(best, earlier)
                total = total * jnp.exp2(best - higher) + jnp.exp2(earlier - higher)
                best = higher
            lse[which, head : head + 1, :] = best + jnp.log2(total)
    part = rows // row_parts
    for step, ref in enumerate(turned, 1):
        for spot in range(row_parts):
            source = (spot + step) % row_parts * part
            ref[:, :, spot * part : (spot + 1) * part] = lse[:, :, source : source + part]


def back_kernel(row_parts, key_parts, blocks, heads, factor, *refs):
    refs = list(refs)
    query_s = [refs.pop(0) for _ in range(row_parts)]
    key_s = [refs.pop(0) for _ in range(key_parts)]
    lse = [refs.pop(0) for _ in range(row_parts)]
    back_hi, back_lo = refs[:2]
    maps = [refs[2 + 6 * i : 8 + 6 * i] for i in range(blocks)]
    sums, for_query, for_key, scale_t, scale_l, back, mix_acc = refs[2 + 6 * blocks :]
    keys, rows = back.shape[1:]
    part, size = rows // row_parts, keys // key_parts
    shards = for_query.shape[0] // row_parts

    lse_all = []
    for which in range(2):
        parts = [ref[which] for ref in lse]
        best = functools.reduce(jnp.maximum, parts)
        total = sum(jnp.exp2(value - best) for value in parts)
        lse_all.append(best + jnp.log2(total))
    own = lax.broadcasted_iota(jnp.int32, (heads, rows), 1) < part
    loss = jnp.where(own, lse_all[1] - lse_all[0], 0.0)
    mix_acc[...] = jnp.zeros_like(mix_acc)
    offset = 0
    for exp_t, exp_l, stu_hi, stu_lo, top, kl in maps:
        scale_t[...] = jnp.exp2(top[0] - lse_all[0])
        scale_l[...] = jnp.exp2(top[1] - lse_all[1])
        loss = loss + scale_t[...] * kl[...]
        for start in range(0, exp_t.shape[1], LIFT_BLOCK):
            block = slice(start, start + LIFT_BLOCK)
            excess = (
                exp_l[:, block, :] * scale_l[...][:, None, :] - exp_t[:, block, :] * scale_t[...][:, None, :]
            )
            high, low = split(excess)
            s_high = stu_hi[:, block, :].reshape(HEADS_S * LIFT_BLOCK, rows)
            s_low = stu_lo[:, block, :].reshape(HEADS_S * LIFT_BLOCK, rows)
            f_high = high.reshape(heads * LIFT_BLOCK, rows)
            f_low = low.reshape(heads * LIFT_BLOCK, rows)
            over_rows = ((1,), (1,))
            mix_acc[...] += dot(f_high, s_high, over_rows) + (
                dot(f_high, s_low, over_rows) + dot(f_low, s_high, over_rows)
            )
            for inner in range(0, LIFT_BLOCK, BACK_BLOCK):
                b_high = high[:, inner : inner + BACK_BLOCK, :].reshape(heads * BACK_BLOCK, rows)
                b_low = low[:, inner : inner + BACK_BLOCK, :].reshape(heads * BACK_BLOCK, rows)
                total = dot(back_hi[...], b_high) + (dot(back_hi[...], b_low) + dot(back_lo[...], b_high))
                first = offset + start + inner
                back[:, first : first + BACK_BLOCK, :] = total.astype(BF16).reshape(HEADS_S, BACK_BLOCK, rows)
        offset += exp_t.shape[1]
    loss = jnp.sum(loss, axis=1, keepdims=True) * LN2

    acc = mix_acc[...].reshape(heads, LIFT_BLOCK, HEADS_S * LIFT_BLOCK)
    sub = lax.broadcasted_iota(jnp.int32, acc.shape, 1)
    within = lax.broadcasted_iota(jnp.int32, acc.shape, 2) & (LIFT_BLOCK - 1)
    diagonal = jnp.sum(jnp.where(sub == within, acc, 0.0), axis=1)
    lane = lax.broadcasted_iota(jnp.int32, diagonal.shape, 1)
    slot = lax.broadcasted_iota(jnp.int32, sums.shape[1:], 1)
    packed = jnp.where(slot == HEADS_S, loss, 0.0)
    for index in range(HEADS_S):
        inside = (lane >= index * LIFT_BLOCK) & (lane < (index + 1) * LIFT_BLOCK)
        column = jnp.sum(jnp.where(inside, diagonal, 0.0), axis=1, keepdims=True)
        packed = jnp.where(slot == index, column, packed)
    sums[...] = jnp.broadcast_to(packed[None], sums.shape)

    place = lax.axis_index("seq")
    across, along = lax.rem(place, row_parts), lax.div(place, row_parts)
    per = HEADS_S // shards
    for index in range(HEADS_S):
        columns = slice(index * HD_S, (index + 1) * HD_S)
        tile = back[index]
        on_keys = dot(tile, stacked(query_s, columns)) * factor
        on_rows = dot(tile, stacked(key_s, columns), ((0,), (0,))) * factor
        shard, inside = index // per, slice(index % per * HD_S, (index % per + 1) * HD_S)
        for spot in range(row_parts):
            owner = shard * row_parts + lax.rem(across + spot, row_parts)
            for_query[owner, :, inside] = on_rows[spot * part : (spot + 1) * part]
        for spot in range(key_parts):
            owner = shard * key_parts + lax.rem(along + spot, key_parts)
            for_key[owner, :, inside] = on_keys[spot * size : (spot + 1) * size]


def finish_kernel(on_rows, on_keys, grad_query, grad_key):
    grad_query[0] = sum([on_rows[i] for i in range(1, on_rows.shape[0])], on_rows[0])
    grad_key[0] = sum([on_keys[i] for i in range(1, on_keys.shape[0])], on_keys[0])


def body(teacher_query, teacher_key, student_query, student_key, head_mix):
    shard_rows = teacher_query.shape[1]
    heads = head_mix.shape[0]
    length = lax.axis_size("seq")
    shards = lax.axis_size("head")
    copies = lax.axis_size("dp")
    row_parts = max(size for size in range(1, math.isqrt(length) + 1) if length % size == 0)
    key_parts = length // row_parts
    rows, keys = row_parts * shard_rows, key_parts * shard_rows

    def along_rows(position, step):
        return position // row_parts * row_parts + (position % row_parts + step) % row_parts

    def along_keys(position, step):
        return (position + step * row_parts) % length

    def fetch(value, target, step):
        return lax.ppermute(value, "seq", [(target(i, step), i) for i in range(length)])

    def swap(value, groups):
        return lax.all_to_all(value, ("head", "seq"), 0, 0, axis_index_groups=groups, tiled=True)

    key_s = [student_key] + [fetch(student_key, along_keys, d) for d in range(1, key_parts)]
    query_s = [student_query] + [fetch(student_query, along_rows, d) for d in range(1, row_parts)]
    key_t = [teacher_key] + [fetch(teacher_key, along_keys, d) for d in range(1, key_parts)]
    query_t = [teacher_query] + [fetch(teacher_query, along_rows, d) for d in range(1, row_parts)]
    lift_hi, lift_lo, back_hi, back_lo = expand_mix(head_mix)

    def maps(block_t, block_s, before):
        count = len(block_t)
        size = count * shard_rows
        exponents = pltpu.VMEM((heads, size, rows), F32)
        student = pltpu.VMEM((HEADS_S, size, rows), BF16)
        stats = pltpu.VMEM((2, heads, rows), F32)
        cells = heads * size * rows
        return pl.pallas_call(
            functools.partial(maps_kernel, row_parts, count, heads, bool(before)),
            out_shape=(exponents, exponents, student, student, stats, pltpu.VMEM((heads, rows), F32))
            + (stats,) * row_parts,
            scratch_shapes=[pltpu.VMEM((heads, size, rows), F32)],
            compiler_params=pltpu.CompilerParams(vmem_limit_bytes=VMEM_LIMIT),
            cost_estimate=pl.CostEstimate(
                flops=cells * 2 * (HD_T + 3 * LIFT_BLOCK * HEADS_S), bytes_accessed=cells * 8, transcendentals=cells * 2
            ),
            name="maps",
        )(*query_t, *block_t, *query_s, *block_s, *before, lift_hi, lift_lo)

    done, before = [], []
    for block in (slice(0, 1), slice(1, key_parts)):
        if key_t[block]:
            results = maps(key_t[block], key_s[block], before)
            done.append(results[:6])
            before, turned = results[6:7], results[7:]
    lse_parts = [*before] + [fetch(turned[step - 1], along_rows, row_parts - step) for step in range(1, row_parts)]

    weight = shard_rows * length / HEADS_T
    width = HEADS_S * HD_S // shards
    peers = length * copies
    sums, for_query, for_key = pl.pallas_call(
        functools.partial(back_kernel, row_parts, key_parts, len(done), heads, weight * HD_S ** (-0.5)),
        out_shape=(
            jax.ShapeDtypeStruct((peers, heads, 128), F32),
            jax.ShapeDtypeStruct((shards * row_parts, shard_rows, width), F32),
            jax.ShapeDtypeStruct((shards * key_parts, shard_rows, width), F32),
        ),
        scratch_shapes=[
            pltpu.VMEM((heads, rows), F32),
            pltpu.VMEM((heads, rows), F32),
            pltpu.VMEM((HEADS_S, keys, rows), BF16),
            pltpu.VMEM((heads * LIFT_BLOCK, HEADS_S * LIFT_BLOCK), F32),
        ],
        compiler_params=pltpu.CompilerParams(vmem_limit_bytes=VMEM_LIMIT),
        name="back",
    )(*query_s, *key_s, *lse_parts, back_hi, back_lo, *[ref for block in done for ref in block])

    row_groups = [
        [h * length + a * row_parts + b for h in range(shards) for b in range(row_parts)] for a in range(key_parts)
    ]
    key_groups = [
        [h * length + a * row_parts + b for h in range(shards) for a in range(key_parts)] for b in range(row_parts)
    ]
    for_query = swap(for_query, row_groups)
    for_key = swap(for_key, key_groups)
    grad = jax.ShapeDtypeStruct((1, shard_rows, width), F32)
    grad_query, grad_key = pl.pallas_call(
        finish_kernel,
        out_shape=(grad, grad),
        compiler_params=pltpu.CompilerParams(vmem_limit_bytes=VMEM_LIMIT),
        name="finish",
    )(for_query, for_key)
    total = jnp.sum(lax.all_to_all(sums, ("seq", "dp"), 0, 0, tiled=True), axis=0)
    samples = copies * teacher_query.shape[0] * shard_rows * length
    grad_mix = total[:, :HEADS_S] * (HD_S ** (-0.5) * weight / samples)
    head_loss = total[:, HEADS_S] / samples
    return (grad_query, grad_key, grad_mix, head_loss)


def solution(mesh):
    return jax.shard_map(
        body,
        mesh=mesh,
        in_specs=(
            P("dp", "seq", "head"),
            P("dp", "seq", "head"),
            P("dp", "seq", None),
            P("dp", "seq", None),
            P("head", None),
        ),
        out_specs=(P("dp", "seq", "head"), P("dp", "seq", "head"), P("head", None), P("head")),
        check_vma=False,
    )
```

profile of v0, /device:TPU:0, one launch (start us, length us, event | category | flops | bytes accessed | tf_op | source)
XLA Modules:
  0.0 84.1 jit_solution(6715843880768380263)
XLA Ops:
  0.6 3.1 %collective-permute-start.2 = (bf16[1,128,1536]{2,1,0:T(8,128)(2,1)}, bf16[1,128,1536]{2,1,0:T(8,128)(2,1)S(1)}, u32[]{:S(2)}, u32[]{:S(2)}) collective-permute-start(bf16[1,128,1536]{2,1,0:T(8,128)(2,1)} %refs_0_.4), channel_id=1, source_target_pairs={{4,0},{0,4},{12,8},{8,12},{5,1},{1,5},{13,9},{9,13},{6,2},{2,6},{1... | collective-permute-start | bytes 1179656 | tf_op jit(solution)/shard_map/ppermute | solution.py:221
  3.7 2.6 %collective-permute-start.3 = (bf16[1,128,1536]{2,1,0:T(8,128)(2,1)}, bf16[1,128,1536]{2,1,0:T(8,128)(2,1)S(1)}, u32[]{:S(2)}, u32[]{:S(2)}) collective-permute-start(bf16[1,128,1536]{2,1,0:T(8,128)(2,1)} %refs_2_.2), channel_id=1, source_target_pairs={{8,0},{12,4},{0,8},{4,12},{9,1},{13,5},{1,9},{5,13},{10,2},{14,6},... | collective-permute-start | bytes 1179656 | tf_op jit(solution)/shard_map/ppermute | solution.py:221
  6.3 0.4 collective-permute-start
  6.8 0.0 collective-permute-start.1
  6.8 0.8 copy.12.mix_ref
  7.5 0.7 copy-done.4
  8.2 0.2 expand.1
  8.4 17.7 %collective-permute-done.refs_4_.refs_1_ = bf16[1,128,512]{2,1,0:T(8,128)(2,1)S(1)} collective-permute-done((bf16[1,128,512]{2,1,0:T(8,128)(2,1)}, bf16[1,128,512]{2,1,0:T(8,128)(2,1)S(1)}, u32[]{:S(2)}, u32[]{:S(2)}) %collective-permute-start) | collective-permute-done | bytes 131104 | tf_op jit(solution)/shard_map/ppermute | solution.py:221
  26.2 0.9 %copy-done = bf16[1,128,512]{2,1,0:T(8,128)(2,1)S(1)} copy-done((bf16[1,128,512]{2,1,0:T(8,128)(2,1)S(1)}, bf16[1,128,512]{2,1,0:T(8,128)(2,1)}, u32[]{:S(2)}) %copy-start) | copy-done | bytes 131096
  27.1 0.9 %copy-done.2 = bf16[1,128,512]{2,1,0:T(8,128)(2,1)S(1)} copy-done((bf16[1,128,512]{2,1,0:T(8,128)(2,1)S(1)}, bf16[1,128,512]{2,1,0:T(8,128)(2,1)}, u32[]{:S(2)}) %copy-start.2) | copy-done | bytes 131096
  28.0 1.0 %copy-done.5 = bf16[1,128,1536]{2,1,0:T(8,128)(2,1)S(1)} copy-done((bf16[1,128,1536]{2,1,0:T(8,128)(2,1)S(1)}, bf16[1,128,1536]{2,1,0:T(8,128)(2,1)}, u32[]{:S(2)}) %copy-start.5) | copy-done | bytes 393240
  29.0 1.0 %copy-done.6 = bf16[1,128,1536]{2,1,0:T(8,128)(2,1)S(1)} copy-done((bf16[1,128,1536]{2,1,0:T(8,128)(2,1)S(1)}, bf16[1,128,1536]{2,1,0:T(8,128)(2,1)}, u32[]{:S(2)}) %copy-start.6) | copy-done | bytes 393240
  30.0 2.6 %maps.2 = (f32[12,128,256]{2,1,0:T(8,128)S(1)}, f32[12,128,256]{2,1,0:T(8,128)S(1)}, bf16[8,128,256]{2,1,0:T(8,128)(2,1)S(1)}, bf16[8,128,256]{2,1,0:T(8,128)(2,...) custom-call(bf16[1,128,1536]{2,1,0:T(8,128)(2,1)S(1)} %copy-done.6, ...), custom_call_target="tpu_custom_call" | custom-call | flops 704643072 | bytes 3145728 | tf_op jit(solution)/shard_map/maps/pallas_call | solution.py:239
  32.6 2.0 %maps.3 = (f32[12,128,256]{2,1,0:T(8,128)S(1)}, f32[12,128,256]{2,1,0:T(8,128)S(1)}, bf16[8,128,256]{2,1,0:T(8,128)(2,1)S(1)}, bf16[8,128,256]{2,1,0:T(8,128)(2,...) custom-call(bf16[1,128,1536]{2,1,0:T(8,128)(2,1)S(1)} %copy-done.6, ...), custom_call_target="tpu_custom_call" | custom-call | flops 704643072 | bytes 3145728 | tf_op jit(solution)/shard_map/maps/pallas_call | solution.py:239
  34.6 1.1 %collective-permute-start.4 = (f32[2,12,256]{2,1,0:T(8,128)S(1)}, f32[2,12,256]{2,1,0:T(8,128)S(1)}, u32[]{:S(2)}, u32[]{:S(2)}) collective-permute-start(f32[2,12,256]{2,1,0:T(8,128)S(1)} %get-tuple-element.32), channel_id=1, source_target_pairs={{4,0},{0,4},{12,8},{8,12},{5,1},{1,5},{13,9},{9,13},{6,2},{2,6},{1... | collective-permute-start | bytes 73736 | tf_op jit(solution)/shard_map/ppermute | solution.py:221
  35.7 2.9 %collective-permute-done.4.refs_5_ = f32[2,12,256]{2,1,0:T(8,128)S(1)} collective-permute-done((f32[2,12,256]{2,1,0:T(8,128)S(1)}, f32[2,12,256]{2,1,0:T(8,128)S(1)}, u32[]{:S(2)}, u32[]{:S(2)}) %collective-permute-start.4) | collective-permute-done | bytes 24608 | tf_op jit(solution)/shard_map/ppermute | solution.py:221
  38.6 3.8 %back.1 = (f32[16,12,128]{2,1,0:T(8,128)S(1)}, f32[4,128,256]{2,1,0:T(8,128)S(1)}, f32[4,128,256]{2,1,0:T(8,128)}) custom-call(bf16[1,128,512]{2,1,0:T(8,128)(2,1)S(1)} %copy-done.1, bf16[1,128,512]{2,1,0:T(8,128)(2,1)S(1)} %collective-permute-done.refs_4_.refs_1_, bf16[1,128,512]{2,1,0:T(8,128)(2,1)S(1)} %copy-done.3, ...), custom_call_target="tpu_custom_call" | custom-call | tf_op jit(solution)/shard_map/back/pallas_call | solution.py:262
  42.4 13.5 %all_to_all.15 = f32[16,12,128]{2,1,0:T(8,128)S(1)} all-to-all(f32[16,12,128]{2,1,0:T(8,128)S(1)} %get-tuple-element.51), channel_id=1, replica_groups=mesh['head'=2,'seq'=4,'dp'=4] {'seq','dp'}, dimensions={0} | all-to-all | bytes 196608 | tf_op jit(solution)/shard_map/all_to_all | solution.py:294
  55.9 10.7 %all_to_all.16.on_rows = f32[4,128,256]{2,1,0:T(8,128)S(1)} all-to-all(f32[4,128,256]{2,1,0:T(8,128)S(1)} %get-tuple-element.47), channel_id=1, replica_groups={{0,4,16,20},{8,12,24,28},{1,5,17,21},{9,13,25,29},{2,6,18,22},{10,14,26..., dimensions={0} | all-to-all | bytes 1048576 | tf_op jit(solution)/shard_map/all_to_all | solution.py:224
  66.6 3.5 %all-to-all-start.1 = ((f32[4,128,256]{2,1,0:T(8,128)}), f32[4,128,256]{2,1,0:T(8,128)S(1)}, u32[]{:S(2)}, u32[]{:S(2)}) async-start(f32[4,128,256]{2,1,0:T(8,128)} %get-tuple-element.48), calls=%async_computation.1 | async-start | bytes 1048576 | tf_op jit(solution)/shard_map/all_to_all | solution.py:224
  70.1 0.7 copy.13
  70.8 0.7 fusion
  71.5 11.9 %all-to-all-done.1.on_keys = f32[4,128,256]{2,1,0:T(8,128)S(1)} async-done(((f32[4,128,256]{2,1,0:T(8,128)}), f32[4,128,256]{2,1,0:T(8,128)S(1)}, u32[]{:S(2)}, u32[]{:S(2)}) %all-to-all-start.1) | async-done | bytes 524320 | tf_op jit(solution)/shard_map/all_to_all | solution.py:224
  83.4 0.7 finish.1
  (14 shorter events, 0.1 us)
Async XLA Ops:
  0.6 25.5 %collective-permute-start.2 = (bf16[1,128,1536]{2,1,0:T(8,128)(2,1)}, bf16[1,128,1536]{2,1,0:T(8,128)(2,1)S(1)}, u32[]{:S(2)}, u32[]{:S(2)}) collective-permute-start(bf16[1,128,1536]{2,1,0:T(8,128)(2,1)} %refs_0_.4), channel_id=1, source_target_pairs={{4,0},{0,4},{12,8},{8,12},{5,1},{1,5},{13,9},{9,13},{6,2},{2,6},{1... | collective-permute-start | bytes 1179656 | tf_op jit(solution)/shard_map/ppermute | solution.py:221
  3.7 28.8 %collective-permute-start.3 = (bf16[1,128,1536]{2,1,0:T(8,128)(2,1)}, bf16[1,128,1536]{2,1,0:T(8,128)(2,1)S(1)}, u32[]{:S(2)}, u32[]{:S(2)}) collective-permute-start(bf16[1,128,1536]{2,1,0:T(8,128)(2,1)} %refs_2_.2), channel_id=1, source_target_pairs={{8,0},{12,4},{0,8},{4,12},{9,1},{13,5},{1,9},{5,13},{10,2},{14,6},... | collective-permute-start | bytes 1179656 | tf_op jit(solution)/shard_map/ppermute | solution.py:221
  6.3 19.9 %collective-permute-start = (bf16[1,128,512]{2,1,0:T(8,128)(2,1)}, bf16[1,128,512]{2,1,0:T(8,128)(2,1)S(1)}, u32[]{:S(2)}, u32[]{:S(2)}) collective-permute-start(bf16[1,128,512]{2,1,0:T(8,128)(2,1)} %refs_0_.5), channel_id=1, source_target_pairs={{4,0},{0,4},{12,8},{8,12},{5,1},{1,5},{13,9},{9,13},{6,2},{2,6},{1... | collective-permute-start | bytes 393224 | tf_op jit(solution)/shard_map/ppermute | solution.py:221
  6.8 25.8 %collective-permute-start.1 = (bf16[1,128,512]{2,1,0:T(8,128)(2,1)}, bf16[1,128,512]{2,1,0:T(8,128)(2,1)S(1)}, u32[]{:S(2)}, u32[]{:S(2)}) collective-permute-start(bf16[1,128,512]{2,1,0:T(8,128)(2,1)} %refs_2_.3), channel_id=1, source_target_pairs={{8,0},{12,4},{0,8},{4,12},{9,1},{13,5},{1,9},{5,13},{10,2},{14,6},... | collective-permute-start | bytes 393224 | tf_op jit(solution)/shard_map/ppermute | solution.py:221
  7.5 0.7 copy-start.4
  26.2 0.9 %copy-start = (bf16[1,128,512]{2,1,0:T(8,128)(2,1)S(1)}, bf16[1,128,512]{2,1,0:T(8,128)(2,1)}, u32[]{:S(2)}) copy-start(bf16[1,128,512]{2,1,0:T(8,128)(2,1)} %refs_0_.5) | copy-start | bytes 393220
  27.1 0.9 %copy-start.2 = (bf16[1,128,512]{2,1,0:T(8,128)(2,1)S(1)}, bf16[1,128,512]{2,1,0:T(8,128)(2,1)}, u32[]{:S(2)}) copy-start(bf16[1,128,512]{2,1,0:T(8,128)(2,1)} %refs_2_.3) | copy-start | bytes 393220
  28.0 1.0 %copy-start.5 = (bf16[1,128,1536]{2,1,0:T(8,128)(2,1)S(1)}, bf16[1,128,1536]{2,1,0:T(8,128)(2,1)}, u32[]{:S(2)}) copy-start(bf16[1,128,1536]{2,1,0:T(8,128)(2,1)} %refs_2_.2) | copy-start | bytes 1179652
  29.0 1.0 %copy-start.6 = (bf16[1,128,1536]{2,1,0:T(8,128)(2,1)S(1)}, bf16[1,128,1536]{2,1,0:T(8,128)(2,1)}, u32[]{:S(2)}) copy-start(bf16[1,128,1536]{2,1,0:T(8,128)(2,1)} %refs_0_.4) | copy-start | bytes 1179652
  30.0 2.6 %copy-start.1 = (bf16[1,128,512]{2,1,0:T(8,128)(2,1)S(1)}, bf16[1,128,512]{2,1,0:T(8,128)(2,1)}, u32[]{:S(2)}) copy-start(bf16[1,128,512]{2,1,0:T(8,128)(2,1)} %refs_0_.5) | copy-start | bytes 393220
  32.6 6.1 %copy-start.3 = (bf16[1,128,512]{2,1,0:T(8,128)(2,1)S(1)}, bf16[1,128,512]{2,1,0:T(8,128)(2,1)}, u32[]{:S(2)}) copy-start(bf16[1,128,512]{2,1,0:T(8,128)(2,1)} %refs_2_.3) | copy-start | bytes 393220
  34.6 4.0 %collective-permute-start.4 = (f32[2,12,256]{2,1,0:T(8,128)S(1)}, f32[2,12,256]{2,1,0:T(8,128)S(1)}, u32[]{:S(2)}, u32[]{:S(2)}) collective-permute-start(f32[2,12,256]{2,1,0:T(8,128)S(1)} %get-tuple-element.32), channel_id=1, source_target_pairs={{4,0},{0,4},{12,8},{8,12},{5,1},{1,5},{13,9},{9,13},{6,2},{2,6},{1... | collective-permute-start | bytes 73736 | tf_op jit(solution)/shard_map/ppermute | solution.py:221
  66.6 16.8 %all-to-all-start.1 = ((f32[4,128,256]{2,1,0:T(8,128)}), f32[4,128,256]{2,1,0:T(8,128)S(1)}, u32[]{:S(2)}, u32[]{:S(2)}) async-start(f32[4,128,256]{2,1,0:T(8,128)} %get-tuple-element.48), calls=%async_computation.1 | async-start | bytes 1048576 | tf_op jit(solution)/shard_map/all_to_all | solution.py:224
where the time goes:
time: 84.5 us; the launch traced here: 84.1 us
  waiting for transfers between devices  32.5 us (38%)
  blocking collectives  24.2 us (29%)
  starting transfers between devices  10.7 us (13%)
  Pallas kernels  9.35 us (11%)
  local copies, waits for them, and re-layouts  5.93 us (7%)
    ppermute x5, waiting for transfers between devices, fetch(): lax.ppermute(value, 'seq', [(target(i, step), i) for i in range(length)])  20.6 us
    all_to_all x1, blocking collectives, body(): lax.all_to_all(sums, ('seq', 'dp'), 0, 0, tiled=True)  13.5 us
    all_to_all x1, waiting for transfers between devices, swap(): lax.all_to_all(value, ('head', 'seq'), 0, 0, axis_index_groups=groups, ti...  11.9 us
    all_to_all x1, blocking collectives, swap(): lax.all_to_all(value, ('head', 'seq'), 0, 0, axis_index_groups=groups, ti...  10.7 us
    ppermute x5, starting transfers between devices, fetch(): lax.ppermute(value, 'seq', [(target(i, step), i) for i in range(length)])  7.23 us
    unnamed x16, local copies, waits for them, and re-layouts  5.93 us
    pallas_call x2, Pallas kernels, maps(): pl.pallas_call(functools.partial(maps_kernel, row_parts, count, heads, bo...  4.62 us
    pallas_call x1, Pallas kernels, body(): pl.pallas_call(functools.partial(back_kernel, row_parts, key_parts, len(d...  3.76 us
  transfers between devices with their start and end apart: 6, of which 3 were waited for; matrix products, arithmetic and copies ran while one was open for 3% of the time, Pallas kernels for 3%

commit v1 on v0

--- a/solution.py
+++ b/solution.py
@@ -16,6 +16,8 @@
 LN2 = math.log(2.0)
 LIFT_BLOCK = 32
 BACK_BLOCK = 16
+RIDE_ROWS = 16
+LANES = 128
 VMEM_LIMIT = 8 * 1024 * 1024
 
 F32 = jnp.float32
@@ -32,7 +34,13 @@
     return high, low
 
 
-def expand_kernel(mix_ref, mix_tr_ref, lift_hi, lift_lo, back_hi, back_lo):
+def prepare_kernel(count, mix_ref, mix_tr_ref, *refs):
+    sources, targets = refs[:count], refs[count : 2 * count]
+    lift_hi, lift_lo, back_hi, back_lo, semaphores = refs[2 * count :]
+    moves = [pltpu.make_async_copy(sources[i], targets[i], semaphores.at[i]) for i in range(count)]
+    for move in moves:
+        move.start()
+
     def kron(values, size):
         rows, columns = values.shape
         lane = lax.broadcasted_iota(jnp.int32, (rows, columns * size), 1)
@@ -49,18 +57,24 @@
     scaled = mix_ref[...] * (HD_S ** (-0.5) * LOG2E)
     lift_hi[...], lift_lo[...] = split(kron(scaled, LIFT_BLOCK))
     back_hi[...], back_lo[...] = split(kron(mix_tr_ref[...], BACK_BLOCK))
-
-
-def expand_mix(head_mix):
+    for move in moves:
+        move.wait()
+
+
+def prepare(head_mix, arrays):
     heads = head_mix.shape[0]
-    lift = jax.ShapeDtypeStruct((heads * LIFT_BLOCK, HEADS_S * LIFT_BLOCK), BF16)
-    back = jax.ShapeDtypeStruct((HEADS_S * BACK_BLOCK, heads * BACK_BLOCK), BF16)
+    lift = pltpu.VMEM((heads * LIFT_BLOCK, HEADS_S * LIFT_BLOCK), BF16)
+    back = pltpu.VMEM((HEADS_S * BACK_BLOCK, heads * BACK_BLOCK), BF16)
+    count = len(arrays)
+    whole = pl.BlockSpec(memory_space=pltpu.VMEM)
     return pl.pallas_call(
-        expand_kernel,
-        out_shape=(lift, lift, back, back),
+        functools.partial(prepare_kernel, count),
+        out_shape=[pltpu.VMEM(array.shape, array.dtype) for array in arrays] + [lift, lift, back, back],
+        in_specs=[whole, whole] + [pl.BlockSpec(memory_space=pl.ANY)] * count,
+        scratch_shapes=[pltpu.SemaphoreType.DMA((count,))],
         compiler_params=pltpu.CompilerParams(vmem_limit_bytes=VMEM_LIMIT // 2),
-        name="expand",
-    )(head_mix, head_mix.T)
+        name="prepare",
+    )(head_mix, head_mix.T, *arrays)
 
 
 def stacked(refs, columns):
@@ -70,10 +84,10 @@
 
 def maps_kernel(row_parts, key_parts, heads, carried, *refs):
     refs = list(refs)
+    key_t = [refs.pop(0) for _ in range(key_parts)]
     query_t = [refs.pop(0) for _ in range(row_parts)]
-    key_t = [refs.pop(0) for _ in range(key_parts)]
+    key_s = [refs.pop(0) for _ in range(key_parts)]
     query_s = [refs.pop(0) for _ in range(row_parts)]
-    key_s = [refs.pop(0) for _ in range(key_parts)]
     before = refs.pop(0) if carried else None
     lift_hi, lift_lo, exp_t, exp_l, stu_hi, stu_lo, top, kl, lse, *turned, lifted = refs
     keys = stu_hi.shape[1]
@@ -117,17 +131,17 @@
             ref[:, :, spot * part : (spot + 1) * part] = lse[:, :, source : source + part]
 
 
-def back_kernel(row_parts, key_parts, blocks, heads, factor, *refs):
+def back_kernel(row_parts, key_parts, shards, blocks, heads, factor, *refs):
     refs = list(refs)
     query_s = [refs.pop(0) for _ in range(row_parts)]
     key_s = [refs.pop(0) for _ in range(key_parts)]
     lse = [refs.pop(0) for _ in range(row_parts)]
     back_hi, back_lo = refs[:2]
     maps = [refs[2 + 6 * i : 8 + 6 * i] for i in range(blocks)]
-    sums, for_query, for_key, scale_t, scale_l, back, mix_acc = refs[2 + 6 * blocks :]
+    *outs, scale_t, scale_l, back, row_side, key_side, mix_acc = refs[2 + 6 * blocks :]
     keys, rows = back.shape[1:]
     part, size = rows // row_parts, keys // key_parts
-    shards = for_query.shape[0] // row_parts
+    sums, pieces = outs[0], outs[1:]
 
     lse_all = []
     for which in range(2):
@@ -171,34 +185,72 @@
     within = lax.broadcasted_iota(jnp.int32, acc.shape, 2) & (LIFT_BLOCK - 1)
     diagonal = jnp.sum(jnp.where(sub == within, acc, 0.0), axis=1)
     lane = lax.broadcasted_iota(jnp.int32, diagonal.shape, 1)
-    slot = lax.broadcasted_iota(jnp.int32, sums.shape[1:], 1)
+    slot = lax.broadcasted_iota(jnp.int32, (heads, LANES), 1)
     packed = jnp.where(slot == HEADS_S, loss, 0.0)
     for index in range(HEADS_S):
         inside = (lane >= index * LIFT_BLOCK) & (lane < (index + 1) * LIFT_BLOCK)
         column = jnp.sum(jnp.where(inside, diagonal, 0.0), axis=1, keepdims=True)
         packed = jnp.where(slot == index, column, packed)
-    sums[...] = jnp.broadcast_to(packed[None], sums.shape)
-
-    place = lax.axis_index("seq")
-    across, along = lax.rem(place, row_parts), lax.div(place, row_parts)
-    per = HEADS_S // shards
+    packed = jnp.concatenate([packed, jnp.zeros((LANES - heads, LANES), F32)], axis=0)
+    packed = jnp.transpose(packed)[:RIDE_ROWS]
+    sums[...] = packed
+
     for index in range(HEADS_S):
         columns = slice(index * HD_S, (index + 1) * HD_S)
-        tile = back[index]
-        on_keys = dot(tile, stacked(query_s, columns)) * factor
-        on_rows = dot(tile, stacked(key_s, columns), ((0,), (0,))) * factor
-        shard, inside = index // per, slice(index % per * HD_S, (index % per + 1) * HD_S)
-        for spot in range(row_parts):
-            owner = shard * row_parts + lax.rem(across + spot, row_parts)
-            for_query[owner, :, inside] = on_rows[spot * part : (spot + 1) * part]
-        for spot in range(key_parts):
-            owner = shard * key_parts + lax.rem(along + spot, key_parts)
-            for_key[owner, :, inside] = on_keys[spot * size : (spot + 1) * size]
-
-
-def finish_kernel(on_rows, on_keys, grad_query, grad_key):
-    grad_query[0] = sum([on_rows[i] for i in range(1, on_rows.shape[0])], on_rows[0])
-    grad_key[0] = sum([on_keys[i] for i in range(1, on_keys.shape[0])], on_keys[0])
+        row_side[index] = stacked(query_s, columns)
+        key_side[index] = stacked(key_s, columns)
+    place = lax.axis_index("head")
+    per = HEADS_S // shards
+    count = row_parts + key_parts - 1
+    for shard in range(shards):
+        own, *others = pieces[shard * count : (shard + 1) * count]
+        first = lax.rem(place + shard, shards) * per
+        for index in range(per):
+            tile = back[first + index]
+            columns = slice(index * HD_S, (index + 1) * HD_S)
+            on_keys = dot(tile, row_side[first + index]) * factor
+            on_rows = dot(tile, key_side[first + index], ((0,), (0,))) * factor
+            own[:part, columns] = on_rows[:part]
+            own[part:, columns] = on_keys[:size]
+            for spot in range(1, row_parts):
+                others[spot - 1][:part, columns] = on_rows[spot * part : (spot + 1) * part]
+            for spot in range(1, key_parts):
+                others[row_parts + spot - 2][:size, columns] = on_keys[spot * size : (spot + 1) * size]
+        for ref in others:
+            if ref.shape[0] > part:
+                ref[part:, :] = jnp.zeros((RIDE_ROWS, ref.shape[1]), F32)
+                ref[part:, :LANES] = packed
+
+
+def tally_kernel(*refs):
+    *parts, total = refs
+    value = parts[0][...]
+    for ref in parts[1:]:
+        value = value + ref[ref.shape[0] - RIDE_ROWS :, :LANES]
+    total[...] = value
+
+
+def finish_kernel(row_parts, key_parts, *refs):
+    *pieces, grad_query, grad_key = refs
+    part = grad_query.shape[1]
+    count = row_parts + key_parts - 1
+    on_rows, on_keys = [], []
+    for i, ref in enumerate(pieces):
+        if i % count == 0:
+            on_rows.append(ref[:part])
+            on_keys.append(ref[part:])
+        elif i % count < row_parts:
+            on_rows.append(ref[:part])
+        else:
+            on_keys.append(ref[:part])
+    grad_query[0] = sum(on_rows[1:], on_rows[0])
+    grad_key[0] = sum(on_keys[1:], on_keys[0])
+
+
+def close_kernel(mix_scale, loss_scale, total, grad_mix, head_loss):
+    heads = grad_mix.shape[1]
+    grad_mix[...] = total[:HEADS_S, :heads] * mix_scale
+    head_loss[...] = total[HEADS_S : HEADS_S + 1, :heads] * loss_scale
 
 
 def body(teacher_query, teacher_key, student_query, student_key, head_mix):
@@ -220,14 +272,21 @@
     def fetch(value, target, step):
         return lax.ppermute(value, "seq", [(target(i, step), i) for i in range(length)])
 
-    def swap(value, groups):
-        return lax.all_to_all(value, ("head", "seq"), 0, 0, axis_index_groups=groups, tiled=True)
-
-    key_s = [student_key] + [fetch(student_key, along_keys, d) for d in range(1, key_parts)]
-    query_s = [student_query] + [fetch(student_query, along_rows, d) for d in range(1, row_parts)]
-    key_t = [teacher_key] + [fetch(teacher_key, along_keys, d) for d in range(1, key_parts)]
-    query_t = [teacher_query] + [fetch(teacher_query, along_rows, d) for d in range(1, row_parts)]
-    lift_hi, lift_lo, back_hi, back_lo = expand_mix(head_mix)
+    def deliver(value, target, step, turn):
+        pairs = [
+            (h * length + i, (h + turn) % shards * length + target(i, step))
+            for h in range(shards)
+            for i in range(length)
+        ]
+        return lax.ppermute(value, ("head", "seq"), pairs)
+
+    own = (teacher_key, teacher_query, student_key, student_query)
+    key_t = [fetch(teacher_key, along_keys, d) for d in range(1, key_parts)]
+    query_t = [fetch(teacher_query, along_rows, d) for d in range(1, row_parts)]
+    key_s = [fetch(student_key, along_keys, d) for d in range(1, key_parts)]
+    query_s = [fetch(student_query, along_rows, d) for d in range(1, row_parts)]
+    *own, lift_hi, lift_lo, back_hi, back_lo = prepare(head_mix, own)
+    key_t, query_t, key_s, query_s = [[mine, *rest] for mine, rest in zip(own, (key_t, query_t, key_s, query_s))]
 
     def maps(block_t, block_s, before):
         count = len(block_t)
@@ -246,7 +305,7 @@
                 flops=cells * 2 * (HD_T + 3 * LIFT_BLOCK * HEADS_S), bytes_accessed=cells * 8, transcendentals=cells * 2
             ),
             name="maps",
-        )(*query_t, *block_t, *query_s, *block_s, *before, lift_hi, lift_lo)
+        )(*block_t, *query_t, *block_s, *query_s, *before, lift_hi, lift_lo)
 
     done, before = [], []
     for block in (slice(0, 1), slice(1, key_parts)):
@@ -258,44 +317,62 @@
 
     weight = shard_rows * length / HEADS_T
     width = HEADS_S * HD_S // shards
-    peers = length * copies
-    sums, for_query, for_key = pl.pallas_call(
-        functools.partial(back_kernel, row_parts, key_parts, len(done), heads, weight * HD_S ** (-0.5)),
-        out_shape=(
-            jax.ShapeDtypeStruct((peers, heads, 128), F32),
-            jax.ShapeDtypeStruct((shards * row_parts, shard_rows, width), F32),
-            jax.ShapeDtypeStruct((shards * key_parts, shard_rows, width), F32),
+    ride = RIDE_ROWS if width >= LANES else 0
+    count = row_parts + key_parts - 1
+    shapes = []
+    for shard in range(shards):
+        extra = ride if shard == 0 else 0
+        shapes += [(2 * shard_rows, width)] + [(shard_rows + extra, width)] * (count - 1)
+    sums, *pieces = pl.pallas_call(
+        functools.partial(
+            back_kernel, row_parts, key_parts, shards, len(done), heads, weight * HD_S ** (-0.5)
         ),
+        out_shape=[jax.ShapeDtypeStruct(shape, F32) for shape in [(RIDE_ROWS, LANES)] + shapes],
         scratch_shapes=[
             pltpu.VMEM((heads, rows), F32),
             pltpu.VMEM((heads, rows), F32),
             pltpu.VMEM((HEADS_S, keys, rows), BF16),
+            pltpu.VMEM((HEADS_S, rows, HD_S), BF16),
+            pltpu.VMEM((HEADS_S, keys, HD_S), BF16),
             pltpu.VMEM((heads * LIFT_BLOCK, HEADS_S * LIFT_BLOCK), F32),
         ],
         compiler_params=pltpu.CompilerParams(vmem_limit_bytes=VMEM_LIMIT),
         name="back",
     )(*query_s, *key_s, *lse_parts, back_hi, back_lo, *[ref for block in done for ref in block])
 
-    row_groups = [
-        [h * length + a * row_parts + b for h in range(shards) for b in range(row_parts)] for a in range(key_parts)
-    ]
-    key_groups = [
-        [h * length + a * row_parts + b for h in range(shards) for a in range(key_parts)] for b in range(row_parts)
-    ]
-    for_query = swap(for_query, row_groups)
-    for_key = swap(for_key, key_groups)
+    moves = [(along_rows, step) for step in range(row_parts)] + [(along_keys, step) for step in range(1, key_parts)]
+    arrived = [deliver(part, *moves[i % count], i // count) if i else part for i, part in enumerate(pieces)]
+    small = functools.partial(pl.pallas_call, compiler_params=pltpu.CompilerParams(vmem_limit_bytes=VMEM_LIMIT // 4))
+
+    def diagonal(across, along):
+        return lambda position, _: along_keys(along_rows(position, across), along)
+
+    if ride:
+        others = arrived[1:count]
+    else:
+        others = [fetch(sums, target, step) for target, step in moves[1:]]
+    for across in range(1, row_parts):
+        others += [fetch(sums, diagonal(across, along), 0) for along in range(1, key_parts)]
+    total = small(tally_kernel, out_shape=jax.ShapeDtypeStruct((RIDE_ROWS, LANES), F32), name="tally")(sums, *others)
+    if copies & (copies - 1) == 0:
+        for bit in range(copies.bit_length() - 1):
+            total = total + lax.ppermute(total, "dp", [(i, i ^ (1 << bit)) for i in range(copies)])
+    else:
+        mine = total
+        for step in range(1, copies):
+            total = total + lax.ppermute(mine, "dp", [(i, (i + step) % copies) for i in range(copies)])
+
     grad = jax.ShapeDtypeStruct((1, shard_rows, width), F32)
-    grad_query, grad_key = pl.pallas_call(
-        finish_kernel,
-        out_shape=(grad, grad),
-        compiler_params=pltpu.CompilerParams(vmem_limit_bytes=VMEM_LIMIT),
-        name="finish",
-    )(for_query, for_key)
-    total = jnp.sum(lax.all_to_all(sums, ("seq", "dp"), 0, 0, tiled=True), axis=0)
+    grad_query, grad_key = small(
+        functools.partial(finish_kernel, row_parts, key_parts), out_shape=(grad, grad), name="finish"
+    )(*arrived)
     samples = copies * teacher_query.shape[0] * shard_rows * length
-    grad_mix = total[:, :HEADS_S] * (HD_S ** (-0.5) * weight / samples)
-    head_loss = total[:, HEADS_S] / samples
-    return (grad_query, grad_key, grad_mix, head_loss)
+    grad_mix, head_loss = small(
+        functools.partial(close_kernel, HD_S ** (-0.5) * weight / samples, 1.0 / samples),
+        out_shape=(jax.ShapeDtypeStruct((HEADS_S, heads), F32), jax.ShapeDtypeStruct((1, heads), F32)),
+        name="close",
+    )(total)
+    return (grad_query, grad_key, grad_mix.T, head_loss[0])
 
 
 def solution(mesh):

time: 84.5 us -> 57.6 us (0.68)
  blocking collectives: 24.2 us -> 0 us
  waiting for transfers between devices: 32.5 us -> 27 us
  starting transfers between devices: 10.7 us -> 14.3 us
    all_to_all x2 -> x0, blocking collectives: 24.2 us -> none  [the longest x1 13.5 us: body(): lax.all_to_all(sums, ('seq', 'dp'), 0, 0, tiled=True)]
    all_to_all x1 -> x0, waiting for transfers between devices: 11.9 us -> none  [swap(): lax.all_to_all(value, ('head', 'seq'), 0, 0, axis_index_groups=groups, ti...]
    ppermute x0 -> x7, starting transfers between devices: none -> 6.51 us  [the longest x5 4.94 us: deliver(): return lax.ppermute(value, ('head', 'seq'), pairs)]
    ppermute x0 -> x7, waiting for transfers between devices: none -> 4.56 us  [the longest x2 3.31 us: body(): lax.ppermute(total, 'dp', [(i, i ^ 1 << bit) for i in range(copies)])]
    all_to_all x1 -> x0, starting transfers between devices: 3.47 us -> none  [swap(): lax.all_to_all(value, ('head', 'seq'), 0, 0, axis_index_groups=groups, ti...]
    ppermute x5 -> x6, waiting for transfers between devices: 20.6 us -> 22.4 us  [fetch(): lax.ppermute(value, 'seq', [(target(i, step), i) for i in range(length)])]
    pallas_call x3 -> x5, Pallas kernels: 4.73 us -> 5.48 us  [the longest x1 3.16 us: body(): pl.pallas_call(functools.partial(back_kernel, row_parts, key_parts, shard...]
    unnamed x16 -> x11, local copies, waits for them, and re-layouts: 5.93 us -> 5.25 us
  transfers between devices with their start and end apart: 6 -> 13, of which waited for: 3 -> 7; matrix products, arithmetic and copies ran while one was open for 3% -> 1% of each run, Pallas kernels for 3% -> 7%
where the time goes in v1:
time: 57.6 us; the launch traced here: 57.3 us
  waiting for transfers between devices  27 us (47%)
  starting transfers between devices  14.3 us (25%)
  Pallas kernels  10.1 us (18%)
  local copies, waits for them, and re-layouts  5.25 us (9%)
  between operations  0.68 us (1%)
    ppermute x6, waiting for transfers between devices, fetch(): lax.ppermute(value, 'seq', [(target(i, step), i) for i in range(length)])  22.4 us
    ppermute x6, starting transfers between devices, fetch(): lax.ppermute(value, 'seq', [(target(i, step), i) for i in range(length)])  7.77 us
    unnamed x11, local copies, waits for them, and re-layouts  5.25 us
    ppermute x5, starting transfers between devices, deliver(): return lax.ppermute(value, ('head', 'seq'), pairs)  4.94 us
    pallas_call x2, Pallas kernels, maps(): pl.pallas_call(functools.partial(maps_kernel, row_parts, count, heads, bo...  4.62 us
    ppermute x2, waiting for transfers between devices, body(): lax.ppermute(total, 'dp', [(i, i ^ 1 << bit) for i in range(copies)])  3.31 us
    pallas_call x1, Pallas kernels, body(): pl.pallas_call(functools.partial(back_kernel, row_parts, key_parts, shard...  3.16 us
    ppermute x2, starting transfers between devices, body(): lax.ppermute(total, 'dp', [(i, i ^ 1 << bit) for i in range(copies)])  1.57 us
  transfers between devices with their start and end apart: 13, of which 7 were waited for; matrix products, arithmetic and copies ran while one was open for 1% of the time, Pallas kernels for 7%

profile of v1, /device:TPU:0, one launch (start us, length us, event | category | flops | bytes accessed | tf_op | source)
XLA Modules:
  0.0 57.3 jit_solution(17585758573513138576)
XLA Ops:
  0.6 3.1 %collective-permute-start.3 = (bf16[1,128,1536]{2,1,0:T(8,128)(2,1)}, bf16[1,128,1536]{2,1,0:T(8,128)(2,1)S(1)}, u32[]{:S(2)}, u32[]{:S(2)}) collective-permute-start(bf16[1,128,1536]{2,1,0:T(8,128)(2,1)} %refs_1_.1), channel_id=1, source_target_pairs={{4,0},{0,4},{12,8},{8,12},{5,1},{1,5},{13,9},{9,13},{6,2},{2,6},{1... | collective-permute-start | bytes 1179656 | tf_op jit(solution)/shard_map/ppermute | solution.py:273
  3.7 2.6 %collective-permute-start.2 = (bf16[1,128,1536]{2,1,0:T(8,128)(2,1)}, bf16[1,128,1536]{2,1,0:T(8,128)(2,1)S(1)}, u32[]{:S(2)}, u32[]{:S(2)}) collective-permute-start(bf16[1,128,1536]{2,1,0:T(8,128)(2,1)} %refs_0_.1), channel_id=1, source_target_pairs={{8,0},{12,4},{0,8},{4,12},{9,1},{13,5},{1,9},{5,13},{10,2},{14,6},... | collective-permute-start | bytes 1179656 | tf_op jit(solution)/shard_map/ppermute | solution.py:273
  6.8 0.8 %copy.9.mix_ref = f32[12,8]{1,0:T(8,128)S(1)} copy(f32[12,8]{0,1:T(8,128)} %param.9) | data formatting | bytes 768 | tf_op args[4]
  7.5 1.0 %copy-done = bf16[1,128,1536]{2,1,0:T(8,128)(2,1)S(1)} copy-done((bf16[1,128,1536]{2,1,0:T(8,128)(2,1)S(1)}, bf16[1,128,1536]{2,1,0:T(8,128)(2,1)}, u32[]{:S(2)}) %copy-start) | copy-done | bytes 393240
  8.5 1.0 %copy-done.1 = bf16[1,128,1536]{2,1,0:T(8,128)(2,1)S(1)} copy-done((bf16[1,128,1536]{2,1,0:T(8,128)(2,1)S(1)}, bf16[1,128,1536]{2,1,0:T(8,128)(2,1)}, u32[]{:S(2)}) %copy-start.1) | copy-done | bytes 393240
  9.5 0.9 %copy-done.2 = bf16[1,128,512]{2,1,0:T(8,128)(2,1)S(1)} copy-done((bf16[1,128,512]{2,1,0:T(8,128)(2,1)S(1)}, bf16[1,128,512]{2,1,0:T(8,128)(2,1)}, u32[]{:S(2)}) %copy-start.2) | copy-done | bytes 131096
  10.4 0.9 %copy-done.3 = bf16[1,128,512]{2,1,0:T(8,128)(2,1)S(1)} copy-done((bf16[1,128,512]{2,1,0:T(8,128)(2,1)S(1)}, bf16[1,128,512]{2,1,0:T(8,128)(2,1)}, u32[]{:S(2)}) %copy-start.3) | copy-done | bytes 131096
  11.3 0.7 %copy-done.4 = f32[12,8]{0,1:T(8,128)S(1)} copy-done((f32[12,8]{0,1:T(8,128)S(1)}, f32[12,8]{0,1:T(8,128)}, u32[]{:S(2)}) %copy-start.4) | copy-done | bytes 408
  12.0 1.0 %prepare.1 = (bf16[1,128,1536]{2,1,0:T(8,128)(2,1)S(1)}, bf16[1,128,1536]{2,1,0:T(8,128)(2,1)S(1)}, bf16[1,128,512]{2,1,0:T(8,128)(2,1)S(1)}, bf16[1,128,512]{2,...) custom-call(f32[12,8]{1,0:T(8,128)S(1)} %copy.9.mix_ref, ...), custom_call_target="tpu_custom_call" | custom-call | tf_op jit(solution)/shard_map/prepare/pallas_call | solution.py:70
  13.0 13.2 %collective-permute-done.refs_5_.refs_1_ = bf16[1,128,512]{2,1,0:T(8,128)(2,1)S(1)} collective-permute-done((bf16[1,128,512]{2,1,0:T(8,128)(2,1)}, bf16[1,128,512]{2,1,0:T(8,128)(2,1)S(1)}, u32[]{:S(2)}, u32[]{:S(2)}) %collective-permute-start) | collective-permute-done | bytes 131104 | tf_op jit(solution)/shard_map/ppermute | solution.py:273
  26.2 2.6 %maps.2 = (f32[12,128,256]{2,1,0:T(8,128)S(1)}, f32[12,128,256]{2,1,0:T(8,128)S(1)}, bf16[8,128,256]{2,1,0:T(8,128)(2,1)S(1)}, bf16[8,128,256]{2,1,0:T(8,128)(2,...) custom-call(bf16[1,128,1536]{2,1,0:T(8,128)(2,1)S(1)} %get-tuple-ele, ...), custom_call_target="tpu_custom_call" | custom-call | flops 704643072 | bytes 3145728 | tf_op jit(solution)/shard_map/maps/pallas_call | solution.py:298
  28.8 0.7 %collective-permute-done.1.refs_3_ = bf16[1,128,512]{2,1,0:T(8,128)(2,1)S(1)} collective-permute-done((bf16[1,128,512]{2,1,0:T(8,128)(2,1)}, bf16[1,128,512]{2,1,0:T(8,128)(2,1)S(1)}, u32[]{:S(2)}, u32[]{:S(2)}) %collective-permute-start.1) | collective-permute-done | bytes 131104 | tf_op jit(solution)/shard_map/ppermute | solution.py:273
  29.5 2.0 %maps.3 = (f32[12,128,256]{2,1,0:T(8,128)S(1)}, f32[12,128,256]{2,1,0:T(8,128)S(1)}, bf16[8,128,256]{2,1,0:T(8,128)(2,1)S(1)}, bf16[8,128,256]{2,1,0:T(8,128)(2,...) custom-call(bf16[1,128,1536]{2,1,0:T(8,128)(2,1)S(1)} %collective-pe, ...), custom_call_target="tpu_custom_call" | custom-call | flops 704643072 | bytes 3145728 | tf_op jit(solution)/shard_map/maps/pallas_call | solution.py:298
  32.1 3.4 %collective-permute-done.4.refs_5_ = f32[2,12,256]{2,1,0:T(8,128)S(1)} collective-permute-done((f32[2,12,256]{2,1,0:T(8,128)S(1)}, f32[2,12,256]{2,1,0:T(8,128)S(1)}, u32[]{:S(2)}, u32[]{:S(2)}) %collective-permute-start.4) | collective-permute-done | bytes 24608 | tf_op jit(solution)/shard_map/ppermute | solution.py:273
  35.5 3.2 %back.1 = (f32[16,128]{1,0:T(8,128)S(1)}, f32[256,256]{1,0:T(8,128)S(1)}, f32[144,256]{1,0:T(8,128)S(1)}, f32[144,256]{1,0:T(8,128)S(1)}, f32[256,256]{1,0:T(8,1...) custom-call(bf16[1,128,512]{2,1,0:T(8,128)(2,1)S(1)} %get-tuple-element.38.refs_4_.refs_0_, ...), custom_call_target="tpu_custom_call" | custom-call | tf_op jit(solution)/shard_map/back/pallas_call | solution.py:326
  38.7 1.6 %collective-permute-start.7 = (f32[256,256]{1,0:T(8,128)S(1)}, f32[256,256]{1,0:T(8,128)S(1)}, u32[]{:S(2)}, u32[]{:S(2)}) collective-permute-start(f32[256,256]{1,0:T(8,128)S(1)} %get-tuple-element.64), channel_id=1, source_target_pairs={{0,16},{4,20},{8,24},{12,28},{16,0},{20,4},{24,8},{28,12},{1,17},{... | collective-permute-start | bytes 786440 | tf_op jit(solution)/shard_map/ppermute | solution.py:281
  40.8 2.8 %collective-permute-start.6 = (f32[144,256]{1,0:T(8,128)S(1)}, f32[144,256]{1,0:T(8,128)S(1)}, u32[]{:S(2)}, u32[]{:S(2)}) collective-permute-start(f32[144,256]{1,0:T(8,128)S(1)} %get-tuple-element.63), channel_id=1, source_target_pairs={{0,8},{4,12},{8,0},{12,4},{16,24},{20,28},{24,16},{28,20},{1,9},{5... | collective-permute-start | bytes 442376 | tf_op jit(solution)/shard_map/ppermute | solution.py:281
  43.6 1.1 %collective-permute-start.10 = (f32[16,128]{1,0:T(8,128)S(1)}, f32[16,128]{1,0:T(8,128)S(1)}, u32[]{:S(2)}, u32[]{:S(2)}) collective-permute-start(f32[16,128]{1,0:T(8,128)S(1)} %get-tuple-element.69.refs_0_), channel_id=1, source_target_pairs={{12,0},{8,4},{4,8},{0,12},{13,1},{9,5},{5,9},{1,13},{14,2},{10,6},... | collective-permute-start | bytes 24584 | tf_op jit(solution)/shard_map/ppermute | solution.py:273
  44.7 5.1 %collective-permute-done.10.refs_3_ = f32[16,128]{1,0:T(8,128)S(1)} collective-permute-done((f32[16,128]{1,0:T(8,128)S(1)}, f32[16,128]{1,0:T(8,128)S(1)}, u32[]{:S(2)}, u32[]{:S(2)}) %collective-permute-start.10) | collective-permute-done | bytes 8224 | tf_op jit(solution)/shard_map/ppermute | solution.py:273
  49.9 1.2 %collective-permute-done.11 = f32[16,128]{1,0:T(8,128)S(1)} collective-permute-done((f32[16,128]{1,0:T(8,128)S(1)}, f32[16,128]{1,0:T(8,128)S(1)}, u32[]{:S(2)}, u32[]{:S(2)}) %collective-permute-start.11) | collective-permute-done | bytes 8224 | tf_op jit(solution)/shard_map/ppermute | solution.py:359
  51.1 1.5 %collective-permute-start.12 = (f32[16,128]{1,0:T(8,128)S(1)}, f32[16,128]{1,0:T(8,128)S(1)}, u32[]{:S(2)}, u32[]{:S(2)}) collective-permute-start(f32[16,128]{1,0:T(8,128)S(1)} %add.6), channel_id=1, source_target_pairs={{0,2},{1,3},{2,0},{3,1},{4,6},{5,7},{6,4},{7,5},{8,10},{9,11},{10,... | collective-permute-start | bytes 24584 | tf_op jit(solution)/shard_map/ppermute | solution.py:359
  52.6 2.2 %collective-permute-done.12 = f32[16,128]{1,0:T(8,128)S(1)} collective-permute-done((f32[16,128]{1,0:T(8,128)S(1)}, f32[16,128]{1,0:T(8,128)S(1)}, u32[]{:S(2)}, u32[]{:S(2)}) %collective-permute-start.12) | collective-permute-done | bytes 8224 | tf_op jit(solution)/shard_map/ppermute | solution.py:359
  55.3 1.2 %collective-permute-done.9.refs_5_ = f32[128,256]{1,0:T(8,128)S(1)} collective-permute-done((f32[128,256]{1,0:T(8,128)S(1)}, f32[128,256]{1,0:T(8,128)S(1)}, u32[]{:S(2)}, u32[]{:S(2)}) %collective-permute-start.9) | collective-permute-done | bytes 131104 | tf_op jit(solution)/shard_map/ppermute | solution.py:281
  56.6 0.7 %finish.1 = (f32[1,128,256]{2,1,0:T(8,128)}, f32[1,128,256]{2,1,0:T(8,128)}) custom-call(f32[256,256]{1,0:T(8,128)S(1)} %get-tuple-element.61.refs_0_, f32[144,256]{1,0:T(8,128)S(1)} %collective-permute-done.5.refs_1_, f32[144,256]{1,0:T(8,128)S(1)} %collective-permute-done.6.refs_2_, f32[256,256]{1,0:T(8,128)S(1)} %collective-permute-done.7.refs_3_, ...), custom_call_target="tpu_custom_call" | custom-call | tf_op jit(solution)/shard_map/finish/pallas_call | solution.py:366
  (22 shorter events, 2.2 us)
Async XLA Ops:
  0.6 25.5 %collective-permute-start.3 = (bf16[1,128,1536]{2,1,0:T(8,128)(2,1)}, bf16[1,128,1536]{2,1,0:T(8,128)(2,1)S(1)}, u32[]{:S(2)}, u32[]{:S(2)}) collective-permute-start(bf16[1,128,1536]{2,1,0:T(8,128)(2,1)} %refs_1_.1), channel_id=1, source_target_pairs={{4,0},{0,4},{12,8},{8,12},{5,1},{1,5},{13,9},{9,13},{6,2},{2,6},{1... | collective-permute-start | bytes 1179656 | tf_op jit(solution)/shard_map/ppermute | solution.py:273
  3.7 25.8 %collective-permute-start.2 = (bf16[1,128,1536]{2,1,0:T(8,128)(2,1)}, bf16[1,128,1536]{2,1,0:T(8,128)(2,1)S(1)}, u32[]{:S(2)}, u32[]{:S(2)}) collective-permute-start(bf16[1,128,1536]{2,1,0:T(8,128)(2,1)} %refs_0_.1), channel_id=1, source_target_pairs={{8,0},{12,4},{0,8},{4,12},{9,1},{13,5},{1,9},{5,13},{10,2},{14,6},... | collective-permute-start | bytes 1179656 | tf_op jit(solution)/shard_map/ppermute | solution.py:273
  6.3 19.9 %collective-permute-start = (bf16[1,128,512]{2,1,0:T(8,128)(2,1)}, bf16[1,128,512]{2,1,0:T(8,128)(2,1)S(1)}, u32[]{:S(2)}, u32[]{:S(2)}) collective-permute-start(bf16[1,128,512]{2,1,0:T(8,128)(2,1)} %refs_3_.1), channel_id=1, source_target_pairs={{4,0},{0,4},{12,8},{8,12},{5,1},{1,5},{13,9},{9,13},{6,2},{2,6},{1... | collective-permute-start | bytes 393224 | tf_op jit(solution)/shard_map/ppermute | solution.py:273
  6.8 22.7 %collective-permute-start.1 = (bf16[1,128,512]{2,1,0:T(8,128)(2,1)}, bf16[1,128,512]{2,1,0:T(8,128)(2,1)S(1)}, u32[]{:S(2)}, u32[]{:S(2)}) collective-permute-start(bf16[1,128,512]{2,1,0:T(8,128)(2,1)} %refs_2_.1), channel_id=1, source_target_pairs={{8,0},{12,4},{0,8},{4,12},{9,1},{13,5},{1,9},{5,13},{10,2},{14,6},... | collective-permute-start | bytes 393224 | tf_op jit(solution)/shard_map/ppermute | solution.py:273
  7.5 1.0 %copy-start = (bf16[1,128,1536]{2,1,0:T(8,128)(2,1)S(1)}, bf16[1,128,1536]{2,1,0:T(8,128)(2,1)}, u32[]{:S(2)}) copy-start(bf16[1,128,1536]{2,1,0:T(8,128)(2,1)} %refs_1_.1) | copy-start | bytes 1179652
  8.5 1.0 %copy-start.1 = (bf16[1,128,1536]{2,1,0:T(8,128)(2,1)S(1)}, bf16[1,128,1536]{2,1,0:T(8,128)(2,1)}, u32[]{:S(2)}) copy-start(bf16[1,128,1536]{2,1,0:T(8,128)(2,1)} %refs_0_.1) | copy-start | bytes 1179652
  9.5 0.9 %copy-start.2 = (bf16[1,128,512]{2,1,0:T(8,128)(2,1)S(1)}, bf16[1,128,512]{2,1,0:T(8,128)(2,1)}, u32[]{:S(2)}) copy-start(bf16[1,128,512]{2,1,0:T(8,128)(2,1)} %refs_3_.1) | copy-start | bytes 393220
  10.4 0.9 %copy-start.3 = (bf16[1,128,512]{2,1,0:T(8,128)(2,1)S(1)}, bf16[1,128,512]{2,1,0:T(8,128)(2,1)}, u32[]{:S(2)}) copy-start(bf16[1,128,512]{2,1,0:T(8,128)(2,1)} %refs_2_.1) | copy-start | bytes 393220
  11.3 0.7 %copy-start.4 = (f32[12,8]{0,1:T(8,128)S(1)}, f32[12,8]{0,1:T(8,128)}, u32[]{:S(2)}) copy-start(f32[12,8]{0,1:T(8,128)} %param.9) | copy-start | bytes 1156
  31.5 4.0 %collective-permute-start.4 = (f32[2,12,256]{2,1,0:T(8,128)S(1)}, f32[2,12,256]{2,1,0:T(8,128)S(1)}, u32[]{:S(2)}, u32[]{:S(2)}) collective-permute-start(f32[2,12,256]{2,1,0:T(8,128)S(1)} %get-tuple-element.46), channel_id=1, source_target_pairs={{4,0},{0,4},{12,8},{8,12},{5,1},{1,5},{13,9},{9,13},{6,2},{2,6},{1... | collective-permute-start | bytes 73736 | tf_op jit(solution)/shard_map/ppermute | solution.py:273
  38.7 17.9 %collective-permute-start.7 = (f32[256,256]{1,0:T(8,128)S(1)}, f32[256,256]{1,0:T(8,128)S(1)}, u32[]{:S(2)}, u32[]{:S(2)}) collective-permute-start(f32[256,256]{1,0:T(8,128)S(1)} %get-tuple-element.64), channel_id=1, source_target_pairs={{0,16},{4,20},{8,24},{12,28},{16,0},{20,4},{24,8},{28,12},{1,17},{... | collective-permute-start | bytes 786440 | tf_op jit(solution)/shard_map/ppermute | solution.py:281
  40.3 9.5 %collective-permute-start.5 = (f32[144,256]{1,0:T(8,128)S(1)}, f32[144,256]{1,0:T(8,128)S(1)}, u32[]{:S(2)}, u32[]{:S(2)}) collective-permute-start(f32[144,256]{1,0:T(8,128)S(1)} %get-tuple-element.62), channel_id=1, source_target_pairs={{0,4},{4,0},{8,12},{12,8},{16,20},{20,16},{24,28},{28,24},{1,5},{5... | collective-permute-start | bytes 442376 | tf_op jit(solution)/shard_map/ppermute | solution.py:281
  40.8 9.0 %collective-permute-start.6 = (f32[144,256]{1,0:T(8,128)S(1)}, f32[144,256]{1,0:T(8,128)S(1)}, u32[]{:S(2)}, u32[]{:S(2)}) collective-permute-start(f32[144,256]{1,0:T(8,128)S(1)} %get-tuple-element.63), channel_id=1, source_target_pairs={{0,8},{4,12},{8,0},{12,4},{16,24},{20,28},{24,16},{28,20},{1,9},{5... | collective-permute-start | bytes 442376 | tf_op jit(solution)/shard_map/ppermute | solution.py:281
  43.6 6.2 %collective-permute-start.10 = (f32[16,128]{1,0:T(8,128)S(1)}, f32[16,128]{1,0:T(8,128)S(1)}, u32[]{:S(2)}, u32[]{:S(2)}) collective-permute-start(f32[16,128]{1,0:T(8,128)S(1)} %get-tuple-element.69.refs_0_), channel_id=1, source_target_pairs={{12,0},{8,4},{4,8},{0,12},{13,1},{9,5},{5,9},{1,13},{14,2},{10,6},... | collective-permute-start | bytes 24584 | tf_op jit(solution)/shard_map/ppermute | solution.py:273
  44.7 10.6 %collective-permute-start.8 = (f32[128,256]{1,0:T(8,128)S(1)}, f32[128,256]{1,0:T(8,128)S(1)}, u32[]{:S(2)}, u32[]{:S(2)}) collective-permute-start(f32[128,256]{1,0:T(8,128)S(1)} %get-tuple-element.65), channel_id=1, source_target_pairs={{0,20},{4,16},{8,28},{12,24},{16,4},{20,0},{24,12},{28,8},{1,21},{... | collective-permute-start | bytes 393224 | tf_op jit(solution)/shard_map/ppermute | solution.py:281
  49.8 6.8 %collective-permute-start.9 = (f32[128,256]{1,0:T(8,128)S(1)}, f32[128,256]{1,0:T(8,128)S(1)}, u32[]{:S(2)}, u32[]{:S(2)}) collective-permute-start(f32[128,256]{1,0:T(8,128)S(1)} %get-tuple-element.66), channel_id=1, source_target_pairs={{0,24},{4,28},{8,16},{12,20},{16,8},{20,12},{24,0},{28,4},{1,25},{... | collective-permute-start | bytes 393224 | tf_op jit(solution)/shard_map/ppermute | solution.py:281
  49.8 1.2 %collective-permute-start.11 = (f32[16,128]{1,0:T(8,128)S(1)}, f32[16,128]{1,0:T(8,128)S(1)}, u32[]{:S(2)}, u32[]{:S(2)}) collective-permute-start(f32[16,128]{1,0:T(8,128)S(1)} %tally.1), channel_id=1, source_target_pairs={{0,1},{1,0},{2,3},{3,2},{4,5},{5,4},{6,7},{7,6},{8,9},{9,8},{10,11... | collective-permute-start | bytes 24584 | tf_op jit(solution)/shard_map/ppermute | solution.py:359
  51.1 3.7 %collective-permute-start.12 = (f32[16,128]{1,0:T(8,128)S(1)}, f32[16,128]{1,0:T(8,128)S(1)}, u32[]{:S(2)}, u32[]{:S(2)}) collective-permute-start(f32[16,128]{1,0:T(8,128)S(1)} %add.6), channel_id=1, source_target_pairs={{0,2},{1,3},{2,0},{3,1},{4,6},{5,7},{6,4},{7,5},{8,10},{9,11},{10,... | collective-permute-start | bytes 24584 | tf_op jit(solution)/shard_map/ppermute | solution.py:359

commit v2 on v1

--- a/solution.py
+++ b/solution.py
@@ -82,20 +82,40 @@
     return parts[0] if len(parts) == 1 else jnp.concatenate(parts, axis=0)
 
 
-def maps_kernel(row_parts, key_parts, heads, carried, *refs):
+def by_head(place, shards, pieces, side):
+    per = HEADS_S // shards
+    low = turn = 0
+    for piece in pieces:
+        size, columns = piece.shape[1], piece.shape[2]
+        whole = columns == HEADS_S * HD_S
+        first = 0 if whole else lax.rem(place + shards - turn, shards) * per
+        for index in range(columns // HD_S):
+            side[first + index, low : low + size] = piece[0, :, index * HD_S : (index + 1) * HD_S]
+        turn = 0 if whole else (turn + 1) % shards
+        low += size if turn == 0 else 0
+
+
+def maps_kernel(row_parts, key_parts, shards, student_parts, heads, carried, *refs):
     refs = list(refs)
-    key_t = [refs.pop(0) for _ in range(key_parts)]
-    query_t = [refs.pop(0) for _ in range(row_parts)]
-    key_s = [refs.pop(0) for _ in range(key_parts)]
-    query_s = [refs.pop(0) for _ in range(row_parts)]
+
+    def take(count):
+        return [refs.pop(0) for _ in range(count)]
+
+    key_t, query_t = take(key_parts), take(row_parts)
+    key_s, query_s = take(student_parts[0]), take(student_parts[1])
     before = refs.pop(0) if carried else None
-    lift_hi, lift_lo, exp_t, exp_l, stu_hi, stu_lo, top, kl, lse, *turned, lifted = refs
+    lift_hi, lift_lo, exp_t, exp_l, stu_hi, stu_lo, top, kl, key_side, *rest = refs
+    query_side = query_s[0]
+    place = lax.axis_index("head")
+    if not carried:
+        query_side = rest.pop(0)
+        by_head(place, shards, query_s, query_side)
+    by_head(place, shards, key_s, key_side)
+    lse, *turned, lifted = rest
     keys = stu_hi.shape[1]
     rows = stu_hi.shape[2]
     for index in range(HEADS_S):
-        columns = slice(index * HD_S, (index + 1) * HD_S)
-        student = dot(stacked(key_s, columns), stacked(query_s, columns), ((1,), (1,)))
-        stu_hi[index], stu_lo[index] = split(student)
+        stu_hi[index], stu_lo[index] = split(dot(key_side[index], query_side[index], ((1,), (1,))))
     for start in range(0, keys, LIFT_BLOCK):
         block = slice(start, start + LIFT_BLOCK)
         high = stu_hi[:, block, :].reshape(HEADS_S * LIFT_BLOCK, rows)
@@ -133,12 +153,11 @@
 
 def back_kernel(row_parts, key_parts, shards, blocks, heads, factor, *refs):
     refs = list(refs)
-    query_s = [refs.pop(0) for _ in range(row_parts)]
-    key_s = [refs.pop(0) for _ in range(key_parts)]
     lse = [refs.pop(0) for _ in range(row_parts)]
-    back_hi, back_lo = refs[:2]
-    maps = [refs[2 + 6 * i : 8 + 6 * i] for i in range(blocks)]
-    *outs, scale_t, scale_l, back, row_side, key_side, mix_acc = refs[2 + 6 * blocks :]
+    back_hi, back_lo, query_side = refs[:3]
+    maps = [refs[3 + 7 * i : 9 + 7 * i] for i in range(blocks)]
+    key_sides = [refs[9 + 7 * i] for i in range(blocks)]
+    *outs, scale_t, scale_l, back, mix_acc = refs[3 + 7 * blocks :]
     keys, rows = back.shape[1:]
     part, size = rows // row_parts, keys // key_parts
     sums, pieces = outs[0], outs[1:]
@@ -195,10 +214,6 @@
     packed = jnp.transpose(packed)[:RIDE_ROWS]
     sums[...] = packed
 
-    for index in range(HEADS_S):
-        columns = slice(index * HD_S, (index + 1) * HD_S)
-        row_side[index] = stacked(query_s, columns)
-        key_side[index] = stacked(key_s, columns)
     place = lax.axis_index("head")
     per = HEADS_S // shards
     count = row_parts + key_parts - 1
@@ -208,8 +223,9 @@
         for index in range(per):
             tile = back[first + index]
             columns = slice(index * HD_S, (index + 1) * HD_S)
-            on_keys = dot(tile, row_side[first + index]) * factor
-            on_rows = dot(tile, key_side[first + index], ((0,), (0,))) * factor
+            sides = [side[first + index] for side in key_sides]
+            on_keys = dot(tile, query_side[first + index]) * factor
+            on_rows = dot(tile, jnp.concatenate(sides, axis=0), ((0,), (0,))) * factor
             own[:part, columns] = on_rows[:part]
             own[part:, columns] = on_keys[:size]
             for spot in range(1, row_parts):
@@ -230,21 +246,18 @@
     total[...] = value
 
 
-def finish_kernel(row_parts, key_parts, *refs):
-    *pieces, grad_query, grad_key = refs
-    part = grad_query.shape[1]
-    count = row_parts + key_parts - 1
-    on_rows, on_keys = [], []
-    for i, ref in enumerate(pieces):
-        if i % count == 0:
-            on_rows.append(ref[:part])
-            on_keys.append(ref[part:])
-        elif i % count < row_parts:
-            on_rows.append(ref[:part])
-        else:
-            on_keys.append(ref[:part])
-    grad_query[0] = sum(on_rows[1:], on_rows[0])
-    grad_key[0] = sum(on_keys[1:], on_keys[0])
+def finish(pieces, low, part, small, sums=()):
+    def kernel(*refs):
+        shares, rest = refs[: len(pieces)], refs[len(pieces) :]
+        first, *others = [ref[low : low + part] if ref.shape[0] == 2 * part else ref[:part] for ref in shares]
+        rest[len(sums)][0] = sum(others, first)
+        if sums:
+            mine, other, _, total = rest
+            total[...] = mine[...] + other[...]
+
+    shapes = [jax.ShapeDtypeStruct((1, part, pieces[0].shape[1]), F32)]
+    shapes += [jax.ShapeDtypeStruct((RIDE_ROWS, LANES), F32)] if sums else []
+    return small(kernel, out_shape=shapes, name="finish")(*pieces, *sums)
 
 
 def close_kernel(mix_scale, loss_scale, total, grad_mix, head_loss):
@@ -280,15 +293,22 @@
         ]
         return lax.ppermute(value, ("head", "seq"), pairs)
 
+    def fetch_student(value, target, step):
+        columns = value.shape[2] // shards
+        share = lax.dynamic_slice_in_dim(value, lax.axis_index("head") * columns, columns, 2)
+        share = fetch(share, target, step)
+        turns = [[(h, (h + turn) % shards) for h in range(shards)] for turn in range(1, shards)]
+        return [share] + [lax.ppermute(share, "head", pairs) for pairs in turns]
+
     own = (teacher_key, teacher_query, student_key, student_query)
     key_t = [fetch(teacher_key, along_keys, d) for d in range(1, key_parts)]
     query_t = [fetch(teacher_query, along_rows, d) for d in range(1, row_parts)]
-    key_s = [fetch(student_key, along_keys, d) for d in range(1, key_parts)]
-    query_s = [fetch(student_query, along_rows, d) for d in range(1, row_parts)]
+    key_s = [piece for d in range(1, key_parts) for piece in fetch_student(student_key, along_keys, d)]
+    query_s = [piece for d in range(1, row_parts) for piece in fetch_student(student_query, along_rows, d)]
     *own, lift_hi, lift_lo, back_hi, back_lo = prepare(head_mix, own)
     key_t, query_t, key_s, query_s = [[mine, *rest] for mine, rest in zip(own, (key_t, query_t, key_s, query_s))]
 
-    def maps(block_t, block_s, before):
+    def maps(block_t, block_s, rows_s, before):
         count = len(block_t)
         size = count * shard_rows
         exponents = pltpu.VMEM((heads, size, rows), F32)
@@ -296,23 +316,26 @@
         stats = pltpu.VMEM((2, heads, rows), F32)
         cells = heads * size * rows
         return pl.pallas_call(
-            functools.partial(maps_kernel, row_parts, count, heads, bool(before)),
-            out_shape=(exponents, exponents, student, student, stats, pltpu.VMEM((heads, rows), F32))
-            + (stats,) * row_parts,
+            functools.partial(
+                maps_kernel, row_parts, count, shards, (len(block_s), len(rows_s)), heads, bool(before)
+            ),
+            out_shape=[exponents, exponents, student, student, stats, pltpu.VMEM((heads, rows), F32)]
+            + [pltpu.VMEM((HEADS_S, size, HD_S), BF16)]
+            + [pltpu.VMEM((HEADS_S, rows, HD_S), BF16)] * (not before)
+            + [stats] * row_parts,
             scratch_shapes=[pltpu.VMEM((heads, size, rows), F32)],
             compiler_params=pltpu.CompilerParams(vmem_limit_bytes=VMEM_LIMIT),
             cost_estimate=pl.CostEstimate(
                 flops=cells * 2 * (HD_T + 3 * LIFT_BLOCK * HEADS_S), bytes_accessed=cells * 8, transcendentals=cells * 2
             ),
             name="maps",
-        )(*block_t, *query_t, *block_s, *query_s, *before, lift_hi, lift_lo)
-
-    done, before = [], []
-    for block in (slice(0, 1), slice(1, key_parts)):
-        if key_t[block]:
-            results = maps(key_t[block], key_s[block], before)
-            done.append(results[:6])
-            before, turned = results[6:7], results[7:]
+        )(*block_t, *query_t, *block_s, *rows_s, *before, lift_hi, lift_lo)
+
+    results = maps(key_t[:1], key_s[:1], query_s, [])
+    done, query_side, before, turned = [results[:7]], results[7], results[8:9], results[9:]
+    if key_parts > 1:
+        results = maps(key_t[1:], key_s[1:], [query_side], before)
+        done, before, turned = done + [results[:7]], results[7:8], results[8:]
     lse_parts = [*before] + [fetch(turned[step - 1], along_rows, row_parts - step) for step in range(1, row_parts)]
 
     weight = shard_rows * length / HEADS_T
@@ -332,13 +355,11 @@
             pltpu.VMEM((heads, rows), F32),
             pltpu.VMEM((heads, rows), F32),
             pltpu.VMEM((HEADS_S, keys, rows), BF16),
-            pltpu.VMEM((HEADS_S, rows, HD_S), BF16),
-            pltpu.VMEM((HEADS_S, keys, HD_S), BF16),
             pltpu.VMEM((heads * LIFT_BLOCK, HEADS_S * LIFT_BLOCK), F32),
         ],
         compiler_params=pltpu.CompilerParams(vmem_limit_bytes=VMEM_LIMIT),
         name="back",
-    )(*query_s, *key_s, *lse_parts, back_hi, back_lo, *[ref for block in done for ref in block])
+    )(*lse_parts, back_hi, back_lo, query_side, *[ref for block in done for ref in block])
 
     moves = [(along_rows, step) for step in range(row_parts)] + [(along_keys, step) for step in range(1, key_parts)]
     arrived = [deliver(part, *moves[i % count], i // count) if i else part for i, part in enumerate(pieces)]
@@ -354,18 +375,21 @@
     for across in range(1, row_parts):
         others += [fetch(sums, diagonal(across, along), 0) for along in range(1, key_parts)]
     total = small(tally_kernel, out_shape=jax.ShapeDtypeStruct((RIDE_ROWS, LANES), F32), name="tally")(sums, *others)
-    if copies & (copies - 1) == 0:
-        for bit in range(copies.bit_length() - 1):
-            total = total + lax.ppermute(total, "dp", [(i, i ^ (1 << bit)) for i in range(copies)])
+    def swapped(value, bit):
+        return lax.ppermute(value, "dp", [(i, i ^ (1 << bit)) for i in range(copies)])
+
+    for_query = [part for i, part in enumerate(arrived) if i % count < row_parts]
+    for_key = [part for i, part in enumerate(arrived) if i % count == 0 or i % count >= row_parts]
+    (grad_query,) = finish(for_query, 0, shard_rows, small)
+    if copies > 1 and copies & (copies - 1) == 0:
+        grad_key, total = finish(for_key, shard_rows, shard_rows, small, (total, swapped(total, 0)))
+        for bit in range(1, copies.bit_length() - 1):
+            total = total + swapped(total, bit)
     else:
+        (grad_key,) = finish(for_key, shard_rows, shard_rows, small)
         mine = total
         for step in range(1, copies):
             total = total + lax.ppermute(mine, "dp", [(i, (i + step) % copies) for i in range(copies)])
-
-    grad = jax.ShapeDtypeStruct((1, shard_rows, width), F32)
-    grad_query, grad_key = small(
-        functools.partial(finish_kernel, row_parts, key_parts), out_shape=(grad, grad), name="finish"
-    )(*arrived)
     samples = copies * teacher_query.shape[0] * shard_rows * length
     grad_mix, head_loss = small(
         functools.partial(close_kernel, HD_S ** (-0.5) * weight / samples, 1.0 / samples),

time: 57.6 us -> 66.3 us (1.15)
  starting transfers between devices: 14.3 us -> 24 us
  waiting for transfers between devices: 27 us -> 23.4 us
  local copies, waits for them, and re-layouts: 5.25 us -> 6.94 us
  Pallas kernels: 10.1 us -> 10.9 us
    ppermute x5, starting transfers between devices: 4.94 us -> 9.46 us  [deliver(): return lax.ppermute(value, ('head', 'seq'), pairs)]
    ppermute x6, starting transfers between devices: 7.77 us -> 10.8 us  [fetch(): lax.ppermute(value, 'seq', [(target(i, step), i) for i in range(length)])]
    ppermute x6, waiting for transfers between devices: 22.4 us -> 19.5 us  [fetch(): lax.ppermute(value, 'seq', [(target(i, step), i) for i in range(length)])]
    ppermute x2 -> x4, starting transfers between devices: 1.57 us -> 3.65 us  [the longest x2 2.09 us: fetch_student(): return [share] + [lax.ppermute(share, 'head', pairs) for pairs in turns]]
    dynamic_slice x0 -> x2, local copies, waits for them, and re-layouts: none -> 1.69 us  [fetch_student(): lax.dynamic_slice_in_dim(value, lax.axis_index('head') * columns, columns...]
    ppermute x5, waiting for transfers between devices: 1.25 us -> 0.01 us  [deliver(): return lax.ppermute(value, ('head', 'seq'), pairs)]
    pallas_call x3 -> x4, Pallas kernels: 5.36 us -> 6.16 us  [the longest x2 4.79 us: maps(): pl.pallas_call(functools.partial(maps_kernel, row_parts, count, shards, (...]
    ppermute x2 -> x4, waiting for transfers between devices: 3.31 us -> 3.95 us  [the longest x2 2.63 us: swapped(): return lax.ppermute(value, 'dp', [(i, i ^ 1 << bit) for i in range(copies)])]
  transfers between devices with their start and end apart: 13 -> 15, of which waited for: 7 -> 6; matrix products, arithmetic and copies ran while one was open for 1% -> 4% of each run, Pallas kernels for 7% -> 8%
where the time goes in v2:
time: 66.3 us; the launch traced here: 65.9 us
  starting transfers between devices  24 us (36%)
  waiting for transfers between devices  23.4 us (35%)
  Pallas kernels  10.9 us (16%)
  local copies, waits for them, and re-layouts  6.94 us (10%)
  between operations  0.69 us (1%)
    ppermute x6, waiting for transfers between devices, fetch(): lax.ppermute(value, 'seq', [(target(i, step), i) for i in range(length)])  19.5 us
    ppermute x6, starting transfers between devices, fetch(): lax.ppermute(value, 'seq', [(target(i, step), i) for i in range(length)])  10.8 us
    ppermute x5, starting transfers between devices, deliver(): return lax.ppermute(value, ('head', 'seq'), pairs)  9.46 us
    unnamed x11, local copies, waits for them, and re-layouts  5.25 us
    pallas_call x2, Pallas kernels, maps(): pl.pallas_call(functools.partial(maps_kernel, row_parts, count, shards, (...  4.79 us
    pallas_call x1, Pallas kernels, body(): pl.pallas_call(functools.partial(back_kernel, row_parts, key_parts, shard...  3.14 us
    ppermute x2, waiting for transfers between devices, swapped(): return lax.ppermute(value, 'dp', [(i, i ^ 1 << bit) for i in range(copies)])  2.63 us
    ppermute x2, starting transfers between devices, fetch_student(): return [share] + [lax.ppermute(share, 'head', pairs) for pairs in turns]  2.09 us
  transfers between devices with their start and end apart: 15, of which 6 were waited for; matrix products, arithmetic and copies ran while one was open for 4% of the time, Pallas kernels for 8%

profile of v2, /device:TPU:0, one launch (start us, length us, event | category | flops | bytes accessed | tf_op | source)
XLA Modules:
  0.0 65.9 jit_solution(1626230021019410486)
XLA Ops:
  0.6 3.1 %collective-permute-start.1 = (bf16[1,128,1536]{2,1,0:T(8,128)(2,1)}, bf16[1,128,1536]{2,1,0:T(8,128)(2,1)S(1)}, u32[]{:S(2)}, u32[]{:S(2)}) collective-permute-start(bf16[1,128,1536]{2,1,0:T(8,128)(2,1)} %refs_1_.1), channel_id=1, source_target_pairs={{4,0},{0,4},{12,8},{8,12},{5,1},{1,5},{13,9},{9,13},{6,2},{2,6},{1... | collective-permute-start | bytes 1179656 | tf_op jit(solution)/shard_map/ppermute | solution.py:286
  3.7 2.6 %collective-permute-start = (bf16[1,128,1536]{2,1,0:T(8,128)(2,1)}, bf16[1,128,1536]{2,1,0:T(8,128)(2,1)S(1)}, u32[]{:S(2)}, u32[]{:S(2)}) collective-permute-start(bf16[1,128,1536]{2,1,0:T(8,128)(2,1)} %refs_0_.1), channel_id=1, source_target_pairs={{8,0},{12,4},{0,8},{4,12},{9,1},{13,5},{1,9},{5,13},{10,2},{14,6},... | collective-permute-start | bytes 1179656 | tf_op jit(solution)/shard_map/ppermute | solution.py:286
  8.5 14.4 %collective-permute-done.4.refs_5_ = bf16[1,128,256]{2,1,0:T(8,128)(2,1)S(1)} collective-permute-done((bf16[1,128,256]{2,1,0:T(8,128)(2,1)S(1)}, bf16[1,128,256]{2,1,0:T(8,128)(2,1)S(1)}, u32[]{:S(2)}, u32[]{:S(2)}) %collective-permute-start.4) | collective-permute-done | bytes 65568 | tf_op jit(solution)/shard_map/ppermute | solution.py:286
  22.9 1.8 %collective-permute-start.5 = (bf16[1,128,256]{2,1,0:T(8,128)(2,1)S(1)}, bf16[1,128,256]{2,1,0:T(8,128)(2,1)S(1)}, u32[]{:S(2)}, u32[]{:S(2)}) collective-permute-start(bf16[1,128,256]{2,1,0:T(8,128)(2,1)S(1)} %collective-permute-done.4.refs_5_), channel_id=1, source_target_pairs={{0,16},{16,0},{1,17},{17,1},{2,18},{18,2},{3,19},{19,3},{4,20},{20... | collective-permute-start | bytes 196616 | tf_op jit(solution)/shard_map/ppermute | solution.py:301
  25.5 1.0 %copy-done = bf16[1,128,1536]{2,1,0:T(8,128)(2,1)S(1)} copy-done((bf16[1,128,1536]{2,1,0:T(8,128)(2,1)S(1)}, bf16[1,128,1536]{2,1,0:T(8,128)(2,1)}, u32[]{:S(2)}) %copy-start) | copy-done | bytes 393240
  26.5 1.0 %copy-done.1 = bf16[1,128,1536]{2,1,0:T(8,128)(2,1)S(1)} copy-done((bf16[1,128,1536]{2,1,0:T(8,128)(2,1)S(1)}, bf16[1,128,1536]{2,1,0:T(8,128)(2,1)}, u32[]{:S(2)}) %copy-start.1) | copy-done | bytes 393240
  27.5 0.9 %copy-done.2 = bf16[1,128,512]{2,1,0:T(8,128)(2,1)S(1)} copy-done((bf16[1,128,512]{2,1,0:T(8,128)(2,1)S(1)}, bf16[1,128,512]{2,1,0:T(8,128)(2,1)}, u32[]{:S(2)}) %copy-start.2) | copy-done | bytes 131096
  28.4 0.9 %copy-done.3 = bf16[1,128,512]{2,1,0:T(8,128)(2,1)S(1)} copy-done((bf16[1,128,512]{2,1,0:T(8,128)(2,1)S(1)}, bf16[1,128,512]{2,1,0:T(8,128)(2,1)}, u32[]{:S(2)}) %copy-start.3) | copy-done | bytes 131096
  30.0 1.0 %prepare.1 = (bf16[1,128,1536]{2,1,0:T(8,128)(2,1)S(1)}, bf16[1,128,1536]{2,1,0:T(8,128)(2,1)S(1)}, bf16[1,128,512]{2,1,0:T(8,128)(2,1)S(1)}, bf16[1,128,512]{2,...) custom-call(f32[12,8]{1,0:T(8,128)S(1)} %copy.9.mix_ref, ...), custom_call_target="tpu_custom_call" | custom-call | tf_op jit(solution)/shard_map/prepare/pallas_call | solution.py:70
  31.2 2.7 %maps.2 = (f32[12,128,256]{2,1,0:T(8,128)S(1)}, f32[12,128,256]{2,1,0:T(8,128)S(1)}, bf16[8,128,256]{2,1,0:T(8,128)(2,1)S(1)}, bf16[8,128,256]{2,1,0:T(8,128)(2,...) custom-call(bf16[1,128,1536]{2,1,0:T(8,128)(2,1)S(1)} %get-tuple-ele, ...), custom_call_target="tpu_custom_call" | custom-call | flops 704643072 | bytes 3145728 | tf_op jit(solution)/shard_map/maps/pallas_call | solution.py:318
  34.0 1.3 %collective-permute-done.3.refs_4_ = bf16[1,128,256]{2,1,0:T(8,128)(2,1)S(1)} collective-permute-done((bf16[1,128,256]{2,1,0:T(8,128)(2,1)S(1)}, bf16[1,128,256]{2,1,0:T(8,128)(2,1)S(1)}, u32[]{:S(2)}, u32[]{:S(2)}) %collective-permute-start.3) | collective-permute-done | bytes 65568 | tf_op jit(solution)/shard_map/ppermute | solution.py:301
  35.3 2.1 %maps.3 = (f32[12,128,256]{2,1,0:T(8,128)S(1)}, f32[12,128,256]{2,1,0:T(8,128)S(1)}, bf16[8,128,256]{2,1,0:T(8,128)(2,1)S(1)}, bf16[8,128,256]{2,1,0:T(8,128)(2,...) custom-call(bf16[1,128,1536]{2,1,0:T(8,128)(2,1)S(1)} %collective-pe, ...), custom_call_target="tpu_custom_call" | custom-call | flops 704643072 | bytes 3145728 | tf_op jit(solution)/shard_map/maps/pallas_call | solution.py:318
  37.3 2.2 %collective-permute-start.6 = (f32[2,12,256]{2,1,0:T(8,128)S(1)}, f32[2,12,256]{2,1,0:T(8,128)S(1)}, u32[]{:S(2)}, u32[]{:S(2)}) collective-permute-start(f32[2,12,256]{2,1,0:T(8,128)S(1)} %get-tuple-element.50), channel_id=1, source_target_pairs={{4,0},{0,4},{12,8},{8,12},{5,1},{1,5},{13,9},{9,13},{6,2},{2,6},{1... | collective-permute-start | bytes 73736 | tf_op jit(solution)/shard_map/ppermute | solution.py:286
  39.6 1.9 %collective-permute-done.6.refs_1_ = f32[2,12,256]{2,1,0:T(8,128)S(1)} collective-permute-done((f32[2,12,256]{2,1,0:T(8,128)S(1)}, f32[2,12,256]{2,1,0:T(8,128)S(1)}, u32[]{:S(2)}, u32[]{:S(2)}) %collective-permute-start.6) | collective-permute-done | bytes 24608 | tf_op jit(solution)/shard_map/ppermute | solution.py:286
  41.5 3.1 %back.1 = (f32[16,128]{1,0:T(8,128)S(1)}, f32[256,256]{1,0:T(8,128)S(1)}, f32[144,256]{1,0:T(8,128)S(1)}, f32[144,256]{1,0:T(8,128)S(1)}, f32[256,256]{1,0:T(8,1...) custom-call(f32[2,12,256]{2,1,0:T(8,128)S(1)} %get-tuple-element.49.refs_0_, ...), custom_call_target="tpu_custom_call" | custom-call | tf_op jit(solution)/shard_map/back/pallas_call | solution.py:349
  45.2 2.0 %collective-permute-start.7 = (f32[144,256]{1,0:T(8,128)S(1)}, f32[144,256]{1,0:T(8,128)S(1)}, u32[]{:S(2)}, u32[]{:S(2)}) collective-permute-start(f32[144,256]{1,0:T(8,128)S(1)} %get-tuple-element.68), channel_id=1, source_target_pairs={{0,4},{4,0},{8,12},{12,8},{16,20},{20,16},{24,28},{28,24},{1,5},{5... | collective-permute-start | bytes 442376 | tf_op jit(solution)/shard_map/ppermute | solution.py:294
  47.2 1.2 %collective-permute-start.10 = (f32[144,256]{1,0:T(8,128)S(1)}, f32[144,256]{1,0:T(8,128)S(1)}, u32[]{:S(2)}, u32[]{:S(2)}) collective-permute-start(f32[144,256]{1,0:T(8,128)S(1)} %get-tuple-element.71), channel_id=1, source_target_pairs={{0,8},{4,12},{8,0},{12,4},{16,24},{20,28},{24,16},{28,20},{1,9},{5... | collective-permute-start | bytes 442376 | tf_op jit(solution)/shard_map/ppermute | solution.py:294
  48.5 2.6 %collective-permute-start.11 = (f32[128,256]{1,0:T(8,128)S(1)}, f32[128,256]{1,0:T(8,128)S(1)}, u32[]{:S(2)}, u32[]{:S(2)}) collective-permute-start(f32[128,256]{1,0:T(8,128)S(1)} %get-tuple-element.72), channel_id=1, source_target_pairs={{0,24},{4,28},{8,16},{12,20},{16,8},{20,12},{24,0},{28,4},{1,25},{... | collective-permute-start | bytes 393224 | tf_op jit(solution)/shard_map/ppermute | solution.py:294
  51.1 2.5 %collective-permute-start.12 = (f32[16,128]{1,0:T(8,128)S(1)}, f32[16,128]{1,0:T(8,128)S(1)}, u32[]{:S(2)}, u32[]{:S(2)}) collective-permute-start(f32[16,128]{1,0:T(8,128)S(1)} %get-tuple-element.73.refs_0_), channel_id=1, source_target_pairs={{12,0},{8,4},{4,8},{0,12},{13,1},{9,5},{5,9},{1,13},{14,2},{10,6},... | collective-permute-start | bytes 24584 | tf_op jit(solution)/shard_map/ppermute | solution.py:286
  53.6 3.1 %collective-permute-done.12.refs_3_ = f32[16,128]{1,0:T(8,128)S(1)} collective-permute-done((f32[16,128]{1,0:T(8,128)S(1)}, f32[16,128]{1,0:T(8,128)S(1)}, u32[]{:S(2)}, u32[]{:S(2)}) %collective-permute-start.12) | collective-permute-done | bytes 8224 | tf_op jit(solution)/shard_map/ppermute | solution.py:286
  56.7 3.0 %collective-permute-start.9 = (f32[128,256]{1,0:T(8,128)S(1)}, f32[128,256]{1,0:T(8,128)S(1)}, u32[]{:S(2)}, u32[]{:S(2)}) collective-permute-start(f32[128,256]{1,0:T(8,128)S(1)} %get-tuple-element.70), channel_id=1, source_target_pairs={{0,20},{4,16},{8,28},{12,24},{16,4},{20,0},{24,12},{28,8},{1,21},{... | collective-permute-start | bytes 393224 | tf_op jit(solution)/shard_map/ppermute | solution.py:294
  59.8 1.1 %collective-permute-done.13.refs_5_ = f32[16,128]{1,0:T(8,128)S(1)} collective-permute-done((f32[16,128]{1,0:T(8,128)S(1)}, f32[16,128]{1,0:T(8,128)S(1)}, u32[]{:S(2)}, u32[]{:S(2)}) %collective-permute-start.13) | collective-permute-done | bytes 8224 | tf_op jit(solution)/shard_map/ppermute | solution.py:379
  61.6 1.5 %collective-permute-start.14 = (f32[16,128]{1,0:T(8,128)S(1)}, f32[16,128]{1,0:T(8,128)S(1)}, u32[]{:S(2)}, u32[]{:S(2)}) collective-permute-start(f32[16,128]{1,0:T(8,128)S(1)} %get-tuple-element.75), channel_id=1, source_target_pairs={{0,2},{1,3},{2,0},{3,1},{4,6},{5,7},{6,4},{7,5},{8,10},{9,11},{10,... | collective-permute-start | bytes 24584 | tf_op jit(solution)/shard_map/ppermute | solution.py:379
  63.8 1.5 %collective-permute-done.14 = f32[16,128]{1,0:T(8,128)S(1)} collective-permute-done((f32[16,128]{1,0:T(8,128)S(1)}, f32[16,128]{1,0:T(8,128)S(1)}, u32[]{:S(2)}, u32[]{:S(2)}) %collective-permute-start.14) | collective-permute-done | bytes 8224 | tf_op jit(solution)/shard_map/ppermute | solution.py:379
  (28 shorter events, 6.5 us)
Async XLA Ops:
  0.6 30.6 %collective-permute-start.1 = (bf16[1,128,1536]{2,1,0:T(8,128)(2,1)}, bf16[1,128,1536]{2,1,0:T(8,128)(2,1)S(1)}, u32[]{:S(2)}, u32[]{:S(2)}) collective-permute-start(bf16[1,128,1536]{2,1,0:T(8,128)(2,1)} %refs_1_.1), channel_id=1, source_target_pairs={{4,0},{0,4},{12,8},{8,12},{5,1},{1,5},{13,9},{9,13},{6,2},{2,6},{1... | collective-permute-start | bytes 1179656 | tf_op jit(solution)/shard_map/ppermute | solution.py:286
  3.7 31.6 %collective-permute-start = (bf16[1,128,1536]{2,1,0:T(8,128)(2,1)}, bf16[1,128,1536]{2,1,0:T(8,128)(2,1)S(1)}, u32[]{:S(2)}, u32[]{:S(2)}) collective-permute-start(bf16[1,128,1536]{2,1,0:T(8,128)(2,1)} %refs_0_.1), channel_id=1, source_target_pairs={{8,0},{12,4},{0,8},{4,12},{9,1},{13,5},{1,9},{5,13},{10,2},{14,6},... | collective-permute-start | bytes 1179656 | tf_op jit(solution)/shard_map/ppermute | solution.py:286
  7.2 15.7 %collective-permute-start.4 = (bf16[1,128,256]{2,1,0:T(8,128)(2,1)S(1)}, bf16[1,128,256]{2,1,0:T(8,128)(2,1)S(1)}, u32[]{:S(2)}, u32[]{:S(2)}) collective-permute-start(bf16[1,128,256]{2,1,0:T(8,128)(2,1)S(1)} %constant_dynamic-slice_fusion), channel_id=1, source_target_pairs={{4,0},{0,4},{12,8},{8,12},{5,1},{1,5},{13,9},{9,13},{6,2},{2,6},{1... | collective-permute-start | bytes 196616 | tf_op jit(solution)/shard_map/ppermute | solution.py:286
  8.4 22.5 %collective-permute-start.2 = (bf16[1,128,256]{2,1,0:T(8,128)(2,1)S(1)}, bf16[1,128,256]{2,1,0:T(8,128)(2,1)S(1)}, u32[]{:S(2)}, u32[]{:S(2)}) collective-permute-start(bf16[1,128,256]{2,1,0:T(8,128)(2,1)S(1)} %constant_dynamic-slice_fusion.1), channel_id=1, source_target_pairs={{8,0},{12,4},{0,8},{4,12},{9,1},{13,5},{1,9},{5,13},{10,2},{14,6},... | collective-permute-start | bytes 196616 | tf_op jit(solution)/shard_map/ppermute | solution.py:286
  22.9 8.3 %collective-permute-start.5 = (bf16[1,128,256]{2,1,0:T(8,128)(2,1)S(1)}, bf16[1,128,256]{2,1,0:T(8,128)(2,1)S(1)}, u32[]{:S(2)}, u32[]{:S(2)}) collective-permute-start(bf16[1,128,256]{2,1,0:T(8,128)(2,1)S(1)} %collective-permute-done.4.refs_5_), channel_id=1, source_target_pairs={{0,16},{16,0},{1,17},{17,1},{2,18},{18,2},{3,19},{19,3},{4,20},{20... | collective-permute-start | bytes 196616 | tf_op jit(solution)/shard_map/ppermute | solution.py:301
  25.5 1.0 %copy-start = (bf16[1,128,1536]{2,1,0:T(8,128)(2,1)S(1)}, bf16[1,128,1536]{2,1,0:T(8,128)(2,1)}, u32[]{:S(2)}) copy-start(bf16[1,128,1536]{2,1,0:T(8,128)(2,1)} %refs_1_.1) | copy-start | bytes 1179652
  26.5 1.0 %copy-start.1 = (bf16[1,128,1536]{2,1,0:T(8,128)(2,1)S(1)}, bf16[1,128,1536]{2,1,0:T(8,128)(2,1)}, u32[]{:S(2)}) copy-start(bf16[1,128,1536]{2,1,0:T(8,128)(2,1)} %refs_0_.1) | copy-start | bytes 1179652
  27.5 0.9 %copy-start.2 = (bf16[1,128,512]{2,1,0:T(8,128)(2,1)S(1)}, bf16[1,128,512]{2,1,0:T(8,128)(2,1)}, u32[]{:S(2)}) copy-start(bf16[1,128,512]{2,1,0:T(8,128)(2,1)} %refs_2_.1) | copy-start | bytes 393220
  28.4 0.9 %copy-start.3 = (bf16[1,128,512]{2,1,0:T(8,128)(2,1)S(1)}, bf16[1,128,512]{2,1,0:T(8,128)(2,1)}, u32[]{:S(2)}) copy-start(bf16[1,128,512]{2,1,0:T(8,128)(2,1)} %refs_3_.1) | copy-start | bytes 393220
  29.3 0.7 %copy-start.4 = (f32[12,8]{0,1:T(8,128)S(1)}, f32[12,8]{0,1:T(8,128)}, u32[]{:S(2)}) copy-start(f32[12,8]{0,1:T(8,128)} %param.9) | copy-start | bytes 1156
  30.9 4.3 %collective-permute-start.3 = (bf16[1,128,256]{2,1,0:T(8,128)(2,1)S(1)}, bf16[1,128,256]{2,1,0:T(8,128)(2,1)S(1)}, u32[]{:S(2)}, u32[]{:S(2)}) collective-permute-start(bf16[1,128,256]{2,1,0:T(8,128)(2,1)S(1)} %collective-permute-done.2.refs_3_), channel_id=1, source_target_pairs={{0,16},{16,0},{1,17},{17,1},{2,18},{18,2},{3,19},{19,3},{4,20},{20... | collective-permute-start | bytes 196616 | tf_op jit(solution)/shard_map/ppermute | solution.py:301
  37.3 4.1 %collective-permute-start.6 = (f32[2,12,256]{2,1,0:T(8,128)S(1)}, f32[2,12,256]{2,1,0:T(8,128)S(1)}, u32[]{:S(2)}, u32[]{:S(2)}) collective-permute-start(f32[2,12,256]{2,1,0:T(8,128)S(1)} %get-tuple-element.50), channel_id=1, source_target_pairs={{4,0},{0,4},{12,8},{8,12},{5,1},{1,5},{13,9},{9,13},{6,2},{2,6},{1... | collective-permute-start | bytes 73736 | tf_op jit(solution)/shard_map/ppermute | solution.py:286
  44.6 16.3 %collective-permute-start.8 = (f32[256,256]{1,0:T(8,128)S(1)}, f32[256,256]{1,0:T(8,128)S(1)}, u32[]{:S(2)}, u32[]{:S(2)}) collective-permute-start(f32[256,256]{1,0:T(8,128)S(1)} %get-tuple-element.69), channel_id=1, source_target_pairs={{0,16},{4,20},{8,24},{12,28},{16,0},{20,4},{24,8},{28,12},{1,17},{... | collective-permute-start | bytes 786440 | tf_op jit(solution)/shard_map/ppermute | solution.py:294
  45.2 14.5 %collective-permute-start.7 = (f32[144,256]{1,0:T(8,128)S(1)}, f32[144,256]{1,0:T(8,128)S(1)}, u32[]{:S(2)}, u32[]{:S(2)}) collective-permute-start(f32[144,256]{1,0:T(8,128)S(1)} %get-tuple-element.68), channel_id=1, source_target_pairs={{0,4},{4,0},{8,12},{12,8},{16,20},{20,16},{24,28},{28,24},{1,5},{5... | collective-permute-start | bytes 442376 | tf_op jit(solution)/shard_map/ppermute | solution.py:294
  47.2 12.5 %collective-permute-start.10 = (f32[144,256]{1,0:T(8,128)S(1)}, f32[144,256]{1,0:T(8,128)S(1)}, u32[]{:S(2)}, u32[]{:S(2)}) collective-permute-start(f32[144,256]{1,0:T(8,128)S(1)} %get-tuple-element.71), channel_id=1, source_target_pairs={{0,8},{4,12},{8,0},{12,4},{16,24},{20,28},{24,16},{28,20},{1,9},{5... | collective-permute-start | bytes 442376 | tf_op jit(solution)/shard_map/ppermute | solution.py:294
  48.5 11.3 %collective-permute-start.11 = (f32[128,256]{1,0:T(8,128)S(1)}, f32[128,256]{1,0:T(8,128)S(1)}, u32[]{:S(2)}, u32[]{:S(2)}) collective-permute-start(f32[128,256]{1,0:T(8,128)S(1)} %get-tuple-element.72), channel_id=1, source_target_pairs={{0,24},{4,28},{8,16},{12,20},{16,8},{20,12},{24,0},{28,4},{1,25},{... | collective-permute-start | bytes 393224 | tf_op jit(solution)/shard_map/ppermute | solution.py:294
  51.1 5.6 %collective-permute-start.12 = (f32[16,128]{1,0:T(8,128)S(1)}, f32[16,128]{1,0:T(8,128)S(1)}, u32[]{:S(2)}, u32[]{:S(2)}) collective-permute-start(f32[16,128]{1,0:T(8,128)S(1)} %get-tuple-element.73.refs_0_), channel_id=1, source_target_pairs={{12,0},{8,4},{4,8},{0,12},{13,1},{9,5},{5,9},{1,13},{14,2},{10,6},... | collective-permute-start | bytes 24584 | tf_op jit(solution)/shard_map/ppermute | solution.py:286
  56.7 6.4 %collective-permute-start.9 = (f32[128,256]{1,0:T(8,128)S(1)}, f32[128,256]{1,0:T(8,128)S(1)}, u32[]{:S(2)}, u32[]{:S(2)}) collective-permute-start(f32[128,256]{1,0:T(8,128)S(1)} %get-tuple-element.70), channel_id=1, source_target_pairs={{0,20},{4,16},{8,28},{12,24},{16,4},{20,0},{24,12},{28,8},{1,21},{... | collective-permute-start | bytes 393224 | tf_op jit(solution)/shard_map/ppermute | solution.py:294
  59.7 1.2 %collective-permute-start.13 = (f32[16,128]{1,0:T(8,128)S(1)}, f32[16,128]{1,0:T(8,128)S(1)}, u32[]{:S(2)}, u32[]{:S(2)}) collective-permute-start(f32[16,128]{1,0:T(8,128)S(1)} %tally.1.refs_4_), channel_id=1, source_target_pairs={{0,1},{1,0},{2,3},{3,2},{4,5},{5,4},{6,7},{7,6},{8,9},{9,8},{10,11... | collective-permute-start | bytes 24584 | tf_op jit(solution)/shard_map/ppermute | solution.py:379
  61.6 3.7 %collective-permute-start.14 = (f32[16,128]{1,0:T(8,128)S(1)}, f32[16,128]{1,0:T(8,128)S(1)}, u32[]{:S(2)}, u32[]{:S(2)}) collective-permute-start(f32[16,128]{1,0:T(8,128)S(1)} %get-tuple-element.75), channel_id=1, source_target_pairs={{0,2},{1,3},{2,0},{3,1},{4,6},{5,7},{6,4},{7,5},{8,10},{9,11},{10,... | collective-permute-start | bytes 24584 | tf_op jit(solution)/shard_map/ppermute | solution.py:379

commit v3 on v1

--- a/solution.py
+++ b/solution.py
@@ -18,6 +18,7 @@
 BACK_BLOCK = 16
 RIDE_ROWS = 16
 LANES = 128
+STUDENT_FLOPS = 64 * 10**8
 VMEM_LIMIT = 8 * 1024 * 1024
 
 F32 = jnp.float32
@@ -82,16 +83,10 @@
     return parts[0] if len(parts) == 1 else jnp.concatenate(parts, axis=0)
 
 
-def maps_kernel(row_parts, key_parts, heads, carried, *refs):
-    refs = list(refs)
-    key_t = [refs.pop(0) for _ in range(key_parts)]
-    query_t = [refs.pop(0) for _ in range(row_parts)]
-    key_s = [refs.pop(0) for _ in range(key_parts)]
-    query_s = [refs.pop(0) for _ in range(row_parts)]
-    before = refs.pop(0) if carried else None
-    lift_hi, lift_lo, exp_t, exp_l, stu_hi, stu_lo, top, kl, lse, *turned, lifted = refs
-    keys = stu_hi.shape[1]
-    rows = stu_hi.shape[2]
+def student_kernel(row_parts, key_parts, heads, *refs):
+    key_s, query_s, refs = refs[:key_parts], refs[key_parts : key_parts + row_parts], refs[key_parts + row_parts :]
+    lift_hi, lift_lo, lifted, exp_l, stu_hi, stu_lo, top, lse = refs
+    keys, rows = stu_hi.shape[1:]
     for index in range(HEADS_S):
         columns = slice(index * HD_S, (index + 1) * HD_S)
         student = dot(stacked(key_s, columns), stacked(query_s, columns), ((1,), (1,)))
@@ -103,27 +98,38 @@
         total = dot(lift_hi[...], high) + (dot(lift_hi[...], low) + dot(lift_lo[...], high))
         lifted[:, block, :] = total.reshape(heads, LIFT_BLOCK, rows)
     for head in range(heads):
+        mixed = lifted[head]
+        best = jnp.max(mixed, axis=0, keepdims=True)
+        prob = jnp.exp2(mixed - best)
+        exp_l[head] = prob
+        top[head : head + 1, :] = best
+        lse[head : head + 1, :] = best + jnp.log2(jnp.sum(prob, axis=0, keepdims=True))
+
+
+def teacher_kernel(row_parts, key_parts, heads, offset, carried, *refs):
+    key_t, query_t, refs = refs[:key_parts], refs[key_parts : key_parts + row_parts], refs[key_parts + row_parts :]
+    lifted, lse_l, *refs = refs
+    before = refs.pop(0) if carried else None
+    exp_t, top, kl, lse, *turned = refs
+    keys, rows = exp_t.shape[1:]
+    for head in range(heads):
         columns = slice(head * HD_T, (head + 1) * HD_T)
         teacher = dot(stacked(key_t, columns), stacked(query_t, columns), ((1,), (1,)))
         teacher = teacher * (HD_T ** (-0.5) * LOG2E)
-        top_t = jnp.max(teacher, axis=0, keepdims=True)
-        prob_t = jnp.exp2(teacher - top_t)
-        exp_t[head] = prob_t
-        mixed = lifted[head]
-        kl[head : head + 1, :] = jnp.sum(prob_t * (teacher - mixed), axis=0, keepdims=True)
-        top_l = jnp.max(mixed, axis=0, keepdims=True)
-        prob_l = jnp.exp2(mixed - top_l)
-        exp_l[head] = prob_l
-        top[0, head : head + 1, :] = top_t
-        top[1, head : head + 1, :] = top_l
-        for which, best, prob in ((0, top_t, prob_t), (1, top_l, prob_l)):
-            total = jnp.sum(prob, axis=0, keepdims=True)
-            if carried:
-                earlier = before[which, head : head + 1, :]
-                higher = jnp.maximum(best, earlier)
-                total = total * jnp.exp2(best - higher) + jnp.exp2(earlier - higher)
-                best = higher
-            lse[which, head : head + 1, :] = best + jnp.log2(total)
+        best = jnp.max(teacher, axis=0, keepdims=True)
+        prob = jnp.exp2(teacher - best)
+        exp_t[head] = prob
+        mixed = lifted[head, offset : offset + keys, :]
+        kl[head : head + 1, :] = jnp.sum(prob * (teacher - mixed), axis=0, keepdims=True)
+        top[head : head + 1, :] = best
+        total = jnp.sum(prob, axis=0, keepdims=True)
+        if carried:
+            earlier = before[0, head : head + 1, :]
+            higher = jnp.maximum(best, earlier)
+            total = total * jnp.exp2(best - higher) + jnp.exp2(earlier - higher)
+            best = higher
+        lse[0, head : head + 1, :] = best + jnp.log2(total)
+    lse[1] = lse_l[...]
     part = rows // row_parts
     for step, ref in enumerate(turned, 1):
         for spot in range(row_parts):
@@ -136,9 +142,9 @@
     query_s = [refs.pop(0) for _ in range(row_parts)]
     key_s = [refs.pop(0) for _ in range(key_parts)]
     lse = [refs.pop(0) for _ in range(row_parts)]
-    back_hi, back_lo = refs[:2]
-    maps = [refs[2 + 6 * i : 8 + 6 * i] for i in range(blocks)]
-    *outs, scale_t, scale_l, back, row_side, key_side, mix_acc = refs[2 + 6 * blocks :]
+    back_hi, back_lo, exp_l, stu_hi, stu_lo, top_l = refs[:6]
+    maps = [refs[6 + 3 * i : 9 + 3 * i] for i in range(blocks)]
+    *outs, scale_t, scale_l, back, row_side, key_side, mix_acc = refs[6 + 3 * blocks :]
     keys, rows = back.shape[1:]
     part, size = rows // row_parts, keys // key_parts
     sums, pieces = outs[0], outs[1:]
@@ -153,18 +159,19 @@
     loss = jnp.where(own, lse_all[1] - lse_all[0], 0.0)
     mix_acc[...] = jnp.zeros_like(mix_acc)
     offset = 0
-    for exp_t, exp_l, stu_hi, stu_lo, top, kl in maps:
-        scale_t[...] = jnp.exp2(top[0] - lse_all[0])
-        scale_l[...] = jnp.exp2(top[1] - lse_all[1])
+    scale_l[...] = jnp.exp2(top_l[...] - lse_all[1])
+    for exp_t, top_t, kl in maps:
+        scale_t[...] = jnp.exp2(top_t[...] - lse_all[0])
         loss = loss + scale_t[...] * kl[...]
         for start in range(0, exp_t.shape[1], LIFT_BLOCK):
             block = slice(start, start + LIFT_BLOCK)
+            place = slice(offset + start, offset + start + LIFT_BLOCK)
             excess = (
-                exp_l[:, block, :] * scale_l[...][:, None, :] - exp_t[:, block, :] * scale_t[...][:, None, :]
+                exp_l[:, place, :] * scale_l[...][:, None, :] - exp_t[:, block, :] * scale_t[...][:, None, :]
             )
             high, low = split(excess)
-            s_high = stu_hi[:, block, :].reshape(HEADS_S * LIFT_BLOCK, rows)
-            s_low = stu_lo[:, block, :].reshape(HEADS_S * LIFT_BLOCK, rows)
+            s_high = stu_hi[:, place, :].reshape(HEADS_S * LIFT_BLOCK, rows)
+            s_low = stu_lo[:, place, :].reshape(HEADS_S * LIFT_BLOCK, rows)
             f_high = high.reshape(heads * LIFT_BLOCK, rows)
             f_low = low.reshape(heads * LIFT_BLOCK, rows)
             over_rows = ((1,), (1,))
@@ -288,31 +295,33 @@
     *own, lift_hi, lift_lo, back_hi, back_lo = prepare(head_mix, own)
     key_t, query_t, key_s, query_s = [[mine, *rest] for mine, rest in zip(own, (key_t, query_t, key_s, query_s))]
 
-    def maps(block_t, block_s, before):
-        count = len(block_t)
-        size = count * shard_rows
-        exponents = pltpu.VMEM((heads, size, rows), F32)
-        student = pltpu.VMEM((HEADS_S, size, rows), BF16)
-        stats = pltpu.VMEM((2, heads, rows), F32)
-        cells = heads * size * rows
+    exponents = pltpu.VMEM((heads, keys, rows), F32)
+    student = pltpu.VMEM((HEADS_S, keys, rows), BF16)
+    stats = pltpu.VMEM((heads, rows), F32)
+    both = pltpu.VMEM((2, heads, rows), F32)
+    lifted, exp_l, stu_hi, stu_lo, top_l, lse_l = pl.pallas_call(
+        functools.partial(student_kernel, row_parts, key_parts, heads),
+        out_shape=(exponents, exponents, student, student, stats, stats),
+        compiler_params=pltpu.CompilerParams(vmem_limit_bytes=VMEM_LIMIT),
+        cost_estimate=pl.CostEstimate(flops=STUDENT_FLOPS, bytes_accessed=1, transcendentals=1),
+        name="student",
+    )(*key_s, *query_s, lift_hi, lift_lo)
+
+    def teacher(block_t, offset, before):
+        size = len(block_t) * shard_rows
         return pl.pallas_call(
-            functools.partial(maps_kernel, row_parts, count, heads, bool(before)),
-            out_shape=(exponents, exponents, student, student, stats, pltpu.VMEM((heads, rows), F32))
-            + (stats,) * row_parts,
-            scratch_shapes=[pltpu.VMEM((heads, size, rows), F32)],
+            functools.partial(teacher_kernel, row_parts, len(block_t), heads, offset, bool(before)),
+            out_shape=(pltpu.VMEM((heads, size, rows), F32), stats, stats, both) + (both,) * (row_parts - 1),
             compiler_params=pltpu.CompilerParams(vmem_limit_bytes=VMEM_LIMIT),
-            cost_estimate=pl.CostEstimate(
-                flops=cells * 2 * (HD_T + 3 * LIFT_BLOCK * HEADS_S), bytes_accessed=cells * 8, transcendentals=cells * 2
-            ),
-            name="maps",
-        )(*block_t, *query_t, *block_s, *query_s, *before, lift_hi, lift_lo)
+            name="teacher",
+        )(*block_t, *query_t, lifted, lse_l, *before)
 
     done, before = [], []
-    for block in (slice(0, 1), slice(1, key_parts)):
-        if key_t[block]:
-            results = maps(key_t[block], key_s[block], before)
-            done.append(results[:6])
-            before, turned = results[6:7], results[7:]
+    for first, block in ((0, key_t[:1]), (1, key_t[1:])):
+        if block:
+            results = teacher(block, first * shard_rows, before)
+            done.append(results[:3])
+            before, turned = results[3:4], results[4:]
     lse_parts = [*before] + [fetch(turned[step - 1], along_rows, row_parts - step) for step in range(1, row_parts)]
 
     weight = shard_rows * length / HEADS_T
@@ -338,7 +347,10 @@
         ],
         compiler_params=pltpu.CompilerParams(vmem_limit_bytes=VMEM_LIMIT),
         name="back",
-    )(*query_s, *key_s, *lse_parts, back_hi, back_lo, *[ref for block in done for ref in block])
+    )(
+        *query_s, *key_s, *lse_parts, back_hi, back_lo, exp_l, stu_hi, stu_lo, top_l,
+        *[ref for block in done for ref in block],
+    )
 
     moves = [(along_rows, step) for step in range(row_parts)] + [(along_keys, step) for step in range(1, key_parts)]
     arrived = [deliver(part, *moves[i % count], i // count) if i else part for i, part in enumerate(pieces)]

time: 57.6 us -> 56.5 us (0.981)
  waiting for transfers between devices: 27 us -> 26.2 us
    ppermute x6, waiting for transfers between devices: 22.4 us -> 21.6 us  [fetch(): lax.ppermute(value, 'seq', [(target(i, step), i) for i in range(length)])]
    pallas_call x2 -> x3, Pallas kernels: 4.62 us -> 4.54 us  [the longest x2 2.35 us: teacher(): pl.pallas_call(functools.partial(teacher_kernel, row_parts, len(block_t),...]
  transfers between devices with their start and end apart: 13 -> 13, of which waited for: 7 -> 8; matrix products, arithmetic and copies ran while one was open for 1% -> 1% of each run, Pallas kernels for 7% -> 9%
where the time goes in v3:
time: 56.5 us; the launch traced here: 56.2 us
  waiting for transfers between devices  26.2 us (46%)
  starting transfers between devices  14.2 us (25%)
  Pallas kernels  9.93 us (18%)
  local copies, waits for them, and re-layouts  5.25 us (9%)
  between operations  0.69 us (1%)
    ppermute x6, waiting for transfers between devices, fetch(): lax.ppermute(value, 'seq', [(target(i, step), i) for i in range(length)])  21.6 us
    ppermute x6, starting transfers between devices, fetch(): lax.ppermute(value, 'seq', [(target(i, step), i) for i in range(length)])  7.96 us
    unnamed x11, local copies, waits for them, and re-layouts  5.25 us
    ppermute x5, starting transfers between devices, deliver(): return lax.ppermute(value, ('head', 'seq'), pairs)  4.66 us
    ppermute x2, waiting for transfers between devices, body(): lax.ppermute(total, 'dp', [(i, i ^ 1 << bit) for i in range(copies)])  3.34 us
    pallas_call x1, Pallas kernels, body(): pl.pallas_call(functools.partial(back_kernel, row_parts, key_parts, shard...  3.07 us
    pallas_call x2, Pallas kernels, teacher(): pl.pallas_call(functools.partial(teacher_kernel, row_parts, len(block_t),...  2.35 us
    pallas_call x1, Pallas kernels, body(): pl.pallas_call(functools.partial(student_kernel, row_parts, key_parts, he...  2.19 us
  transfers between devices with their start and end apart: 13, of which 8 were waited for; matrix products, arithmetic and copies ran while one was open for 1% of the time, Pallas kernels for 9%

profile of v3, /device:TPU:0, one launch (start us, length us, event | category | flops | bytes accessed | tf_op | source)
XLA Modules:
  0.0 56.2 jit_solution(4583940237768865252)
XLA Ops:
  0.6 3.1 %collective-permute-start = (bf16[1,128,512]{2,1,0:T(8,128)(2,1)}, bf16[1,128,512]{2,1,0:T(8,128)(2,1)S(1)}, u32[]{:S(2)}, u32[]{:S(2)}) collective-permute-start(bf16[1,128,512]{2,1,0:T(8,128)(2,1)} %refs_3_.1), channel_id=1, source_target_pairs={{4,0},{0,4},{12,8},{8,12},{5,1},{1,5},{13,9},{9,13},{6,2},{2,6},{1... | collective-permute-start | bytes 393224 | tf_op jit(solution)/shard_map/ppermute | solution.py:280
  3.7 2.6 %collective-permute-start.1 = (bf16[1,128,512]{2,1,0:T(8,128)(2,1)}, bf16[1,128,512]{2,1,0:T(8,128)(2,1)S(1)}, u32[]{:S(2)}, u32[]{:S(2)}) collective-permute-start(bf16[1,128,512]{2,1,0:T(8,128)(2,1)} %refs_2_.1), channel_id=1, source_target_pairs={{8,0},{12,4},{0,8},{4,12},{9,1},{13,5},{1,9},{5,13},{10,2},{14,6},... | collective-permute-start | bytes 393224 | tf_op jit(solution)/shard_map/ppermute | solution.py:280
  6.8 0.8 %copy.9.mix_ref = f32[12,8]{1,0:T(8,128)S(1)} copy(f32[12,8]{0,1:T(8,128)} %param.9) | data formatting | bytes 768 | tf_op args[4]
  7.5 1.0 %copy-done = bf16[1,128,1536]{2,1,0:T(8,128)(2,1)S(1)} copy-done((bf16[1,128,1536]{2,1,0:T(8,128)(2,1)S(1)}, bf16[1,128,1536]{2,1,0:T(8,128)(2,1)}, u32[]{:S(2)}) %copy-start) | copy-done | bytes 393240
  8.5 1.0 %copy-done.1 = bf16[1,128,1536]{2,1,0:T(8,128)(2,1)S(1)} copy-done((bf16[1,128,1536]{2,1,0:T(8,128)(2,1)S(1)}, bf16[1,128,1536]{2,1,0:T(8,128)(2,1)}, u32[]{:S(2)}) %copy-start.1) | copy-done | bytes 393240
  9.5 0.9 %copy-done.2 = bf16[1,128,512]{2,1,0:T(8,128)(2,1)S(1)} copy-done((bf16[1,128,512]{2,1,0:T(8,128)(2,1)S(1)}, bf16[1,128,512]{2,1,0:T(8,128)(2,1)}, u32[]{:S(2)}) %copy-start.2) | copy-done | bytes 131096
  10.4 0.9 %copy-done.3 = bf16[1,128,512]{2,1,0:T(8,128)(2,1)S(1)} copy-done((bf16[1,128,512]{2,1,0:T(8,128)(2,1)S(1)}, bf16[1,128,512]{2,1,0:T(8,128)(2,1)}, u32[]{:S(2)}) %copy-start.3) | copy-done | bytes 131096
  12.0 1.0 %prepare.1 = (bf16[1,128,1536]{2,1,0:T(8,128)(2,1)S(1)}, bf16[1,128,1536]{2,1,0:T(8,128)(2,1)S(1)}, bf16[1,128,512]{2,1,0:T(8,128)(2,1)S(1)}, bf16[1,128,512]{2,...) custom-call(f32[12,8]{1,0:T(8,128)S(1)} %copy.9.mix_ref, ...), custom_call_target="tpu_custom_call" | custom-call | tf_op jit(solution)/shard_map/prepare/pallas_call | solution.py:71
  13.4 2.2 %student.1 = (f32[12,256,256]{2,1,0:T(8,128)S(1)}, f32[12,256,256]{2,1,0:T(8,128)S(1)}, bf16[8,256,256]{2,1,0:T(8,128)(2,1)S(1)}, bf16[8,256,256]{2,1,0:T(8,128)...) custom-call(bf16[1,128,512]{2,1,0:T(8,128)(2,1)S(1)} %get-tuple-element.39.refs_0_.refs_2_, ...), custom_call_target="tpu_custom_call" | custom-call | flops 6400000000 | bytes 1 | tf_op jit(solution)/shard_map/student/pallas_call | solution.py:302
  15.6 11.3 %collective-permute-done.3.refs_2_ = bf16[1,128,1536]{2,1,0:T(8,128)(2,1)S(1)} collective-permute-done((bf16[1,128,1536]{2,1,0:T(8,128)(2,1)}, bf16[1,128,1536]{2,1,0:T(8,128)(2,1)S(1)}, u32[]{:S(2)}, u32[]{:S(2)}) %collective-permute-start.3) | collective-permute-done | bytes 393248 | tf_op jit(solution)/shard_map/ppermute | solution.py:280
  26.9 1.5 %teacher.2 = (f32[12,128,256]{2,1,0:T(8,128)S(1)}, f32[12,256]{1,0:T(8,128)S(1)}, f32[12,256]{1,0:T(8,128)S(1)}, f32[2,12,256]{2,1,0:T(8,128)S(1)}, f32[2,12,256]{2,1,0:T(8,128)}) custom-call(bf16[1,128,1536]{2,1,0:T(8,128)(2,1)S(1)} %get-tuple-element.45.refs_0_, bf16[1,128,1536]{2,1,0:T(8,128)(2,1)S(1)} %get-tuple-element.40.refs_1_, ...), custom_call_target="tpu_custom_call" | custom-call | tf_op jit(solution)/shard_map/teacher/pallas_call | solution.py:312
  28.4 1.1 %collective-permute-done.2.refs_0_ = bf16[1,128,1536]{2,1,0:T(8,128)(2,1)S(1)} collective-permute-done((bf16[1,128,1536]{2,1,0:T(8,128)(2,1)}, bf16[1,128,1536]{2,1,0:T(8,128)(2,1)S(1)}, u32[]{:S(2)}, u32[]{:S(2)}) %collective-permute-start.2) | collective-permute-done | bytes 393248 | tf_op jit(solution)/shard_map/ppermute | solution.py:280
  29.5 0.9 %teacher.3 = (f32[12,128,256]{2,1,0:T(8,128)S(1)}, f32[12,256]{1,0:T(8,128)S(1)}, f32[12,256]{1,0:T(8,128)S(1)}, f32[2,12,256]{2,1,0:T(8,128)S(1)}, f32[2,12,256]{2,1,0:T(8,128)S(1)}) custom-call(bf16[1,128,1536]{2,1,0:T(8,128)(2,1)S(1)} %collective-permute-done.2.refs_0_, bf16[1,128,1536]{2,1,0:T(8,128)(2,1)S(1)} %get-tuple-element.40.refs_1_, ...), custom_call_target="tpu_custom_call" | custom-call | tf_op jit(solution)/shard_map/teacher/pallas_call | solution.py:312
  30.9 3.5 %collective-permute-done.4.refs_5_ = f32[2,12,256]{2,1,0:T(8,128)S(1)} collective-permute-done((f32[2,12,256]{2,1,0:T(8,128)S(1)}, f32[2,12,256]{2,1,0:T(8,128)S(1)}, u32[]{:S(2)}, u32[]{:S(2)}) %collective-permute-start.4) | collective-permute-done | bytes 24608 | tf_op jit(solution)/shard_map/ppermute | solution.py:280
  34.4 3.1 %back.1 = (f32[16,128]{1,0:T(8,128)S(1)}, f32[256,256]{1,0:T(8,128)S(1)}, f32[144,256]{1,0:T(8,128)S(1)}, f32[144,256]{1,0:T(8,128)S(1)}, f32[256,256]{1,0:T(8,1...) custom-call(bf16[1,128,512]{2,1,0:T(8,128)(2,1)S(1)} %get-tuple-element.38.refs_2_.refs_0_, ...), custom_call_target="tpu_custom_call" | custom-call | tf_op jit(solution)/shard_map/back/pallas_call | solution.py:335
  37.5 1.6 %collective-permute-start.7 = (f32[256,256]{1,0:T(8,128)S(1)}, f32[256,256]{1,0:T(8,128)S(1)}, u32[]{:S(2)}, u32[]{:S(2)}) collective-permute-start(f32[256,256]{1,0:T(8,128)S(1)} %get-tuple-element.64), channel_id=1, source_target_pairs={{0,16},{4,20},{8,24},{12,28},{16,0},{20,4},{24,8},{28,12},{1,17},{... | collective-permute-start | bytes 786440 | tf_op jit(solution)/shard_map/ppermute | solution.py:288
  39.5 2.6 %collective-permute-start.6 = (f32[144,256]{1,0:T(8,128)S(1)}, f32[144,256]{1,0:T(8,128)S(1)}, u32[]{:S(2)}, u32[]{:S(2)}) collective-permute-start(f32[144,256]{1,0:T(8,128)S(1)} %get-tuple-element.63), channel_id=1, source_target_pairs={{0,8},{4,12},{8,0},{12,4},{16,24},{20,28},{24,16},{28,20},{1,9},{5... | collective-permute-start | bytes 442376 | tf_op jit(solution)/shard_map/ppermute | solution.py:288
  42.1 1.3 %collective-permute-start.10 = (f32[16,128]{1,0:T(8,128)S(1)}, f32[16,128]{1,0:T(8,128)S(1)}, u32[]{:S(2)}, u32[]{:S(2)}) collective-permute-start(f32[16,128]{1,0:T(8,128)S(1)} %get-tuple-element.69.refs_0_), channel_id=1, source_target_pairs={{12,0},{8,4},{4,8},{0,12},{13,1},{9,5},{5,9},{1,13},{14,2},{10,6},... | collective-permute-start | bytes 24584 | tf_op jit(solution)/shard_map/ppermute | solution.py:280
  43.5 5.2 %collective-permute-done.10.refs_3_ = f32[16,128]{1,0:T(8,128)S(1)} collective-permute-done((f32[16,128]{1,0:T(8,128)S(1)}, f32[16,128]{1,0:T(8,128)S(1)}, u32[]{:S(2)}, u32[]{:S(2)}) %collective-permute-start.10) | collective-permute-done | bytes 8224 | tf_op jit(solution)/shard_map/ppermute | solution.py:280
  48.8 1.2 %collective-permute-done.11 = f32[16,128]{1,0:T(8,128)S(1)} collective-permute-done((f32[16,128]{1,0:T(8,128)S(1)}, f32[16,128]{1,0:T(8,128)S(1)}, u32[]{:S(2)}, u32[]{:S(2)}) %collective-permute-start.11) | collective-permute-done | bytes 8224 | tf_op jit(solution)/shard_map/ppermute | solution.py:371
  49.9 1.5 %collective-permute-start.12 = (f32[16,128]{1,0:T(8,128)S(1)}, f32[16,128]{1,0:T(8,128)S(1)}, u32[]{:S(2)}, u32[]{:S(2)}) collective-permute-start(f32[16,128]{1,0:T(8,128)S(1)} %add.6), channel_id=1, source_target_pairs={{0,2},{1,3},{2,0},{3,1},{4,6},{5,7},{6,4},{7,5},{8,10},{9,11},{10,... | collective-permute-start | bytes 24584 | tf_op jit(solution)/shard_map/ppermute | solution.py:371
  51.4 2.2 %collective-permute-done.12 = f32[16,128]{1,0:T(8,128)S(1)} collective-permute-done((f32[16,128]{1,0:T(8,128)S(1)}, f32[16,128]{1,0:T(8,128)S(1)}, u32[]{:S(2)}, u32[]{:S(2)}) %collective-permute-start.12) | collective-permute-done | bytes 8224 | tf_op jit(solution)/shard_map/ppermute | solution.py:371
  54.2 1.2 %collective-permute-done.9.refs_5_ = f32[128,256]{1,0:T(8,128)S(1)} collective-permute-done((f32[128,256]{1,0:T(8,128)S(1)}, f32[128,256]{1,0:T(8,128)S(1)}, u32[]{:S(2)}, u32[]{:S(2)}) %collective-permute-start.9) | collective-permute-done | bytes 131104 | tf_op jit(solution)/shard_map/ppermute | solution.py:288
  55.4 0.7 %finish.1 = (f32[1,128,256]{2,1,0:T(8,128)}, f32[1,128,256]{2,1,0:T(8,128)}) custom-call(f32[256,256]{1,0:T(8,128)S(1)} %get-tuple-element.61.refs_0_, f32[144,256]{1,0:T(8,128)S(1)} %collective-permute-done.5.refs_1_, f32[144,256]{1,0:T(8,128)S(1)} %collective-permute-done.6.refs_2_, f32[256,256]{1,0:T(8,128)S(1)} %collective-permute-done.7.refs_3_, ...), custom_call_target="tpu_custom_call" | custom-call | tf_op jit(solution)/shard_map/finish/pallas_call | solution.py:378
  (23 shorter events, 3.1 us)
Async XLA Ops:
  0.6 12.4 %collective-permute-start = (bf16[1,128,512]{2,1,0:T(8,128)(2,1)}, bf16[1,128,512]{2,1,0:T(8,128)(2,1)S(1)}, u32[]{:S(2)}, u32[]{:S(2)}) collective-permute-start(bf16[1,128,512]{2,1,0:T(8,128)(2,1)} %refs_3_.1), channel_id=1, source_target_pairs={{4,0},{0,4},{12,8},{8,12},{5,1},{1,5},{13,9},{9,13},{6,2},{2,6},{1... | collective-permute-start | bytes 393224 | tf_op jit(solution)/shard_map/ppermute | solution.py:280
  3.7 9.7 %collective-permute-start.1 = (bf16[1,128,512]{2,1,0:T(8,128)(2,1)}, bf16[1,128,512]{2,1,0:T(8,128)(2,1)S(1)}, u32[]{:S(2)}, u32[]{:S(2)}) collective-permute-start(bf16[1,128,512]{2,1,0:T(8,128)(2,1)} %refs_2_.1), channel_id=1, source_target_pairs={{8,0},{12,4},{0,8},{4,12},{9,1},{13,5},{1,9},{5,13},{10,2},{14,6},... | collective-permute-start | bytes 393224 | tf_op jit(solution)/shard_map/ppermute | solution.py:280
  6.3 20.6 %collective-permute-start.3 = (bf16[1,128,1536]{2,1,0:T(8,128)(2,1)}, bf16[1,128,1536]{2,1,0:T(8,128)(2,1)S(1)}, u32[]{:S(2)}, u32[]{:S(2)}) collective-permute-start(bf16[1,128,1536]{2,1,0:T(8,128)(2,1)} %refs_1_.1), channel_id=1, source_target_pairs={{4,0},{0,4},{12,8},{8,12},{5,1},{1,5},{13,9},{9,13},{6,2},{2,6},{1... | collective-permute-start | bytes 1179656 | tf_op jit(solution)/shard_map/ppermute | solution.py:280
  6.8 22.8 %collective-permute-start.2 = (bf16[1,128,1536]{2,1,0:T(8,128)(2,1)}, bf16[1,128,1536]{2,1,0:T(8,128)(2,1)S(1)}, u32[]{:S(2)}, u32[]{:S(2)}) collective-permute-start(bf16[1,128,1536]{2,1,0:T(8,128)(2,1)} %refs_0_.1), channel_id=1, source_target_pairs={{8,0},{12,4},{0,8},{4,12},{9,1},{13,5},{1,9},{5,13},{10,2},{14,6},... | collective-permute-start | bytes 1179656 | tf_op jit(solution)/shard_map/ppermute | solution.py:280
  7.5 1.0 %copy-start = (bf16[1,128,1536]{2,1,0:T(8,128)(2,1)S(1)}, bf16[1,128,1536]{2,1,0:T(8,128)(2,1)}, u32[]{:S(2)}) copy-start(bf16[1,128,1536]{2,1,0:T(8,128)(2,1)} %refs_1_.1) | copy-start | bytes 1179652
  8.5 1.0 %copy-start.1 = (bf16[1,128,1536]{2,1,0:T(8,128)(2,1)S(1)}, bf16[1,128,1536]{2,1,0:T(8,128)(2,1)}, u32[]{:S(2)}) copy-start(bf16[1,128,1536]{2,1,0:T(8,128)(2,1)} %refs_0_.1) | copy-start | bytes 1179652
  9.5 0.9 %copy-start.2 = (bf16[1,128,512]{2,1,0:T(8,128)(2,1)S(1)}, bf16[1,128,512]{2,1,0:T(8,128)(2,1)}, u32[]{:S(2)}) copy-start(bf16[1,128,512]{2,1,0:T(8,128)(2,1)} %refs_3_.1) | copy-start | bytes 393220
  10.4 0.9 %copy-start.3 = (bf16[1,128,512]{2,1,0:T(8,128)(2,1)S(1)}, bf16[1,128,512]{2,1,0:T(8,128)(2,1)}, u32[]{:S(2)}) copy-start(bf16[1,128,512]{2,1,0:T(8,128)(2,1)} %refs_2_.1) | copy-start | bytes 393220
  11.3 0.7 %copy-start.4 = (f32[12,8]{0,1:T(8,128)S(1)}, f32[12,8]{0,1:T(8,128)}, u32[]{:S(2)}) copy-start(f32[12,8]{0,1:T(8,128)} %param.9) | copy-start | bytes 1156
  30.4 4.0 %collective-permute-start.4 = (f32[2,12,256]{2,1,0:T(8,128)S(1)}, f32[2,12,256]{2,1,0:T(8,128)S(1)}, u32[]{:S(2)}, u32[]{:S(2)}) collective-permute-start(f32[2,12,256]{2,1,0:T(8,128)S(1)} %get-tuple-element.48), channel_id=1, source_target_pairs={{4,0},{0,4},{12,8},{8,12},{5,1},{1,5},{13,9},{9,13},{6,2},{2,6},{1... | collective-permute-start | bytes 73736 | tf_op jit(solution)/shard_map/ppermute | solution.py:280
  37.5 18.0 %collective-permute-start.7 = (f32[256,256]{1,0:T(8,128)S(1)}, f32[256,256]{1,0:T(8,128)S(1)}, u32[]{:S(2)}, u32[]{:S(2)}) collective-permute-start(f32[256,256]{1,0:T(8,128)S(1)} %get-tuple-element.64), channel_id=1, source_target_pairs={{0,16},{4,20},{8,24},{12,28},{16,0},{20,4},{24,8},{28,12},{1,17},{... | collective-permute-start | bytes 786440 | tf_op jit(solution)/shard_map/ppermute | solution.py:288
  39.1 9.6 %collective-permute-start.5 = (f32[144,256]{1,0:T(8,128)S(1)}, f32[144,256]{1,0:T(8,128)S(1)}, u32[]{:S(2)}, u32[]{:S(2)}) collective-permute-start(f32[144,256]{1,0:T(8,128)S(1)} %get-tuple-element.62), channel_id=1, source_target_pairs={{0,4},{4,0},{8,12},{12,8},{16,20},{20,16},{24,28},{28,24},{1,5},{5... | collective-permute-start | bytes 442376 | tf_op jit(solution)/shard_map/ppermute | solution.py:288
  39.5 9.2 %collective-permute-start.6 = (f32[144,256]{1,0:T(8,128)S(1)}, f32[144,256]{1,0:T(8,128)S(1)}, u32[]{:S(2)}, u32[]{:S(2)}) collective-permute-start(f32[144,256]{1,0:T(8,128)S(1)} %get-tuple-element.63), channel_id=1, source_target_pairs={{0,8},{4,12},{8,0},{12,4},{16,24},{20,28},{24,16},{28,20},{1,9},{5... | collective-permute-start | bytes 442376 | tf_op jit(solution)/shard_map/ppermute | solution.py:288
  42.1 6.6 %collective-permute-start.10 = (f32[16,128]{1,0:T(8,128)S(1)}, f32[16,128]{1,0:T(8,128)S(1)}, u32[]{:S(2)}, u32[]{:S(2)}) collective-permute-start(f32[16,128]{1,0:T(8,128)S(1)} %get-tuple-element.69.refs_0_), channel_id=1, source_target_pairs={{12,0},{8,4},{4,8},{0,12},{13,1},{9,5},{5,9},{1,13},{14,2},{10,6},... | collective-permute-start | bytes 24584 | tf_op jit(solution)/shard_map/ppermute | solution.py:280
  43.5 10.7 %collective-permute-start.8 = (f32[128,256]{1,0:T(8,128)S(1)}, f32[128,256]{1,0:T(8,128)S(1)}, u32[]{:S(2)}, u32[]{:S(2)}) collective-permute-start(f32[128,256]{1,0:T(8,128)S(1)} %get-tuple-element.65), channel_id=1, source_target_pairs={{0,20},{4,16},{8,28},{12,24},{16,4},{20,0},{24,12},{28,8},{1,21},{... | collective-permute-start | bytes 393224 | tf_op jit(solution)/shard_map/ppermute | solution.py:288
  48.7 6.8 %collective-permute-start.9 = (f32[128,256]{1,0:T(8,128)S(1)}, f32[128,256]{1,0:T(8,128)S(1)}, u32[]{:S(2)}, u32[]{:S(2)}) collective-permute-start(f32[128,256]{1,0:T(8,128)S(1)} %get-tuple-element.66), channel_id=1, source_target_pairs={{0,24},{4,28},{8,16},{12,20},{16,8},{20,12},{24,0},{28,4},{1,25},{... | collective-permute-start | bytes 393224 | tf_op jit(solution)/shard_map/ppermute | solution.py:288
  48.7 1.2 %collective-permute-start.11 = (f32[16,128]{1,0:T(8,128)S(1)}, f32[16,128]{1,0:T(8,128)S(1)}, u32[]{:S(2)}, u32[]{:S(2)}) collective-permute-start(f32[16,128]{1,0:T(8,128)S(1)} %tally.1), channel_id=1, source_target_pairs={{0,1},{1,0},{2,3},{3,2},{4,5},{5,4},{6,7},{7,6},{8,9},{9,8},{10,11... | collective-permute-start | bytes 24584 | tf_op jit(solution)/shard_map/ppermute | solution.py:371
  49.9 3.7 %collective-permute-start.12 = (f32[16,128]{1,0:T(8,128)S(1)}, f32[16,128]{1,0:T(8,128)S(1)}, u32[]{:S(2)}, u32[]{:S(2)}) collective-permute-start(f32[16,128]{1,0:T(8,128)S(1)} %add.6), channel_id=1, source_target_pairs={{0,2},{1,3},{2,0},{3,1},{4,6},{5,7},{6,4},{7,5},{8,10},{9,11},{10,... | collective-permute-start | bytes 24584 | tf_op jit(solution)/shard_map/ppermute | solution.py:371

commit v4 on v3

--- a/solution.py
+++ b/solution.py
@@ -237,10 +237,17 @@
     total[...] = value
 
 
-def finish_kernel(row_parts, key_parts, *refs):
-    *pieces, grad_query, grad_key = refs
+def finish_kernel(row_parts, key_parts, addends, mix_scale, loss_scale, *refs):
+    *pieces, grad_query, grad_key, grad_mix, head_loss = refs
+    terms, pieces = pieces[:addends], pieces[addends:]
     part = grad_query.shape[1]
+    heads = grad_mix.shape[1]
     count = row_parts + key_parts - 1
+    total = terms[0][...]
+    for ref in terms[1:]:
+        total = total + ref[...]
+    grad_mix[...] = total[:HEADS_S, :heads] * mix_scale
+    head_loss[...] = total[HEADS_S : HEADS_S + 1, :heads] * loss_scale
     on_rows, on_keys = [], []
     for i, ref in enumerate(pieces):
         if i % count == 0:
@@ -254,12 +261,6 @@
     grad_key[0] = sum(on_keys[1:], on_keys[0])
 
 
-def close_kernel(mix_scale, loss_scale, total, grad_mix, head_loss):
-    heads = grad_mix.shape[1]
-    grad_mix[...] = total[:HEADS_S, :heads] * mix_scale
-    head_loss[...] = total[HEADS_S : HEADS_S + 1, :heads] * loss_scale
-
-
 def body(teacher_query, teacher_key, student_query, student_key, head_mix):
     shard_rows = teacher_query.shape[1]
     heads = head_mix.shape[0]
@@ -331,7 +332,8 @@
     shapes = []
     for shard in range(shards):
         extra = ride if shard == 0 else 0
-        shapes += [(2 * shard_rows, width)] + [(shard_rows + extra, width)] * (count - 1)
+        shapes += [(2 * shard_rows, width)] + [(shard_rows + extra, width)] * (row_parts - 1)
+        shapes += [(shard_rows, width)] * (key_parts - 1)
     sums, *pieces = pl.pallas_call(
         functools.partial(
             back_kernel, row_parts, key_parts, shards, len(done), heads, weight * HD_S ** (-0.5)
@@ -356,34 +358,35 @@
     arrived = [deliver(part, *moves[i % count], i // count) if i else part for i, part in enumerate(pieces)]
     small = functools.partial(pl.pallas_call, compiler_params=pltpu.CompilerParams(vmem_limit_bytes=VMEM_LIMIT // 4))
 
-    def diagonal(across, along):
-        return lambda position, _: along_keys(along_rows(position, across), along)
-
-    if ride:
-        others = arrived[1:count]
-    else:
-        others = [fetch(sums, target, step) for target, step in moves[1:]]
-    for across in range(1, row_parts):
-        others += [fetch(sums, diagonal(across, along), 0) for along in range(1, key_parts)]
+    def everyone(value, axis):
+        size = lax.axis_size(axis)
+        if size & (size - 1) == 0:
+            for bit in range(size.bit_length() - 1):
+                value = value + lax.ppermute(value, axis, [(i, i ^ (1 << bit)) for i in range(size)])
+            return value
+        mine = value
+        for step in range(1, size):
+            value = value + lax.ppermute(mine, axis, [(i, (i + step) % size) for i in range(size)])
+        return value
+
+    others = arrived[1:row_parts] if ride else [fetch(sums, along_rows, step) for step in range(1, row_parts)]
     total = small(tally_kernel, out_shape=jax.ShapeDtypeStruct((RIDE_ROWS, LANES), F32), name="tally")(sums, *others)
-    if copies & (copies - 1) == 0:
-        for bit in range(copies.bit_length() - 1):
-            total = total + lax.ppermute(total, "dp", [(i, i ^ (1 << bit)) for i in range(copies)])
-    else:
-        mine = total
-        for step in range(1, copies):
-            total = total + lax.ppermute(mine, "dp", [(i, (i + step) % copies) for i in range(copies)])
+    total = everyone(total, "dp")
+    terms = [total] + [fetch(total, along_keys, step) for step in range(1, key_parts)]
 
     grad = jax.ShapeDtypeStruct((1, shard_rows, width), F32)
-    grad_query, grad_key = small(
-        functools.partial(finish_kernel, row_parts, key_parts), out_shape=(grad, grad), name="finish"
-    )(*arrived)
     samples = copies * teacher_query.shape[0] * shard_rows * length
-    grad_mix, head_loss = small(
-        functools.partial(close_kernel, HD_S ** (-0.5) * weight / samples, 1.0 / samples),
-        out_shape=(jax.ShapeDtypeStruct((HEADS_S, heads), F32), jax.ShapeDtypeStruct((1, heads), F32)),
-        name="close",
-    )(total)
+    scales = (HD_S ** (-0.5) * weight / samples, 1.0 / samples)
+    grad_query, grad_key, grad_mix, head_loss = small(
+        functools.partial(finish_kernel, row_parts, key_parts, len(terms), *scales),
+        out_shape=(
+            grad,
+            grad,
+            jax.ShapeDtypeStruct((HEADS_S, heads), F32),
+            jax.ShapeDtypeStruct((1, heads), F32),
+        ),
+        name="finish",
+    )(*terms, *arrived)
     return (grad_query, grad_key, grad_mix.T, head_loss[0])
 
 

time: 56.5 us -> 58 us (1.027)
  starting transfers between devices: 14.2 us -> 16.5 us
  Pallas kernels: 9.93 us -> 9.34 us
    ppermute x5, starting transfers between devices: 4.66 us -> 7.47 us  [deliver(): return lax.ppermute(value, ('head', 'seq'), pairs)]
    ppermute x6, waiting for transfers between devices: 21.6 us -> 20 us  [fetch(): lax.ppermute(value, 'seq', [(target(i, step), i) for i in range(length)])]
    ppermute x5, waiting for transfers between devices: 1.25 us -> 2.56 us  [deliver(): return lax.ppermute(value, ('head', 'seq'), pairs)]
    pallas_call x2 -> x1, Pallas kernels: 1.35 us -> 0.76 us  [body(): small(functools.partial(finish_kernel, row_parts, key_parts, len(terms),...]
  transfers between devices with their start and end apart: 13 -> 13, of which waited for: 8 -> 8; matrix products, arithmetic and copies ran while one was open for 1% -> 1% of each run, Pallas kernels for 9% -> 8%
where the time goes in v4:
time: 58 us; the launch traced here: 57.7 us
  waiting for transfers between devices  25.9 us (45%)
  starting transfers between devices  16.5 us (28%)
  Pallas kernels  9.34 us (16%)
  local copies, waits for them, and re-layouts  5.25 us (9%)
  between operations  0.67 us (1%)
    ppermute x6, waiting for transfers between devices, fetch(): lax.ppermute(value, 'seq', [(target(i, step), i) for i in range(length)])  20 us
    ppermute x6, starting transfers between devices, fetch(): lax.ppermute(value, 'seq', [(target(i, step), i) for i in range(length)])  7.59 us
    ppermute x5, starting transfers between devices, deliver(): return lax.ppermute(value, ('head', 'seq'), pairs)  7.47 us
    unnamed x11, local copies, waits for them, and re-layouts  5.25 us
    ppermute x2, waiting for transfers between devices, everyone(): lax.ppermute(value, axis, [(i, i ^ 1 << bit) for i in range(size)])  3.33 us
    pallas_call x1, Pallas kernels, body(): pl.pallas_call(functools.partial(back_kernel, row_parts, key_parts, shard...  3.07 us
    ppermute x5, waiting for transfers between devices, deliver(): return lax.ppermute(value, ('head', 'seq'), pairs)  2.56 us
    pallas_call x2, Pallas kernels, teacher(): pl.pallas_call(functools.partial(teacher_kernel, row_parts, len(block_t),...  2.35 us
  transfers between devices with their start and end apart: 13, of which 8 were waited for; matrix products, arithmetic and copies ran while one was open for 1% of the time, Pallas kernels for 8%

profile of v4, /device:TPU:0, one launch (start us, length us, event | category | flops | bytes accessed | tf_op | source)
XLA Modules:
  0.0 57.7 jit_solution(7685165896557035971)
XLA Ops:
  0.6 3.1 %collective-permute-start = (bf16[1,128,512]{2,1,0:T(8,128)(2,1)}, bf16[1,128,512]{2,1,0:T(8,128)(2,1)S(1)}, u32[]{:S(2)}, u32[]{:S(2)}) collective-permute-start(bf16[1,128,512]{2,1,0:T(8,128)(2,1)} %refs_3_.1), channel_id=1, source_target_pairs={{4,0},{0,4},{12,8},{8,12},{5,1},{1,5},{13,9},{9,13},{6,2},{2,6},{1... | collective-permute-start | bytes 393224 | tf_op jit(solution)/shard_map/ppermute | solution.py:281
  3.7 2.6 %collective-permute-start.1 = (bf16[1,128,512]{2,1,0:T(8,128)(2,1)}, bf16[1,128,512]{2,1,0:T(8,128)(2,1)S(1)}, u32[]{:S(2)}, u32[]{:S(2)}) collective-permute-start(bf16[1,128,512]{2,1,0:T(8,128)(2,1)} %refs_2_.1), channel_id=1, source_target_pairs={{8,0},{12,4},{0,8},{4,12},{9,1},{13,5},{1,9},{5,13},{10,2},{14,6},... | collective-permute-start | bytes 393224 | tf_op jit(solution)/shard_map/ppermute | solution.py:281
  6.8 0.8 %copy.9.mix_ref = f32[12,8]{1,0:T(8,128)S(1)} copy(f32[12,8]{0,1:T(8,128)} %param.9) | data formatting | bytes 768 | tf_op args[4]
  7.5 1.0 %copy-done = bf16[1,128,1536]{2,1,0:T(8,128)(2,1)S(1)} copy-done((bf16[1,128,1536]{2,1,0:T(8,128)(2,1)S(1)}, bf16[1,128,1536]{2,1,0:T(8,128)(2,1)}, u32[]{:S(2)}) %copy-start) | copy-done | bytes 393240
  8.5 1.0 %copy-done.1 = bf16[1,128,1536]{2,1,0:T(8,128)(2,1)S(1)} copy-done((bf16[1,128,1536]{2,1,0:T(8,128)(2,1)S(1)}, bf16[1,128,1536]{2,1,0:T(8,128)(2,1)}, u32[]{:S(2)}) %copy-start.1) | copy-done | bytes 393240
  9.5 0.9 %copy-done.2 = bf16[1,128,512]{2,1,0:T(8,128)(2,1)S(1)} copy-done((bf16[1,128,512]{2,1,0:T(8,128)(2,1)S(1)}, bf16[1,128,512]{2,1,0:T(8,128)(2,1)}, u32[]{:S(2)}) %copy-start.2) | copy-done | bytes 131096
  10.4 0.9 %copy-done.3 = bf16[1,128,512]{2,1,0:T(8,128)(2,1)S(1)} copy-done((bf16[1,128,512]{2,1,0:T(8,128)(2,1)S(1)}, bf16[1,128,512]{2,1,0:T(8,128)(2,1)}, u32[]{:S(2)}) %copy-start.3) | copy-done | bytes 131096
  12.0 1.0 %prepare.1 = (bf16[1,128,1536]{2,1,0:T(8,128)(2,1)S(1)}, bf16[1,128,1536]{2,1,0:T(8,128)(2,1)S(1)}, bf16[1,128,512]{2,1,0:T(8,128)(2,1)S(1)}, bf16[1,128,512]{2,...) custom-call(f32[12,8]{1,0:T(8,128)S(1)} %copy.9.mix_ref, ...), custom_call_target="tpu_custom_call" | custom-call | tf_op jit(solution)/shard_map/prepare/pallas_call | solution.py:71
  13.4 2.2 %student.1 = (f32[12,256,256]{2,1,0:T(8,128)S(1)}, f32[12,256,256]{2,1,0:T(8,128)S(1)}, bf16[8,256,256]{2,1,0:T(8,128)(2,1)S(1)}, bf16[8,256,256]{2,1,0:T(8,128)...) custom-call(bf16[1,128,512]{2,1,0:T(8,128)(2,1)S(1)} %get-tuple-element.39.refs_0_.refs_2_, ...), custom_call_target="tpu_custom_call" | custom-call | flops 6400000000 | bytes 1 | tf_op jit(solution)/shard_map/student/pallas_call | solution.py:303
  15.6 11.3 %collective-permute-done.3.refs_2_ = bf16[1,128,1536]{2,1,0:T(8,128)(2,1)S(1)} collective-permute-done((bf16[1,128,1536]{2,1,0:T(8,128)(2,1)}, bf16[1,128,1536]{2,1,0:T(8,128)(2,1)S(1)}, u32[]{:S(2)}, u32[]{:S(2)}) %collective-permute-start.3) | collective-permute-done | bytes 393248 | tf_op jit(solution)/shard_map/ppermute | solution.py:281
  26.9 1.5 %teacher.2 = (f32[12,128,256]{2,1,0:T(8,128)S(1)}, f32[12,256]{1,0:T(8,128)S(1)}, f32[12,256]{1,0:T(8,128)S(1)}, f32[2,12,256]{2,1,0:T(8,128)S(1)}, f32[2,12,256]{2,1,0:T(8,128)}) custom-call(bf16[1,128,1536]{2,1,0:T(8,128)(2,1)S(1)} %get-tuple-element.45.refs_0_, bf16[1,128,1536]{2,1,0:T(8,128)(2,1)S(1)} %get-tuple-element.40.refs_1_, ...), custom_call_target="tpu_custom_call" | custom-call | tf_op jit(solution)/shard_map/teacher/pallas_call | solution.py:313
  28.4 1.1 %collective-permute-done.2.refs_0_ = bf16[1,128,1536]{2,1,0:T(8,128)(2,1)S(1)} collective-permute-done((bf16[1,128,1536]{2,1,0:T(8,128)(2,1)}, bf16[1,128,1536]{2,1,0:T(8,128)(2,1)S(1)}, u32[]{:S(2)}, u32[]{:S(2)}) %collective-permute-start.2) | collective-permute-done | bytes 393248 | tf_op jit(solution)/shard_map/ppermute | solution.py:281
  29.5 0.9 %teacher.3 = (f32[12,128,256]{2,1,0:T(8,128)S(1)}, f32[12,256]{1,0:T(8,128)S(1)}, f32[12,256]{1,0:T(8,128)S(1)}, f32[2,12,256]{2,1,0:T(8,128)S(1)}, f32[2,12,256]{2,1,0:T(8,128)S(1)}) custom-call(bf16[1,128,1536]{2,1,0:T(8,128)(2,1)S(1)} %collective-permute-done.2.refs_0_, bf16[1,128,1536]{2,1,0:T(8,128)(2,1)S(1)} %get-tuple-element.40.refs_1_, ...), custom_call_target="tpu_custom_call" | custom-call | tf_op jit(solution)/shard_map/teacher/pallas_call | solution.py:313
  30.9 3.5 %collective-permute-done.4.refs_5_ = f32[2,12,256]{2,1,0:T(8,128)S(1)} collective-permute-done((f32[2,12,256]{2,1,0:T(8,128)S(1)}, f32[2,12,256]{2,1,0:T(8,128)S(1)}, u32[]{:S(2)}, u32[]{:S(2)}) %collective-permute-start.4) | collective-permute-done | bytes 24608 | tf_op jit(solution)/shard_map/ppermute | solution.py:281
  34.4 3.1 %back.1 = (f32[16,128]{1,0:T(8,128)S(1)}, f32[256,256]{1,0:T(8,128)S(1)}, f32[144,256]{1,0:T(8,128)S(1)}, f32[128,256]{1,0:T(8,128)S(1)}, f32[256,256]{1,0:T(8,1...) custom-call(bf16[1,128,512]{2,1,0:T(8,128)(2,1)S(1)} %get-tuple-element.38.refs_2_.refs_0_, ...), custom_call_target="tpu_custom_call" | custom-call | tf_op jit(solution)/shard_map/back/pallas_call | solution.py:337
  37.5 1.6 %collective-permute-start.10 = (f32[256,256]{1,0:T(8,128)S(1)}, f32[256,256]{1,0:T(8,128)S(1)}, u32[]{:S(2)}, u32[]{:S(2)}) collective-permute-start(f32[256,256]{1,0:T(8,128)S(1)} %get-tuple-element.65), channel_id=1, source_target_pairs={{0,16},{4,20},{8,24},{12,28},{16,0},{20,4},{24,8},{28,12},{1,17},{... | collective-permute-start | bytes 786440 | tf_op jit(solution)/shard_map/ppermute | solution.py:289
  39.5 2.6 %collective-permute-start.9 = (f32[128,256]{1,0:T(8,128)S(1)}, f32[128,256]{1,0:T(8,128)S(1)}, u32[]{:S(2)}, u32[]{:S(2)}) collective-permute-start(f32[128,256]{1,0:T(8,128)S(1)} %get-tuple-element.64), channel_id=1, source_target_pairs={{0,8},{4,12},{8,0},{12,4},{16,24},{20,28},{24,16},{28,20},{1,9},{5... | collective-permute-start | bytes 393224 | tf_op jit(solution)/shard_map/ppermute | solution.py:289
  42.1 2.8 %collective-permute-start.12 = (f32[128,256]{1,0:T(8,128)S(1)}, f32[128,256]{1,0:T(8,128)S(1)}, u32[]{:S(2)}, u32[]{:S(2)}) collective-permute-start(f32[128,256]{1,0:T(8,128)S(1)} %get-tuple-element.67), channel_id=1, source_target_pairs={{0,24},{4,28},{8,16},{12,20},{16,8},{20,12},{24,0},{28,4},{1,25},{... | collective-permute-start | bytes 393224 | tf_op jit(solution)/shard_map/ppermute | solution.py:289
  44.9 2.5 %collective-permute-done.5.refs_1_.refs_3_ = f32[144,256]{1,0:T(8,128)S(1)} collective-permute-done((f32[144,256]{1,0:T(8,128)S(1)}, f32[144,256]{1,0:T(8,128)S(1)}, u32[]{:S(2)}, u32[]{:S(2)}) %collective-permute-start.5) | collective-permute-done | bytes 147488 | tf_op jit(solution)/shard_map/ppermute | solution.py:289
  47.5 1.2 %collective-permute-done.6 = f32[16,128]{1,0:T(8,128)S(1)} collective-permute-done((f32[16,128]{1,0:T(8,128)S(1)}, f32[16,128]{1,0:T(8,128)S(1)}, u32[]{:S(2)}, u32[]{:S(2)}) %collective-permute-start.6) | collective-permute-done | bytes 8224 | tf_op jit(solution)/shard_map/ppermute | solution.py:365
  48.7 1.5 %collective-permute-start.7 = (f32[16,128]{1,0:T(8,128)S(1)}, f32[16,128]{1,0:T(8,128)S(1)}, u32[]{:S(2)}, u32[]{:S(2)}) collective-permute-start(f32[16,128]{1,0:T(8,128)S(1)} %add.6), channel_id=1, source_target_pairs={{0,2},{1,3},{2,0},{3,1},{4,6},{5,7},{6,4},{7,5},{8,10},{9,11},{10,... | collective-permute-start | bytes 24584 | tf_op jit(solution)/shard_map/ppermute | solution.py:365
  50.2 2.2 %collective-permute-done.7 = f32[16,128]{1,0:T(8,128)S(1)} collective-permute-done((f32[16,128]{1,0:T(8,128)S(1)}, f32[16,128]{1,0:T(8,128)S(1)}, u32[]{:S(2)}, u32[]{:S(2)}) %collective-permute-start.7) | collective-permute-done | bytes 8224 | tf_op jit(solution)/shard_map/ppermute | solution.py:365
  52.3 1.0 %collective-permute-start.8 = (f32[16,128]{1,0:T(8,128)S(1)}, f32[16,128]{1,0:T(8,128)S(1)}, u32[]{:S(2)}, u32[]{:S(2)}) collective-permute-start(f32[16,128]{1,0:T(8,128)S(1)} %add.7.refs_0_), channel_id=1, source_target_pairs={{8,0},{12,4},{0,8},{4,12},{9,1},{13,5},{1,9},{5,13},{10,2},{14,6},... | collective-permute-start | bytes 24584 | tf_op jit(solution)/shard_map/ppermute | solution.py:281
  53.3 3.6 %collective-permute-done.8.refs_1_ = f32[16,128]{1,0:T(8,128)S(1)} collective-permute-done((f32[16,128]{1,0:T(8,128)S(1)}, f32[16,128]{1,0:T(8,128)S(1)}, u32[]{:S(2)}, u32[]{:S(2)}) %collective-permute-start.8) | collective-permute-done | bytes 8224 | tf_op jit(solution)/shard_map/ppermute | solution.py:281
  (22 shorter events, 3.2 us)
Async XLA Ops:
  0.6 12.4 %collective-permute-start = (bf16[1,128,512]{2,1,0:T(8,128)(2,1)}, bf16[1,128,512]{2,1,0:T(8,128)(2,1)S(1)}, u32[]{:S(2)}, u32[]{:S(2)}) collective-permute-start(bf16[1,128,512]{2,1,0:T(8,128)(2,1)} %refs_3_.1), channel_id=1, source_target_pairs={{4,0},{0,4},{12,8},{8,12},{5,1},{1,5},{13,9},{9,13},{6,2},{2,6},{1... | collective-permute-start | bytes 393224 | tf_op jit(solution)/shard_map/ppermute | solution.py:281
  3.7 9.7 %collective-permute-start.1 = (bf16[1,128,512]{2,1,0:T(8,128)(2,1)}, bf16[1,128,512]{2,1,0:T(8,128)(2,1)S(1)}, u32[]{:S(2)}, u32[]{:S(2)}) collective-permute-start(bf16[1,128,512]{2,1,0:T(8,128)(2,1)} %refs_2_.1), channel_id=1, source_target_pairs={{8,0},{12,4},{0,8},{4,12},{9,1},{13,5},{1,9},{5,13},{10,2},{14,6},... | collective-permute-start | bytes 393224 | tf_op jit(solution)/shard_map/ppermute | solution.py:281
  6.3 20.6 %collective-permute-start.3 = (bf16[1,128,1536]{2,1,0:T(8,128)(2,1)}, bf16[1,128,1536]{2,1,0:T(8,128)(2,1)S(1)}, u32[]{:S(2)}, u32[]{:S(2)}) collective-permute-start(bf16[1,128,1536]{2,1,0:T(8,128)(2,1)} %refs_1_.1), channel_id=1, source_target_pairs={{4,0},{0,4},{12,8},{8,12},{5,1},{1,5},{13,9},{9,13},{6,2},{2,6},{1... | collective-permute-start | bytes 1179656 | tf_op jit(solution)/shard_map/ppermute | solution.py:281
  6.8 22.8 %collective-permute-start.2 = (bf16[1,128,1536]{2,1,0:T(8,128)(2,1)}, bf16[1,128,1536]{2,1,0:T(8,128)(2,1)S(1)}, u32[]{:S(2)}, u32[]{:S(2)}) collective-permute-start(bf16[1,128,1536]{2,1,0:T(8,128)(2,1)} %refs_0_.1), channel_id=1, source_target_pairs={{8,0},{12,4},{0,8},{4,12},{9,1},{13,5},{1,9},{5,13},{10,2},{14,6},... | collective-permute-start | bytes 1179656 | tf_op jit(solution)/shard_map/ppermute | solution.py:281
  7.5 1.0 %copy-start = (bf16[1,128,1536]{2,1,0:T(8,128)(2,1)S(1)}, bf16[1,128,1536]{2,1,0:T(8,128)(2,1)}, u32[]{:S(2)}) copy-start(bf16[1,128,1536]{2,1,0:T(8,128)(2,1)} %refs_1_.1) | copy-start | bytes 1179652
  8.5 1.0 %copy-start.1 = (bf16[1,128,1536]{2,1,0:T(8,128)(2,1)S(1)}, bf16[1,128,1536]{2,1,0:T(8,128)(2,1)}, u32[]{:S(2)}) copy-start(bf16[1,128,1536]{2,1,0:T(8,128)(2,1)} %refs_0_.1) | copy-start | bytes 1179652
  9.5 0.9 %copy-start.2 = (bf16[1,128,512]{2,1,0:T(8,128)(2,1)S(1)}, bf16[1,128,512]{2,1,0:T(8,128)(2,1)}, u32[]{:S(2)}) copy-start(bf16[1,128,512]{2,1,0:T(8,128)(2,1)} %refs_3_.1) | copy-start | bytes 393220
  10.4 0.9 %copy-start.3 = (bf16[1,128,512]{2,1,0:T(8,128)(2,1)S(1)}, bf16[1,128,512]{2,1,0:T(8,128)(2,1)}, u32[]{:S(2)}) copy-start(bf16[1,128,512]{2,1,0:T(8,128)(2,1)} %refs_2_.1) | copy-start | bytes 393220
  11.3 0.7 %copy-start.4 = (f32[12,8]{0,1:T(8,128)S(1)}, f32[12,8]{0,1:T(8,128)}, u32[]{:S(2)}) copy-start(f32[12,8]{0,1:T(8,128)} %param.9) | copy-start | bytes 1156
  30.4 4.0 %collective-permute-start.4 = (f32[2,12,256]{2,1,0:T(8,128)S(1)}, f32[2,12,256]{2,1,0:T(8,128)S(1)}, u32[]{:S(2)}, u32[]{:S(2)}) collective-permute-start(f32[2,12,256]{2,1,0:T(8,128)S(1)} %get-tuple-element.48), channel_id=1, source_target_pairs={{4,0},{0,4},{12,8},{8,12},{5,1},{1,5},{13,9},{9,13},{6,2},{2,6},{1... | collective-permute-start | bytes 73736 | tf_op jit(solution)/shard_map/ppermute | solution.py:281
  37.5 19.5 %collective-permute-start.10 = (f32[256,256]{1,0:T(8,128)S(1)}, f32[256,256]{1,0:T(8,128)S(1)}, u32[]{:S(2)}, u32[]{:S(2)}) collective-permute-start(f32[256,256]{1,0:T(8,128)S(1)} %get-tuple-element.65), channel_id=1, source_target_pairs={{0,16},{4,20},{8,24},{12,28},{16,0},{20,4},{24,8},{28,12},{1,17},{... | collective-permute-start | bytes 786440 | tf_op jit(solution)/shard_map/ppermute | solution.py:289
  39.1 8.4 %collective-permute-start.5 = (f32[144,256]{1,0:T(8,128)S(1)}, f32[144,256]{1,0:T(8,128)S(1)}, u32[]{:S(2)}, u32[]{:S(2)}) collective-permute-start(f32[144,256]{1,0:T(8,128)S(1)} %get-tuple-element.62), channel_id=1, source_target_pairs={{0,4},{4,0},{8,12},{12,8},{16,20},{20,16},{24,28},{28,24},{1,5},{5... | collective-permute-start | bytes 442376 | tf_op jit(solution)/shard_map/ppermute | solution.py:289
  39.5 13.8 %collective-permute-start.9 = (f32[128,256]{1,0:T(8,128)S(1)}, f32[128,256]{1,0:T(8,128)S(1)}, u32[]{:S(2)}, u32[]{:S(2)}) collective-permute-start(f32[128,256]{1,0:T(8,128)S(1)} %get-tuple-element.64), channel_id=1, source_target_pairs={{0,8},{4,12},{8,0},{12,4},{16,24},{20,28},{24,16},{28,20},{1,9},{5... | collective-permute-start | bytes 393224 | tf_op jit(solution)/shard_map/ppermute | solution.py:289
  42.1 11.2 %collective-permute-start.11 = (f32[128,256]{1,0:T(8,128)S(1)}, f32[128,256]{1,0:T(8,128)S(1)}, u32[]{:S(2)}, u32[]{:S(2)}) collective-permute-start(f32[128,256]{1,0:T(8,128)S(1)} %get-tuple-element.66), channel_id=1, source_target_pairs={{0,20},{4,16},{8,28},{12,24},{16,4},{20,0},{24,12},{28,8},{1,21},{... | collective-permute-start | bytes 393224 | tf_op jit(solution)/shard_map/ppermute | solution.py:289
  42.1 11.2 %collective-permute-start.12 = (f32[128,256]{1,0:T(8,128)S(1)}, f32[128,256]{1,0:T(8,128)S(1)}, u32[]{:S(2)}, u32[]{:S(2)}) collective-permute-start(f32[128,256]{1,0:T(8,128)S(1)} %get-tuple-element.67), channel_id=1, source_target_pairs={{0,24},{4,28},{8,16},{12,20},{16,8},{20,12},{24,0},{28,4},{1,25},{... | collective-permute-start | bytes 393224 | tf_op jit(solution)/shard_map/ppermute | solution.py:289
  47.5 1.2 %collective-permute-start.6 = (f32[16,128]{1,0:T(8,128)S(1)}, f32[16,128]{1,0:T(8,128)S(1)}, u32[]{:S(2)}, u32[]{:S(2)}) collective-permute-start(f32[16,128]{1,0:T(8,128)S(1)} %tally.1), channel_id=1, source_target_pairs={{0,1},{1,0},{2,3},{3,2},{4,5},{5,4},{6,7},{7,6},{8,9},{9,8},{10,11... | collective-permute-start | bytes 24584 | tf_op jit(solution)/shard_map/ppermute | solution.py:365
  48.7 3.7 %collective-permute-start.7 = (f32[16,128]{1,0:T(8,128)S(1)}, f32[16,128]{1,0:T(8,128)S(1)}, u32[]{:S(2)}, u32[]{:S(2)}) collective-permute-start(f32[16,128]{1,0:T(8,128)S(1)} %add.6), channel_id=1, source_target_pairs={{0,2},{1,3},{2,0},{3,1},{4,6},{5,7},{6,4},{7,5},{8,10},{9,11},{10,... | collective-permute-start | bytes 24584 | tf_op jit(solution)/shard_map/ppermute | solution.py:365
  52.3 4.6 %collective-permute-start.8 = (f32[16,128]{1,0:T(8,128)S(1)}, f32[16,128]{1,0:T(8,128)S(1)}, u32[]{:S(2)}, u32[]{:S(2)}) collective-permute-start(f32[16,128]{1,0:T(8,128)S(1)} %add.7.refs_0_), channel_id=1, source_target_pairs={{8,0},{12,4},{0,8},{4,12},{9,1},{13,5},{1,9},{5,13},{10,2},{14,6},... | collective-permute-start | bytes 24584 | tf_op jit(solution)/shard_map/ppermute | solution.py:281

commit v5 on v3

--- a/solution.py
+++ b/solution.py
@@ -23,10 +23,17 @@
 
 F32 = jnp.float32
 BF16 = jnp.bfloat16
+F16 = jnp.float16
+MIX_TOP = 0.25
+VALUE_TOP = 6.0
 
 
 def dot(lhs, rhs, dims=((1,), (0,))):
     return lax.dot_general(lhs, rhs, (dims, ((), ())), preferred_element_type=F32)
+
+
+def room(bound):
+    return 2.0 ** math.floor(math.log2(float(jnp.finfo(F16).max) / (1.01 * bound)))
 
 
 def split(value):
@@ -137,7 +144,7 @@
             ref[:, :, spot * part : (spot + 1) * part] = lse[:, :, source : source + part]
 
 
-def back_kernel(row_parts, key_parts, shards, blocks, heads, factor, *refs):
+def back_kernel(row_parts, key_parts, shards, blocks, heads, factors, *refs):
     refs = list(refs)
     query_s = [refs.pop(0) for _ in range(row_parts)]
     key_s = [refs.pop(0) for _ in range(key_parts)]
@@ -215,8 +222,8 @@
         for index in range(per):
             tile = back[first + index]
             columns = slice(index * HD_S, (index + 1) * HD_S)
-            on_keys = dot(tile, row_side[first + index]) * factor
-            on_rows = dot(tile, key_side[first + index], ((0,), (0,))) * factor
+            on_keys = dot(tile, row_side[first + index]) * factors[1]
+            on_rows = dot(tile, key_side[first + index], ((0,), (0,))) * factors[0]
             own[:part, columns] = on_rows[:part]
             own[part:, columns] = on_keys[:size]
             for spot in range(1, row_parts):
@@ -225,33 +232,9 @@
                 others[row_parts + spot - 2][:size, columns] = on_keys[spot * size : (spot + 1) * size]
         for ref in others:
             if ref.shape[0] > part:
-                ref[part:, :] = jnp.zeros((RIDE_ROWS, ref.shape[1]), F32)
-                ref[part:, :LANES] = packed
-
-
-def tally_kernel(*refs):
-    *parts, total = refs
-    value = parts[0][...]
-    for ref in parts[1:]:
-        value = value + ref[ref.shape[0] - RIDE_ROWS :, :LANES]
-    total[...] = value
-
-
-def finish_kernel(row_parts, key_parts, *refs):
-    *pieces, grad_query, grad_key = refs
-    part = grad_query.shape[1]
-    count = row_parts + key_parts - 1
-    on_rows, on_keys = [], []
-    for i, ref in enumerate(pieces):
-        if i % count == 0:
-            on_rows.append(ref[:part])
-            on_keys.append(ref[part:])
-        elif i % count < row_parts:
-            on_rows.append(ref[:part])
-        else:
-            on_keys.append(ref[:part])
-    grad_query[0] = sum(on_rows[1:], on_rows[0])
-    grad_key[0] = sum(on_keys[1:], on_keys[0])
+                high, low = split(packed * factors[2])
+                ref[part:, :LANES] = high.astype(F32)
+                ref[part:, LANES:] = low.astype(F32)
 
 
 def close_kernel(mix_scale, loss_scale, total, grad_mix, head_loss):
@@ -326,7 +309,11 @@
 
     weight = shard_rows * length / HEADS_T
     width = HEADS_S * HD_S // shards
-    ride = RIDE_ROWS if width >= LANES else 0
+    ride = RIDE_ROWS if width == 2 * LANES else 0
+    factor = weight * HD_S ** (-0.5)
+    room_query = room(2.0 * heads * MIX_TOP * VALUE_TOP * factor)
+    room_key = room(rows * heads * MIX_TOP * VALUE_TOP * factor)
+    room_sums = room(2.0 * rows * HD_S * VALUE_TOP**2)
     count = row_parts + key_parts - 1
     shapes = []
     for shard in range(shards):
@@ -334,7 +321,13 @@
         shapes += [(2 * shard_rows, width)] + [(shard_rows + extra, width)] * (count - 1)
     sums, *pieces = pl.pallas_call(
         functools.partial(
-            back_kernel, row_parts, key_parts, shards, len(done), heads, weight * HD_S ** (-0.5)
+            back_kernel,
+            row_parts,
+            key_parts,
+            shards,
+            len(done),
+            heads,
+            (factor * room_query, factor * room_key, room_sums),
         ),
         out_shape=[jax.ShapeDtypeStruct(shape, F32) for shape in [(RIDE_ROWS, LANES)] + shapes],
         scratch_shapes=[
@@ -353,19 +346,22 @@
     )
 
     moves = [(along_rows, step) for step in range(row_parts)] + [(along_keys, step) for step in range(1, key_parts)]
-    arrived = [deliver(part, *moves[i % count], i // count) if i else part for i, part in enumerate(pieces)]
+    arrived = [
+        deliver(part.astype(F16), *moves[i % count], i // count) if i else part for i, part in enumerate(pieces)
+    ]
     small = functools.partial(pl.pallas_call, compiler_params=pltpu.CompilerParams(vmem_limit_bytes=VMEM_LIMIT // 4))
 
     def diagonal(across, along):
         return lambda position, _: along_keys(along_rows(position, across), along)
 
     if ride:
-        others = arrived[1:count]
+        rides = [part[shard_rows:].astype(F32) for part in arrived[1:count]]
+        others = [(part[:, :LANES] + part[:, LANES:]) * (1.0 / room_sums) for part in rides]
     else:
         others = [fetch(sums, target, step) for target, step in moves[1:]]
     for across in range(1, row_parts):
         others += [fetch(sums, diagonal(across, along), 0) for along in range(1, key_parts)]
-    total = small(tally_kernel, out_shape=jax.ShapeDtypeStruct((RIDE_ROWS, LANES), F32), name="tally")(sums, *others)
+    total = sum(others, sums)
     if copies & (copies - 1) == 0:
         for bit in range(copies.bit_length() - 1):
             total = total + lax.ppermute(total, "dp", [(i, i ^ (1 << bit)) for i in range(copies)])
@@ -374,10 +370,14 @@
         for step in range(1, copies):
             total = total + lax.ppermute(mine, "dp", [(i, (i + step) % copies) for i in range(copies)])
 
-    grad = jax.ShapeDtypeStruct((1, shard_rows, width), F32)
-    grad_query, grad_key = small(
-        functools.partial(finish_kernel, row_parts, key_parts), out_shape=(grad, grad), name="finish"
-    )(*arrived)
+    for_query = [part[:shard_rows].astype(F32) for i, part in enumerate(arrived) if i % count < row_parts]
+    for_key = [
+        part[-shard_rows:].astype(F32) if i % count == 0 else part[:shard_rows].astype(F32)
+        for i, part in enumerate(arrived)
+        if i % count == 0 or i % count >= row_parts
+    ]
+    grad_query = (sum(for_query[1:], for_query[0]) * (1.0 / room_query))[None]
+    grad_key = (sum(for_key[1:], for_key[0]) * (1.0 / room_key))[None]
     samples = copies * teacher_query.shape[0] * shard_rows * length
     grad_mix, head_loss = small(
         functools.partial(close_kernel, HD_S ** (-0.5) * weight / samples, 1.0 / samples),

time: 56.5 us -> 55.2 us (0.977)
  waiting for transfers between devices: 26.2 us -> 21.5 us
  starting transfers between devices: 14.2 us -> 17.3 us
  other arithmetic: 0.01 us -> 0.86 us
  Pallas kernels: 9.93 us -> 9.18 us
    ppermute x6, waiting for transfers between devices: 21.6 us -> 16.4 us  [fetch(): lax.ppermute(value, 'seq', [(target(i, step), i) for i in range(length)])]
    ppermute x5, starting transfers between devices: 4.66 us -> 7.43 us  [deliver(): return lax.ppermute(value, ('head', 'seq'), pairs)]
    broadcast_in_dim x0 -> x1, other arithmetic: none -> 0.78 us  [body(): grad_key = (sum(for_key[1:], for_key[0]) * (1.0 / room_key))[None]]
    pallas_call x2 -> x0, Pallas kernels: 0.75 us -> none  [the longest x1 0.75 us: body(): small(functools.partial(finish_kernel, row_parts, key_parts), out_shape=(...]
    ppermute x5, waiting for transfers between devices: 1.25 us -> 1.84 us  [deliver(): return lax.ppermute(value, ('head', 'seq'), pairs)]
  transfers between devices with their start and end apart: 13 -> 13, of which waited for: 8 -> 7; matrix products, arithmetic and copies ran while one was open for 1% -> 2% of each run, Pallas kernels for 9% -> 10%
where the time goes in v5:
time: 55.2 us; the launch traced here: 54.9 us
  waiting for transfers between devices  21.5 us (39%)
  starting transfers between devices  17.3 us (31%)
  Pallas kernels  9.18 us (17%)
  local copies, waits for them, and re-layouts  5.25 us (10%)
  other arithmetic  0.86 us (2%)
  between operations  0.72 us (1%)
    ppermute x6, waiting for transfers between devices, fetch(): lax.ppermute(value, 'seq', [(target(i, step), i) for i in range(length)])  16.4 us
    ppermute x6, starting transfers between devices, fetch(): lax.ppermute(value, 'seq', [(target(i, step), i) for i in range(length)])  8.36 us
    ppermute x5, starting transfers between devices, deliver(): return lax.ppermute(value, ('head', 'seq'), pairs)  7.43 us
    unnamed x11, local copies, waits for them, and re-layouts  5.25 us
    ppermute x2, waiting for transfers between devices, body(): lax.ppermute(total, 'dp', [(i, i ^ 1 << bit) for i in range(copies)])  3.33 us
    pallas_call x1, Pallas kernels, body(): pl.pallas_call(functools.partial(back_kernel, row_parts, key_parts, shard...  3.07 us
    pallas_call x2, Pallas kernels, teacher(): pl.pallas_call(functools.partial(teacher_kernel, row_parts, len(block_t),...  2.35 us
    pallas_call x1, Pallas kernels, body(): pl.pallas_call(functools.partial(student_kernel, row_parts, key_parts, he...  2.19 us
  transfers between devices with their start and end apart: 13, of which 7 were waited for; matrix products, arithmetic and copies ran while one was open for 2% of the time, Pallas kernels for 10%

profile of v5, /device:TPU:0, one launch (start us, length us, event | category | flops | bytes accessed | tf_op | source)
XLA Modules:
  0.0 54.9 jit_solution(17018731499090708523)
XLA Ops:
  0.6 3.1 %collective-permute-start = (bf16[1,128,512]{2,1,0:T(8,128)(2,1)}, bf16[1,128,512]{2,1,0:T(8,128)(2,1)S(1)}, u32[]{:S(2)}, u32[]{:S(2)}) collective-permute-start(bf16[1,128,512]{2,1,0:T(8,128)(2,1)} %refs_3_.1), channel_id=1, source_target_pairs={{4,0},{0,4},{12,8},{8,12},{5,1},{1,5},{13,9},{9,13},{6,2},{2,6},{1... | collective-permute-start | bytes 393224 | tf_op jit(solution)/shard_map/ppermute | solution.py:263
  3.7 2.6 %collective-permute-start.1 = (bf16[1,128,512]{2,1,0:T(8,128)(2,1)}, bf16[1,128,512]{2,1,0:T(8,128)(2,1)S(1)}, u32[]{:S(2)}, u32[]{:S(2)}) collective-permute-start(bf16[1,128,512]{2,1,0:T(8,128)(2,1)} %refs_2_.1), channel_id=1, source_target_pairs={{8,0},{12,4},{0,8},{4,12},{9,1},{13,5},{1,9},{5,13},{10,2},{14,6},... | collective-permute-start | bytes 393224 | tf_op jit(solution)/shard_map/ppermute | solution.py:263
  7.5 1.0 %copy-done = bf16[1,128,1536]{2,1,0:T(8,128)(2,1)S(1)} copy-done((bf16[1,128,1536]{2,1,0:T(8,128)(2,1)S(1)}, bf16[1,128,1536]{2,1,0:T(8,128)(2,1)}, u32[]{:S(2)}) %copy-start) | copy-done | bytes 393240
  8.5 1.0 %copy-done.1 = bf16[1,128,1536]{2,1,0:T(8,128)(2,1)S(1)} copy-done((bf16[1,128,1536]{2,1,0:T(8,128)(2,1)S(1)}, bf16[1,128,1536]{2,1,0:T(8,128)(2,1)}, u32[]{:S(2)}) %copy-start.1) | copy-done | bytes 393240
  9.5 0.9 %copy-done.2 = bf16[1,128,512]{2,1,0:T(8,128)(2,1)S(1)} copy-done((bf16[1,128,512]{2,1,0:T(8,128)(2,1)S(1)}, bf16[1,128,512]{2,1,0:T(8,128)(2,1)}, u32[]{:S(2)}) %copy-start.2) | copy-done | bytes 131096
  10.4 0.9 %copy-done.3 = bf16[1,128,512]{2,1,0:T(8,128)(2,1)S(1)} copy-done((bf16[1,128,512]{2,1,0:T(8,128)(2,1)S(1)}, bf16[1,128,512]{2,1,0:T(8,128)(2,1)}, u32[]{:S(2)}) %copy-start.3) | copy-done | bytes 131096
  12.0 1.0 %prepare.1 = (bf16[1,128,1536]{2,1,0:T(8,128)(2,1)S(1)}, bf16[1,128,1536]{2,1,0:T(8,128)(2,1)S(1)}, bf16[1,128,512]{2,1,0:T(8,128)(2,1)S(1)}, bf16[1,128,512]{2,...) custom-call(f32[12,8]{1,0:T(8,128)S(1)} %copy.9.mix_ref, ...), custom_call_target="tpu_custom_call" | custom-call | tf_op jit(solution)/shard_map/prepare/pallas_call | solution.py:78
  13.4 2.2 %student.1 = (f32[12,256,256]{2,1,0:T(8,128)S(1)}, f32[12,256,256]{2,1,0:T(8,128)S(1)}, bf16[8,256,256]{2,1,0:T(8,128)(2,1)S(1)}, bf16[8,256,256]{2,1,0:T(8,128)...) custom-call(bf16[1,128,512]{2,1,0:T(8,128)(2,1)S(1)} %get-tuple-element.37.refs_0_.refs_2_, ...), custom_call_target="tpu_custom_call" | custom-call | flops 6400000000 | bytes 1 | tf_op jit(solution)/shard_map/student/pallas_call | solution.py:285
  15.6 11.3 %collective-permute-done.3.refs_2_ = bf16[1,128,1536]{2,1,0:T(8,128)(2,1)S(1)} collective-permute-done((bf16[1,128,1536]{2,1,0:T(8,128)(2,1)}, bf16[1,128,1536]{2,1,0:T(8,128)(2,1)S(1)}, u32[]{:S(2)}, u32[]{:S(2)}) %collective-permute-start.3) | collective-permute-done | bytes 393248 | tf_op jit(solution)/shard_map/ppermute | solution.py:263
  26.9 1.5 %teacher.2 = (f32[12,128,256]{2,1,0:T(8,128)S(1)}, f32[12,256]{1,0:T(8,128)S(1)}, f32[12,256]{1,0:T(8,128)S(1)}, f32[2,12,256]{2,1,0:T(8,128)S(1)}, f32[2,12,256]{2,1,0:T(8,128)}) custom-call(bf16[1,128,1536]{2,1,0:T(8,128)(2,1)S(1)} %get-tuple-element.43.refs_0_, bf16[1,128,1536]{2,1,0:T(8,128)(2,1)S(1)} %get-tuple-element.38.refs_1_, ...), custom_call_target="tpu_custom_call" | custom-call | tf_op jit(solution)/shard_map/teacher/pallas_call | solution.py:295
  28.4 1.1 %collective-permute-done.2.refs_0_ = bf16[1,128,1536]{2,1,0:T(8,128)(2,1)S(1)} collective-permute-done((bf16[1,128,1536]{2,1,0:T(8,128)(2,1)}, bf16[1,128,1536]{2,1,0:T(8,128)(2,1)S(1)}, u32[]{:S(2)}, u32[]{:S(2)}) %collective-permute-start.2) | collective-permute-done | bytes 393248 | tf_op jit(solution)/shard_map/ppermute | solution.py:263
  29.5 0.9 %teacher.3 = (f32[12,128,256]{2,1,0:T(8,128)S(1)}, f32[12,256]{1,0:T(8,128)S(1)}, f32[12,256]{1,0:T(8,128)S(1)}, f32[2,12,256]{2,1,0:T(8,128)S(1)}, f32[2,12,256]{2,1,0:T(8,128)S(1)}) custom-call(bf16[1,128,1536]{2,1,0:T(8,128)(2,1)S(1)} %collective-permute-done.2.refs_0_, bf16[1,128,1536]{2,1,0:T(8,128)(2,1)S(1)} %get-tuple-element.38.refs_1_, ...), custom_call_target="tpu_custom_call" | custom-call | tf_op jit(solution)/shard_map/teacher/pallas_call | solution.py:295
  30.9 3.5 %collective-permute-done.4.refs_5_ = f32[2,12,256]{2,1,0:T(8,128)S(1)} collective-permute-done((f32[2,12,256]{2,1,0:T(8,128)S(1)}, f32[2,12,256]{2,1,0:T(8,128)S(1)}, u32[]{:S(2)}, u32[]{:S(2)}) %collective-permute-start.4) | collective-permute-done | bytes 24608 | tf_op jit(solution)/shard_map/ppermute | solution.py:263
  34.4 3.1 %back.1 = (f32[16,128]{1,0:T(8,128)S(1)}, f32[256,256]{1,0:T(8,128)S(1)}, f32[144,256]{1,0:T(8,128)S(1)}, f32[144,256]{1,0:T(8,128)S(1)}, f32[256,256]{1,0:T(8,1...) custom-call(bf16[1,128,512]{2,1,0:T(8,128)(2,1)S(1)} %get-tuple-element.36.refs_2_.refs_0_, ...), custom_call_target="tpu_custom_call" | custom-call | tf_op jit(solution)/shard_map/back/pallas_call | solution.py:322
  37.5 1.1 %collective-permute-start.8 = (f16[144,256]{1,0:T(8,128)(2,1)S(1)}, f16[144,256]{1,0:T(8,128)(2,1)S(1)}, u32[]{:S(2)}, u32[]{:S(2)}) collective-permute-start(f16[144,256]{1,0:T(8,128)(2,1)S(1)} %convert_element_type.45), channel_id=1, source_target_pairs={{0,8},{4,12},{8,0},{12,4},{16,24},{20,28},{24,16},{28,20},{1,9},{5... | collective-permute-start | bytes 221192 | tf_op jit(solution)/shard_map/ppermute | solution.py:271
  38.6 1.7 %collective-permute-start.10 = (f32[16,128]{1,0:T(8,128)S(1)}, f32[16,128]{1,0:T(8,128)S(1)}, u32[]{:S(2)}, u32[]{:S(2)}) collective-permute-start(f32[16,128]{1,0:T(8,128)S(1)} %get-tuple-element.65), channel_id=1, source_target_pairs={{12,0},{8,4},{4,8},{0,12},{13,1},{9,5},{5,9},{1,13},{14,2},{10,6},... | collective-permute-start | bytes 24584 | tf_op jit(solution)/shard_map/ppermute | solution.py:263
  40.4 2.8 %collective-permute-start.9 = (f16[128,256]{1,0:T(8,128)(2,1)S(1)}, f16[128,256]{1,0:T(8,128)(2,1)S(1)}, u32[]{:S(2)}, u32[]{:S(2)}) collective-permute-start(f16[128,256]{1,0:T(8,128)(2,1)S(1)} %convert_element_type.48), channel_id=1, source_target_pairs={{0,24},{4,28},{8,16},{12,20},{16,8},{20,12},{24,0},{28,4},{1,25},{... | collective-permute-start | bytes 196616 | tf_op jit(solution)/shard_map/ppermute | solution.py:271
  43.2 0.8 %collective-permute-start.7 = (f16[128,256]{1,0:T(8,128)(2,1)S(1)}, f16[128,256]{1,0:T(8,128)(2,1)S(1)}, u32[]{:S(2)}, u32[]{:S(2)}) collective-permute-start(f16[128,256]{1,0:T(8,128)(2,1)S(1)} %convert_element_type.43), channel_id=1, source_target_pairs={{0,20},{4,16},{8,28},{12,24},{16,4},{20,0},{24,12},{28,8},{1,21},{... | collective-permute-start | bytes 196616 | tf_op jit(solution)/shard_map/ppermute | solution.py:271
  44.0 1.1 %collective-permute-start.5 = (f16[144,256]{1,0:T(8,128)(2,1)S(1)}, f16[144,256]{1,0:T(8,128)(2,1)S(1)}, u32[]{:S(2)}, u32[]{:S(2)}) collective-permute-start(f16[144,256]{1,0:T(8,128)(2,1)S(1)} %convert_element_type.39), channel_id=1, source_target_pairs={{0,4},{4,0},{8,12},{12,8},{16,20},{20,16},{24,28},{28,24},{1,5},{5... | collective-permute-start | bytes 221192 | tf_op jit(solution)/shard_map/ppermute | solution.py:271
  45.1 1.6 %collective-permute-start.6 = (f16[256,256]{1,0:T(8,128)(2,1)S(1)}, f16[256,256]{1,0:T(8,128)(2,1)S(1)}, u32[]{:S(2)}, u32[]{:S(2)}) collective-permute-start(f16[256,256]{1,0:T(8,128)(2,1)S(1)} %convert_element_type.41), channel_id=1, source_target_pairs={{0,16},{4,20},{8,24},{12,28},{16,0},{20,4},{24,8},{28,12},{1,17},{... | collective-permute-start | bytes 393224 | tf_op jit(solution)/shard_map/ppermute | solution.py:271
  46.7 1.8 %collective-permute-done.5 = f16[144,256]{1,0:T(8,128)(2,1)S(1)} collective-permute-done((f16[144,256]{1,0:T(8,128)(2,1)S(1)}, f16[144,256]{1,0:T(8,128)(2,1)S(1)}, u32[]{:S(2)}, u32[]{:S(2)}) %collective-permute-start.5) | collective-permute-done | bytes 73760 | tf_op jit(solution)/shard_map/ppermute | solution.py:271
  48.7 1.2 %collective-permute-done.11 = f32[16,128]{1,0:T(8,128)S(1)} collective-permute-done((f32[16,128]{1,0:T(8,128)S(1)}, f32[16,128]{1,0:T(8,128)S(1)}, u32[]{:S(2)}, u32[]{:S(2)}) %collective-permute-start.11) | collective-permute-done | bytes 8224 | tf_op jit(solution)/shard_map/ppermute | solution.py:367
  49.8 1.5 %collective-permute-start.12 = (f32[16,128]{1,0:T(8,128)S(1)}, f32[16,128]{1,0:T(8,128)S(1)}, u32[]{:S(2)}, u32[]{:S(2)}) collective-permute-start(f32[16,128]{1,0:T(8,128)S(1)} %add.50), channel_id=1, source_target_pairs={{0,2},{1,3},{2,0},{3,1},{4,6},{5,7},{6,4},{7,5},{8,10},{9,11},{10,... | collective-permute-start | bytes 24584 | tf_op jit(solution)/shard_map/ppermute | solution.py:367
  51.3 2.2 %collective-permute-done.12 = f32[16,128]{1,0:T(8,128)S(1)} collective-permute-done((f32[16,128]{1,0:T(8,128)S(1)}, f32[16,128]{1,0:T(8,128)S(1)}, u32[]{:S(2)}, u32[]{:S(2)}) %collective-permute-start.12) | collective-permute-done | bytes 8224 | tf_op jit(solution)/shard_map/ppermute | solution.py:367
  (30 shorter events, 4.4 us)
Async XLA Ops:
  0.6 12.4 %collective-permute-start = (bf16[1,128,512]{2,1,0:T(8,128)(2,1)}, bf16[1,128,512]{2,1,0:T(8,128)(2,1)S(1)}, u32[]{:S(2)}, u32[]{:S(2)}) collective-permute-start(bf16[1,128,512]{2,1,0:T(8,128)(2,1)} %refs_3_.1), channel_id=1, source_target_pairs={{4,0},{0,4},{12,8},{8,12},{5,1},{1,5},{13,9},{9,13},{6,2},{2,6},{1... | collective-permute-start | bytes 393224 | tf_op jit(solution)/shard_map/ppermute | solution.py:263
  3.7 9.7 %collective-permute-start.1 = (bf16[1,128,512]{2,1,0:T(8,128)(2,1)}, bf16[1,128,512]{2,1,0:T(8,128)(2,1)S(1)}, u32[]{:S(2)}, u32[]{:S(2)}) collective-permute-start(bf16[1,128,512]{2,1,0:T(8,128)(2,1)} %refs_2_.1), channel_id=1, source_target_pairs={{8,0},{12,4},{0,8},{4,12},{9,1},{13,5},{1,9},{5,13},{10,2},{14,6},... | collective-permute-start | bytes 393224 | tf_op jit(solution)/shard_map/ppermute | solution.py:263
  6.3 20.6 %collective-permute-start.3 = (bf16[1,128,1536]{2,1,0:T(8,128)(2,1)}, bf16[1,128,1536]{2,1,0:T(8,128)(2,1)S(1)}, u32[]{:S(2)}, u32[]{:S(2)}) collective-permute-start(bf16[1,128,1536]{2,1,0:T(8,128)(2,1)} %refs_1_.1), channel_id=1, source_target_pairs={{4,0},{0,4},{12,8},{8,12},{5,1},{1,5},{13,9},{9,13},{6,2},{2,6},{1... | collective-permute-start | bytes 1179656 | tf_op jit(solution)/shard_map/ppermute | solution.py:263
  6.8 22.8 %collective-permute-start.2 = (bf16[1,128,1536]{2,1,0:T(8,128)(2,1)}, bf16[1,128,1536]{2,1,0:T(8,128)(2,1)S(1)}, u32[]{:S(2)}, u32[]{:S(2)}) collective-permute-start(bf16[1,128,1536]{2,1,0:T(8,128)(2,1)} %refs_0_.1), channel_id=1, source_target_pairs={{8,0},{12,4},{0,8},{4,12},{9,1},{13,5},{1,9},{5,13},{10,2},{14,6},... | collective-permute-start | bytes 1179656 | tf_op jit(solution)/shard_map/ppermute | solution.py:263
  7.5 1.0 %copy-start = (bf16[1,128,1536]{2,1,0:T(8,128)(2,1)S(1)}, bf16[1,128,1536]{2,1,0:T(8,128)(2,1)}, u32[]{:S(2)}) copy-start(bf16[1,128,1536]{2,1,0:T(8,128)(2,1)} %refs_1_.1) | copy-start | bytes 1179652
  8.5 1.0 %copy-start.1 = (bf16[1,128,1536]{2,1,0:T(8,128)(2,1)S(1)}, bf16[1,128,1536]{2,1,0:T(8,128)(2,1)}, u32[]{:S(2)}) copy-start(bf16[1,128,1536]{2,1,0:T(8,128)(2,1)} %refs_0_.1) | copy-start | bytes 1179652
  9.5 0.9 %copy-start.2 = (bf16[1,128,512]{2,1,0:T(8,128)(2,1)S(1)}, bf16[1,128,512]{2,1,0:T(8,128)(2,1)}, u32[]{:S(2)}) copy-start(bf16[1,128,512]{2,1,0:T(8,128)(2,1)} %refs_3_.1) | copy-start | bytes 393220
  10.4 0.9 %copy-start.3 = (bf16[1,128,512]{2,1,0:T(8,128)(2,1)S(1)}, bf16[1,128,512]{2,1,0:T(8,128)(2,1)}, u32[]{:S(2)}) copy-start(bf16[1,128,512]{2,1,0:T(8,128)(2,1)} %refs_2_.1) | copy-start | bytes 393220
  11.3 0.7 %copy-start.4 = (f32[12,8]{0,1:T(8,128)S(1)}, f32[12,8]{0,1:T(8,128)}, u32[]{:S(2)}) copy-start(f32[12,8]{0,1:T(8,128)} %param.9) | copy-start | bytes 1156
  30.4 4.0 %collective-permute-start.4 = (f32[2,12,256]{2,1,0:T(8,128)S(1)}, f32[2,12,256]{2,1,0:T(8,128)S(1)}, u32[]{:S(2)}, u32[]{:S(2)}) collective-permute-start(f32[2,12,256]{2,1,0:T(8,128)S(1)} %get-tuple-element.46), channel_id=1, source_target_pairs={{4,0},{0,4},{12,8},{8,12},{5,1},{1,5},{13,9},{9,13},{6,2},{2,6},{1... | collective-permute-start | bytes 73736 | tf_op jit(solution)/shard_map/ppermute | solution.py:263
  37.5 7.6 %collective-permute-start.8 = (f16[144,256]{1,0:T(8,128)(2,1)S(1)}, f16[144,256]{1,0:T(8,128)(2,1)S(1)}, u32[]{:S(2)}, u32[]{:S(2)}) collective-permute-start(f16[144,256]{1,0:T(8,128)(2,1)S(1)} %convert_element_type.45), channel_id=1, source_target_pairs={{0,8},{4,12},{8,0},{12,4},{16,24},{20,28},{24,16},{28,20},{1,9},{5... | collective-permute-start | bytes 221192 | tf_op jit(solution)/shard_map/ppermute | solution.py:271
  38.6 10.0 %collective-permute-start.10 = (f32[16,128]{1,0:T(8,128)S(1)}, f32[16,128]{1,0:T(8,128)S(1)}, u32[]{:S(2)}, u32[]{:S(2)}) collective-permute-start(f32[16,128]{1,0:T(8,128)S(1)} %get-tuple-element.65), channel_id=1, source_target_pairs={{12,0},{8,4},{4,8},{0,12},{13,1},{9,5},{5,9},{1,13},{14,2},{10,6},... | collective-permute-start | bytes 24584 | tf_op jit(solution)/shard_map/ppermute | solution.py:263
  40.4 13.7 %collective-permute-start.9 = (f16[128,256]{1,0:T(8,128)(2,1)S(1)}, f16[128,256]{1,0:T(8,128)(2,1)S(1)}, u32[]{:S(2)}, u32[]{:S(2)}) collective-permute-start(f16[128,256]{1,0:T(8,128)(2,1)S(1)} %convert_element_type.48), channel_id=1, source_target_pairs={{0,24},{4,28},{8,16},{12,20},{16,8},{20,12},{24,0},{28,4},{1,25},{... | collective-permute-start | bytes 196616 | tf_op jit(solution)/shard_map/ppermute | solution.py:271
  43.2 10.9 %collective-permute-start.7 = (f16[128,256]{1,0:T(8,128)(2,1)S(1)}, f16[128,256]{1,0:T(8,128)(2,1)S(1)}, u32[]{:S(2)}, u32[]{:S(2)}) collective-permute-start(f16[128,256]{1,0:T(8,128)(2,1)S(1)} %convert_element_type.43), channel_id=1, source_target_pairs={{0,20},{4,16},{8,28},{12,24},{16,4},{20,0},{24,12},{28,8},{1,21},{... | collective-permute-start | bytes 196616 | tf_op jit(solution)/shard_map/ppermute | solution.py:271
  44.0 4.6 %collective-permute-start.5 = (f16[144,256]{1,0:T(8,128)(2,1)S(1)}, f16[144,256]{1,0:T(8,128)(2,1)S(1)}, u32[]{:S(2)}, u32[]{:S(2)}) collective-permute-start(f16[144,256]{1,0:T(8,128)(2,1)S(1)} %convert_element_type.39), channel_id=1, source_target_pairs={{0,4},{4,0},{8,12},{12,8},{16,20},{20,16},{24,28},{28,24},{1,5},{5... | collective-permute-start | bytes 221192 | tf_op jit(solution)/shard_map/ppermute | solution.py:271
  45.1 9.0 %collective-permute-start.6 = (f16[256,256]{1,0:T(8,128)(2,1)S(1)}, f16[256,256]{1,0:T(8,128)(2,1)S(1)}, u32[]{:S(2)}, u32[]{:S(2)}) collective-permute-start(f16[256,256]{1,0:T(8,128)(2,1)S(1)} %convert_element_type.41), channel_id=1, source_target_pairs={{0,16},{4,20},{8,24},{12,28},{16,0},{20,4},{24,8},{28,12},{1,17},{... | collective-permute-start | bytes 393224 | tf_op jit(solution)/shard_map/ppermute | solution.py:271
  48.6 1.2 %collective-permute-start.11 = (f32[16,128]{1,0:T(8,128)S(1)}, f32[16,128]{1,0:T(8,128)S(1)}, u32[]{:S(2)}, u32[]{:S(2)}) collective-permute-start(f32[16,128]{1,0:T(8,128)S(1)} %fusion.2), channel_id=1, source_target_pairs={{0,1},{1,0},{2,3},{3,2},{4,5},{5,4},{6,7},{7,6},{8,9},{9,8},{10,11... | collective-permute-start | bytes 24584 | tf_op jit(solution)/shard_map/ppermute | solution.py:367
  49.8 3.7 %collective-permute-start.12 = (f32[16,128]{1,0:T(8,128)S(1)}, f32[16,128]{1,0:T(8,128)S(1)}, u32[]{:S(2)}, u32[]{:S(2)}) collective-permute-start(f32[16,128]{1,0:T(8,128)S(1)} %add.50), channel_id=1, source_target_pairs={{0,2},{1,3},{2,0},{3,1},{4,6},{5,7},{6,4},{7,5},{8,10},{9,11},{10,... | collective-permute-start | bytes 24584 | tf_op jit(solution)/shard_map/ppermute | solution.py:367

commit v6 on v5

--- a/solution.py
+++ b/solution.py
@@ -44,7 +44,7 @@
 
 def prepare_kernel(count, mix_ref, mix_tr_ref, *refs):
     sources, targets = refs[:count], refs[count : 2 * count]
-    lift_hi, lift_lo, back_hi, back_lo, semaphores = refs[2 * count :]
+    lift_hi, lift_lo, back_both, semaphores = refs[2 * count :]
     moves = [pltpu.make_async_copy(sources[i], targets[i], semaphores.at[i]) for i in range(count)]
     for move in moves:
         move.start()
@@ -64,7 +64,9 @@
 
     scaled = mix_ref[...] * (HD_S ** (-0.5) * LOG2E)
     lift_hi[...], lift_lo[...] = split(kron(scaled, LIFT_BLOCK))
-    back_hi[...], back_lo[...] = split(kron(mix_tr_ref[...], BACK_BLOCK))
+    high, low = split(kron(mix_tr_ref[...], BACK_BLOCK))
+    back_both[: high.shape[0]] = high
+    back_both[high.shape[0] :] = low
     for move in moves:
         move.wait()
 
@@ -72,12 +74,12 @@
 def prepare(head_mix, arrays):
     heads = head_mix.shape[0]
     lift = pltpu.VMEM((heads * LIFT_BLOCK, HEADS_S * LIFT_BLOCK), BF16)
-    back = pltpu.VMEM((HEADS_S * BACK_BLOCK, heads * BACK_BLOCK), BF16)
+    back = pltpu.VMEM((2 * HEADS_S * BACK_BLOCK, heads * BACK_BLOCK), BF16)
     count = len(arrays)
     whole = pl.BlockSpec(memory_space=pltpu.VMEM)
     return pl.pallas_call(
         functools.partial(prepare_kernel, count),
-        out_shape=[pltpu.VMEM(array.shape, array.dtype) for array in arrays] + [lift, lift, back, back],
+        out_shape=[pltpu.VMEM(array.shape, array.dtype) for array in arrays] + [lift, lift, back],
         in_specs=[whole, whole] + [pl.BlockSpec(memory_space=pl.ANY)] * count,
         scratch_shapes=[pltpu.SemaphoreType.DMA((count,))],
         compiler_params=pltpu.CompilerParams(vmem_limit_bytes=VMEM_LIMIT // 2),
@@ -149,9 +151,9 @@
     query_s = [refs.pop(0) for _ in range(row_parts)]
     key_s = [refs.pop(0) for _ in range(key_parts)]
     lse = [refs.pop(0) for _ in range(row_parts)]
-    back_hi, back_lo, exp_l, stu_hi, stu_lo, top_l = refs[:6]
-    maps = [refs[6 + 3 * i : 9 + 3 * i] for i in range(blocks)]
-    *outs, scale_t, scale_l, back, row_side, key_side, mix_acc = refs[6 + 3 * blocks :]
+    back_both, exp_l, stu_hi, stu_lo, top_l = refs[:5]
+    maps = [refs[5 + 3 * i : 8 + 3 * i] for i in range(blocks)]
+    *outs, scale_t, scale_l, back, row_side, key_side, mix_acc = refs[5 + 3 * blocks :]
     keys, rows = back.shape[1:]
     part, size = rows // row_parts, keys // key_parts
     sums, pieces = outs[0], outs[1:]
@@ -188,7 +190,9 @@
             for inner in range(0, LIFT_BLOCK, BACK_BLOCK):
                 b_high = high[:, inner : inner + BACK_BLOCK, :].reshape(heads * BACK_BLOCK, rows)
                 b_low = low[:, inner : inner + BACK_BLOCK, :].reshape(heads * BACK_BLOCK, rows)
-                total = dot(back_hi[...], b_high) + (dot(back_hi[...], b_low) + dot(back_lo[...], b_high))
+                half = HEADS_S * BACK_BLOCK
+                twice = dot(back_both[...], b_high)
+                total = twice[:half] + (dot(back_both[:half], b_low) + twice[half:])
                 first = offset + start + inner
                 back[:, first : first + BACK_BLOCK, :] = total.astype(BF16).reshape(HEADS_S, BACK_BLOCK, rows)
         offset += exp_t.shape[1]
@@ -275,7 +279,7 @@
     query_t = [fetch(teacher_query, along_rows, d) for d in range(1, row_parts)]
     key_s = [fetch(student_key, along_keys, d) for d in range(1, key_parts)]
     query_s = [fetch(student_query, along_rows, d) for d in range(1, row_parts)]
-    *own, lift_hi, lift_lo, back_hi, back_lo = prepare(head_mix, own)
+    *own, lift_hi, lift_lo, back_both = prepare(head_mix, own)
     key_t, query_t, key_s, query_s = [[mine, *rest] for mine, rest in zip(own, (key_t, query_t, key_s, query_s))]
 
     exponents = pltpu.VMEM((heads, keys, rows), F32)
@@ -341,7 +345,7 @@
         compiler_params=pltpu.CompilerParams(vmem_limit_bytes=VMEM_LIMIT),
         name="back",
     )(
-        *query_s, *key_s, *lse_parts, back_hi, back_lo, exp_l, stu_hi, stu_lo, top_l,
+        *query_s, *key_s, *lse_parts, back_both, exp_l, stu_hi, stu_lo, top_l,
         *[ref for block in done for ref in block],
     )
 
@@ -362,14 +366,6 @@
     for across in range(1, row_parts):
         others += [fetch(sums, diagonal(across, along), 0) for along in range(1, key_parts)]
     total = sum(others, sums)
-    if copies & (copies - 1) == 0:
-        for bit in range(copies.bit_length() - 1):
-            total = total + lax.ppermute(total, "dp", [(i, i ^ (1 << bit)) for i in range(copies)])
-    else:
-        mine = total
-        for step in range(1, copies):
-            total = total + lax.ppermute(mine, "dp", [(i, (i + step) % copies) for i in range(copies)])
-
     for_query = [part[:shard_rows].astype(F32) for i, part in enumerate(arrived) if i % count < row_parts]
     for_key = [
         part[-shard_rows:].astype(F32) if i % count == 0 else part[:shard_rows].astype(F32)
@@ -378,6 +374,18 @@
     ]
     grad_query = (sum(for_query[1:], for_query[0]) * (1.0 / room_query))[None]
     grad_key = (sum(for_key[1:], for_key[0]) * (1.0 / room_key))[None]
+    last = total
+    if copies > 1 and copies & (copies - 1) == 0:
+        for bit in range(copies.bit_length() - 1):
+            total = total if bit == 0 else total + last
+            last = lax.ppermute(total, "dp", [(i, i ^ (1 << bit)) for i in range(copies)])
+    else:
+        last = sum(
+            [lax.ppermute(total, "dp", [(i, (i + step) % copies) for i in range(copies)]) for step in range(1, copies)],
+            jnp.zeros_like(total),
+        )
+    last, grad_query, grad_key = lax.optimization_barrier((last, grad_query, grad_key))
+    total = total + last
     samples = copies * teacher_query.shape[0] * shard_rows * length
     grad_mix, head_loss = small(
         functools.partial(close_kernel, HD_S ** (-0.5) * weight / samples, 1.0 / samples),

time: 55.2 us -> 54.4 us (0.986)
  waiting for transfers between devices: 21.5 us -> 20.7 us
    ppermute x2, waiting for transfers between devices: 3.33 us -> 2.53 us  [body(): last = lax.ppermute(total, 'dp', [(i, i ^ 1 << bit) for i in range(copies)])]
  transfers between devices with their start and end apart: 13 -> 13, of which waited for: 7 -> 7; matrix products, arithmetic and copies ran while one was open for 2% -> 3% of each run, Pallas kernels for 10% -> 9%
where the time goes in v6:
time: 54.4 us; the launch traced here: 54.1 us
  waiting for transfers between devices  20.7 us (38%)
  starting transfers between devices  17.4 us (32%)
  Pallas kernels  9.16 us (17%)
  local copies, waits for them, and re-layouts  5.25 us (10%)
  other arithmetic  0.86 us (2%)
  between operations  0.71 us (1%)
    ppermute x6, waiting for transfers between devices, fetch(): lax.ppermute(value, 'seq', [(target(i, step), i) for i in range(length)])  16.4 us
    ppermute x6, starting transfers between devices, fetch(): lax.ppermute(value, 'seq', [(target(i, step), i) for i in range(length)])  8.42 us
    ppermute x5, starting transfers between devices, deliver(): return lax.ppermute(value, ('head', 'seq'), pairs)  7.43 us
    unnamed x11, local copies, waits for them, and re-layouts  5.25 us
    pallas_call x1, Pallas kernels, body(): pl.pallas_call(functools.partial(back_kernel, row_parts, key_parts, shard...  3.05 us
    ppermute x2, waiting for transfers between devices, body(): last = lax.ppermute(total, 'dp', [(i, i ^ 1 << bit) for i in range(copies)])  2.53 us
    pallas_call x2, Pallas kernels, teacher(): pl.pallas_call(functools.partial(teacher_kernel, row_parts, len(block_t),...  2.35 us
    pallas_call x1, Pallas kernels, body(): pl.pallas_call(functools.partial(student_kernel, row_parts, key_parts, he...  2.19 us
  transfers between devices with their start and end apart: 13, of which 7 were waited for; matrix products, arithmetic and copies ran while one was open for 3% of the time, Pallas kernels for 9%

profile of v6, /device:TPU:0, one launch (start us, length us, event | category | flops | bytes accessed | tf_op | source)
XLA Modules:
  0.0 54.1 jit_solution(1617220522203015817)
XLA Ops:
  0.6 3.1 %collective-permute-start = (bf16[1,128,512]{2,1,0:T(8,128)(2,1)}, bf16[1,128,512]{2,1,0:T(8,128)(2,1)S(1)}, u32[]{:S(2)}, u32[]{:S(2)}) collective-permute-start(bf16[1,128,512]{2,1,0:T(8,128)(2,1)} %refs_3_.1), channel_id=1, source_target_pairs={{4,0},{0,4},{12,8},{8,12},{5,1},{1,5},{13,9},{9,13},{6,2},{2,6},{1... | collective-permute-start | bytes 393224 | tf_op jit(solution)/shard_map/ppermute | solution.py:267
  3.7 2.6 %collective-permute-start.1 = (bf16[1,128,512]{2,1,0:T(8,128)(2,1)}, bf16[1,128,512]{2,1,0:T(8,128)(2,1)S(1)}, u32[]{:S(2)}, u32[]{:S(2)}) collective-permute-start(bf16[1,128,512]{2,1,0:T(8,128)(2,1)} %refs_2_.1), channel_id=1, source_target_pairs={{8,0},{12,4},{0,8},{4,12},{9,1},{13,5},{1,9},{5,13},{10,2},{14,6},... | collective-permute-start | bytes 393224 | tf_op jit(solution)/shard_map/ppermute | solution.py:267
  7.5 1.0 %copy-done = bf16[1,128,1536]{2,1,0:T(8,128)(2,1)S(1)} copy-done((bf16[1,128,1536]{2,1,0:T(8,128)(2,1)S(1)}, bf16[1,128,1536]{2,1,0:T(8,128)(2,1)}, u32[]{:S(2)}) %copy-start) | copy-done | bytes 393240
  8.5 1.0 %copy-done.1 = bf16[1,128,1536]{2,1,0:T(8,128)(2,1)S(1)} copy-done((bf16[1,128,1536]{2,1,0:T(8,128)(2,1)S(1)}, bf16[1,128,1536]{2,1,0:T(8,128)(2,1)}, u32[]{:S(2)}) %copy-start.1) | copy-done | bytes 393240
  9.5 0.9 %copy-done.2 = bf16[1,128,512]{2,1,0:T(8,128)(2,1)S(1)} copy-done((bf16[1,128,512]{2,1,0:T(8,128)(2,1)S(1)}, bf16[1,128,512]{2,1,0:T(8,128)(2,1)}, u32[]{:S(2)}) %copy-start.2) | copy-done | bytes 131096
  10.4 0.9 %copy-done.3 = bf16[1,128,512]{2,1,0:T(8,128)(2,1)S(1)} copy-done((bf16[1,128,512]{2,1,0:T(8,128)(2,1)S(1)}, bf16[1,128,512]{2,1,0:T(8,128)(2,1)}, u32[]{:S(2)}) %copy-start.3) | copy-done | bytes 131096
  12.0 1.0 %prepare.1 = (bf16[1,128,1536]{2,1,0:T(8,128)(2,1)S(1)}, bf16[1,128,1536]{2,1,0:T(8,128)(2,1)S(1)}, bf16[1,128,512]{2,1,0:T(8,128)(2,1)S(1)}, bf16[1,128,512]{2,...) custom-call(f32[12,8]{1,0:T(8,128)S(1)} %copy.9.mix_ref, ...), custom_call_target="tpu_custom_call" | custom-call | tf_op jit(solution)/shard_map/prepare/pallas_call | solution.py:80
  13.4 2.2 %student.1 = (f32[12,256,256]{2,1,0:T(8,128)S(1)}, f32[12,256,256]{2,1,0:T(8,128)S(1)}, bf16[8,256,256]{2,1,0:T(8,128)(2,1)S(1)}, bf16[8,256,256]{2,1,0:T(8,128)...) custom-call(bf16[1,128,512]{2,1,0:T(8,128)(2,1)S(1)} %get-tuple-element.39.refs_0_.refs_2_, ...), custom_call_target="tpu_custom_call" | custom-call | flops 6400000000 | bytes 1 | tf_op jit(solution)/shard_map/student/pallas_call | solution.py:289
  15.6 11.3 %collective-permute-done.3.refs_2_ = bf16[1,128,1536]{2,1,0:T(8,128)(2,1)S(1)} collective-permute-done((bf16[1,128,1536]{2,1,0:T(8,128)(2,1)}, bf16[1,128,1536]{2,1,0:T(8,128)(2,1)S(1)}, u32[]{:S(2)}, u32[]{:S(2)}) %collective-permute-start.3) | collective-permute-done | bytes 393248 | tf_op jit(solution)/shard_map/ppermute | solution.py:267
  26.9 1.5 %teacher.2 = (f32[12,128,256]{2,1,0:T(8,128)S(1)}, f32[12,256]{1,0:T(8,128)S(1)}, f32[12,256]{1,0:T(8,128)S(1)}, f32[2,12,256]{2,1,0:T(8,128)S(1)}, f32[2,12,256]{2,1,0:T(8,128)}) custom-call(bf16[1,128,1536]{2,1,0:T(8,128)(2,1)S(1)} %get-tuple-element.45.refs_0_, bf16[1,128,1536]{2,1,0:T(8,128)(2,1)S(1)} %get-tuple-element.40.refs_1_, ...), custom_call_target="tpu_custom_call" | custom-call | tf_op jit(solution)/shard_map/teacher/pallas_call | solution.py:299
  28.4 1.1 %collective-permute-done.2.refs_0_ = bf16[1,128,1536]{2,1,0:T(8,128)(2,1)S(1)} collective-permute-done((bf16[1,128,1536]{2,1,0:T(8,128)(2,1)}, bf16[1,128,1536]{2,1,0:T(8,128)(2,1)S(1)}, u32[]{:S(2)}, u32[]{:S(2)}) %collective-permute-start.2) | collective-permute-done | bytes 393248 | tf_op jit(solution)/shard_map/ppermute | solution.py:267
  29.5 0.9 %teacher.3 = (f32[12,128,256]{2,1,0:T(8,128)S(1)}, f32[12,256]{1,0:T(8,128)S(1)}, f32[12,256]{1,0:T(8,128)S(1)}, f32[2,12,256]{2,1,0:T(8,128)S(1)}, f32[2,12,256]{2,1,0:T(8,128)S(1)}) custom-call(bf16[1,128,1536]{2,1,0:T(8,128)(2,1)S(1)} %collective-permute-done.2.refs_0_, bf16[1,128,1536]{2,1,0:T(8,128)(2,1)S(1)} %get-tuple-element.40.refs_1_, ...), custom_call_target="tpu_custom_call" | custom-call | tf_op jit(solution)/shard_map/teacher/pallas_call | solution.py:299
  30.9 3.5 %collective-permute-done.4.refs_5_ = f32[2,12,256]{2,1,0:T(8,128)S(1)} collective-permute-done((f32[2,12,256]{2,1,0:T(8,128)S(1)}, f32[2,12,256]{2,1,0:T(8,128)S(1)}, u32[]{:S(2)}, u32[]{:S(2)}) %collective-permute-start.4) | collective-permute-done | bytes 24608 | tf_op jit(solution)/shard_map/ppermute | solution.py:267
  34.4 3.1 %back.1 = (f32[16,128]{1,0:T(8,128)S(1)}, f32[256,256]{1,0:T(8,128)S(1)}, f32[144,256]{1,0:T(8,128)S(1)}, f32[144,256]{1,0:T(8,128)S(1)}, f32[256,256]{1,0:T(8,1...) custom-call(bf16[1,128,512]{2,1,0:T(8,128)(2,1)S(1)} %get-tuple-element.38.refs_2_.refs_0_, ...), custom_call_target="tpu_custom_call" | custom-call | tf_op jit(solution)/shard_map/back/pallas_call | solution.py:326
  37.5 1.1 %collective-permute-start.6 = (f16[144,256]{1,0:T(8,128)(2,1)S(1)}, f16[144,256]{1,0:T(8,128)(2,1)S(1)}, u32[]{:S(2)}, u32[]{:S(2)}) collective-permute-start(f16[144,256]{1,0:T(8,128)(2,1)S(1)} %convert_element_type.41), channel_id=1, source_target_pairs={{0,8},{4,12},{8,0},{12,4},{16,24},{20,28},{24,16},{28,20},{1,9},{5... | collective-permute-start | bytes 221192 | tf_op jit(solution)/shard_map/ppermute | solution.py:275
  38.6 1.8 %collective-permute-start.7 = (f32[16,128]{1,0:T(8,128)S(1)}, f32[16,128]{1,0:T(8,128)S(1)}, u32[]{:S(2)}, u32[]{:S(2)}) collective-permute-start(f32[16,128]{1,0:T(8,128)S(1)} %get-tuple-element.60), channel_id=1, source_target_pairs={{12,0},{8,4},{4,8},{0,12},{13,1},{9,5},{5,9},{1,13},{14,2},{10,6},... | collective-permute-start | bytes 24584 | tf_op jit(solution)/shard_map/ppermute | solution.py:267
  40.4 2.8 %collective-permute-start.12 = (f16[128,256]{1,0:T(8,128)(2,1)S(1)}, f16[128,256]{1,0:T(8,128)(2,1)S(1)}, u32[]{:S(2)}, u32[]{:S(2)}) collective-permute-start(f16[128,256]{1,0:T(8,128)(2,1)S(1)} %convert_element_type.50), channel_id=1, source_target_pairs={{0,24},{4,28},{8,16},{12,20},{16,8},{20,12},{24,0},{28,4},{1,25},{... | collective-permute-start | bytes 196616 | tf_op jit(solution)/shard_map/ppermute | solution.py:275
  43.2 0.8 %collective-permute-start.11 = (f16[128,256]{1,0:T(8,128)(2,1)S(1)}, f16[128,256]{1,0:T(8,128)(2,1)S(1)}, u32[]{:S(2)}, u32[]{:S(2)}) collective-permute-start(f16[128,256]{1,0:T(8,128)(2,1)S(1)} %convert_element_type.46), channel_id=1, source_target_pairs={{0,20},{4,16},{8,28},{12,24},{16,4},{20,0},{24,12},{28,8},{1,21},{... | collective-permute-start | bytes 196616 | tf_op jit(solution)/shard_map/ppermute | solution.py:275
  44.0 1.1 %collective-permute-start.5 = (f16[144,256]{1,0:T(8,128)(2,1)S(1)}, f16[144,256]{1,0:T(8,128)(2,1)S(1)}, u32[]{:S(2)}, u32[]{:S(2)}) collective-permute-start(f16[144,256]{1,0:T(8,128)(2,1)S(1)} %convert_element_type.39), channel_id=1, source_target_pairs={{0,4},{4,0},{8,12},{12,8},{16,20},{20,16},{24,28},{28,24},{1,5},{5... | collective-permute-start | bytes 221192 | tf_op jit(solution)/shard_map/ppermute | solution.py:275
  45.2 1.6 %collective-permute-start.10 = (f16[256,256]{1,0:T(8,128)(2,1)S(1)}, f16[256,256]{1,0:T(8,128)(2,1)S(1)}, u32[]{:S(2)}, u32[]{:S(2)}) collective-permute-start(f16[256,256]{1,0:T(8,128)(2,1)S(1)} %convert_element_type.44), channel_id=1, source_target_pairs={{0,16},{4,20},{8,24},{12,28},{16,0},{20,4},{24,8},{28,12},{1,17},{... | collective-permute-start | bytes 393224 | tf_op jit(solution)/shard_map/ppermute | solution.py:275
  46.8 1.8 %collective-permute-done.5 = f16[144,256]{1,0:T(8,128)(2,1)S(1)} collective-permute-done((f16[144,256]{1,0:T(8,128)(2,1)S(1)}, f16[144,256]{1,0:T(8,128)(2,1)S(1)}, u32[]{:S(2)}, u32[]{:S(2)}) %collective-permute-start.5) | collective-permute-done | bytes 73760 | tf_op jit(solution)/shard_map/ppermute | solution.py:275
  48.7 1.2 %collective-permute-done.8 = f32[16,128]{1,0:T(8,128)S(1)} collective-permute-done((f32[16,128]{1,0:T(8,128)S(1)}, f32[16,128]{1,0:T(8,128)S(1)}, u32[]{:S(2)}, u32[]{:S(2)}) %collective-permute-start.8) | collective-permute-done | bytes 8224 | tf_op jit(solution)/shard_map/ppermute | solution.py:381
  49.9 1.5 %collective-permute-start.9 = (f32[16,128]{1,0:T(8,128)S(1)}, f32[16,128]{1,0:T(8,128)S(1)}, u32[]{:S(2)}, u32[]{:S(2)}) collective-permute-start(f32[16,128]{1,0:T(8,128)S(1)} %add.44), channel_id=1, source_target_pairs={{0,2},{1,3},{2,0},{3,1},{4,6},{5,7},{6,4},{7,5},{8,10},{9,11},{10,... | collective-permute-start | bytes 24584 | tf_op jit(solution)/shard_map/ppermute | solution.py:381
  52.2 1.4 %collective-permute-done.9 = f32[16,128]{1,0:T(8,128)S(1)} collective-permute-done((f32[16,128]{1,0:T(8,128)S(1)}, f32[16,128]{1,0:T(8,128)S(1)}, u32[]{:S(2)}, u32[]{:S(2)}) %collective-permute-start.9) | collective-permute-done | bytes 8224 | tf_op jit(solution)/shard_map/ppermute | solution.py:381
  (30 shorter events, 4.4 us)
Async XLA Ops:
  0.6 12.4 %collective-permute-start = (bf16[1,128,512]{2,1,0:T(8,128)(2,1)}, bf16[1,128,512]{2,1,0:T(8,128)(2,1)S(1)}, u32[]{:S(2)}, u32[]{:S(2)}) collective-permute-start(bf16[1,128,512]{2,1,0:T(8,128)(2,1)} %refs_3_.1), channel_id=1, source_target_pairs={{4,0},{0,4},{12,8},{8,12},{5,1},{1,5},{13,9},{9,13},{6,2},{2,6},{1... | collective-permute-start | bytes 393224 | tf_op jit(solution)/shard_map/ppermute | solution.py:267
  3.7 9.7 %collective-permute-start.1 = (bf16[1,128,512]{2,1,0:T(8,128)(2,1)}, bf16[1,128,512]{2,1,0:T(8,128)(2,1)S(1)}, u32[]{:S(2)}, u32[]{:S(2)}) collective-permute-start(bf16[1,128,512]{2,1,0:T(8,128)(2,1)} %refs_2_.1), channel_id=1, source_target_pairs={{8,0},{12,4},{0,8},{4,12},{9,1},{13,5},{1,9},{5,13},{10,2},{14,6},... | collective-permute-start | bytes 393224 | tf_op jit(solution)/shard_map/ppermute | solution.py:267
  6.3 20.6 %collective-permute-start.3 = (bf16[1,128,1536]{2,1,0:T(8,128)(2,1)}, bf16[1,128,1536]{2,1,0:T(8,128)(2,1)S(1)}, u32[]{:S(2)}, u32[]{:S(2)}) collective-permute-start(bf16[1,128,1536]{2,1,0:T(8,128)(2,1)} %refs_1_.1), channel_id=1, source_target_pairs={{4,0},{0,4},{12,8},{8,12},{5,1},{1,5},{13,9},{9,13},{6,2},{2,6},{1... | collective-permute-start | bytes 1179656 | tf_op jit(solution)/shard_map/ppermute | solution.py:267
  6.8 22.8 %collective-permute-start.2 = (bf16[1,128,1536]{2,1,0:T(8,128)(2,1)}, bf16[1,128,1536]{2,1,0:T(8,128)(2,1)S(1)}, u32[]{:S(2)}, u32[]{:S(2)}) collective-permute-start(bf16[1,128,1536]{2,1,0:T(8,128)(2,1)} %refs_0_.1), channel_id=1, source_target_pairs={{8,0},{12,4},{0,8},{4,12},{9,1},{13,5},{1,9},{5,13},{10,2},{14,6},... | collective-permute-start | bytes 1179656 | tf_op jit(solution)/shard_map/ppermute | solution.py:267
  7.5 1.0 %copy-start = (bf16[1,128,1536]{2,1,0:T(8,128)(2,1)S(1)}, bf16[1,128,1536]{2,1,0:T(8,128)(2,1)}, u32[]{:S(2)}) copy-start(bf16[1,128,1536]{2,1,0:T(8,128)(2,1)} %refs_1_.1) | copy-start | bytes 1179652
  8.5 1.0 %copy-start.1 = (bf16[1,128,1536]{2,1,0:T(8,128)(2,1)S(1)}, bf16[1,128,1536]{2,1,0:T(8,128)(2,1)}, u32[]{:S(2)}) copy-start(bf16[1,128,1536]{2,1,0:T(8,128)(2,1)} %refs_0_.1) | copy-start | bytes 1179652
  9.5 0.9 %copy-start.2 = (bf16[1,128,512]{2,1,0:T(8,128)(2,1)S(1)}, bf16[1,128,512]{2,1,0:T(8,128)(2,1)}, u32[]{:S(2)}) copy-start(bf16[1,128,512]{2,1,0:T(8,128)(2,1)} %refs_3_.1) | copy-start | bytes 393220
  10.4 0.9 %copy-start.3 = (bf16[1,128,512]{2,1,0:T(8,128)(2,1)S(1)}, bf16[1,128,512]{2,1,0:T(8,128)(2,1)}, u32[]{:S(2)}) copy-start(bf16[1,128,512]{2,1,0:T(8,128)(2,1)} %refs_2_.1) | copy-start | bytes 393220
  11.3 0.7 %copy-start.4 = (f32[12,8]{0,1:T(8,128)S(1)}, f32[12,8]{0,1:T(8,128)}, u32[]{:S(2)}) copy-start(f32[12,8]{0,1:T(8,128)} %param.9) | copy-start | bytes 1156
  30.4 4.0 %collective-permute-start.4 = (f32[2,12,256]{2,1,0:T(8,128)S(1)}, f32[2,12,256]{2,1,0:T(8,128)S(1)}, u32[]{:S(2)}, u32[]{:S(2)}) collective-permute-start(f32[2,12,256]{2,1,0:T(8,128)S(1)} %get-tuple-element.48), channel_id=1, source_target_pairs={{4,0},{0,4},{12,8},{8,12},{5,1},{1,5},{13,9},{9,13},{6,2},{2,6},{1... | collective-permute-start | bytes 73736 | tf_op jit(solution)/shard_map/ppermute | solution.py:267
  37.5 7.7 %collective-permute-start.6 = (f16[144,256]{1,0:T(8,128)(2,1)S(1)}, f16[144,256]{1,0:T(8,128)(2,1)S(1)}, u32[]{:S(2)}, u32[]{:S(2)}) collective-permute-start(f16[144,256]{1,0:T(8,128)(2,1)S(1)} %convert_element_type.41), channel_id=1, source_target_pairs={{0,8},{4,12},{8,0},{12,4},{16,24},{20,28},{24,16},{28,20},{1,9},{5... | collective-permute-start | bytes 221192 | tf_op jit(solution)/shard_map/ppermute | solution.py:275
  38.6 10.0 %collective-permute-start.7 = (f32[16,128]{1,0:T(8,128)S(1)}, f32[16,128]{1,0:T(8,128)S(1)}, u32[]{:S(2)}, u32[]{:S(2)}) collective-permute-start(f32[16,128]{1,0:T(8,128)S(1)} %get-tuple-element.60), channel_id=1, source_target_pairs={{12,0},{8,4},{4,8},{0,12},{13,1},{9,5},{5,9},{1,13},{14,2},{10,6},... | collective-permute-start | bytes 24584 | tf_op jit(solution)/shard_map/ppermute | solution.py:267
  40.4 10.9 %collective-permute-start.12 = (f16[128,256]{1,0:T(8,128)(2,1)S(1)}, f16[128,256]{1,0:T(8,128)(2,1)S(1)}, u32[]{:S(2)}, u32[]{:S(2)}) collective-permute-start(f16[128,256]{1,0:T(8,128)(2,1)S(1)} %convert_element_type.50), channel_id=1, source_target_pairs={{0,24},{4,28},{8,16},{12,20},{16,8},{20,12},{24,0},{28,4},{1,25},{... | collective-permute-start | bytes 196616 | tf_op jit(solution)/shard_map/ppermute | solution.py:275
  43.2 8.2 %collective-permute-start.11 = (f16[128,256]{1,0:T(8,128)(2,1)S(1)}, f16[128,256]{1,0:T(8,128)(2,1)S(1)}, u32[]{:S(2)}, u32[]{:S(2)}) collective-permute-start(f16[128,256]{1,0:T(8,128)(2,1)S(1)} %convert_element_type.46), channel_id=1, source_target_pairs={{0,20},{4,16},{8,28},{12,24},{16,4},{20,0},{24,12},{28,8},{1,21},{... | collective-permute-start | bytes 196616 | tf_op jit(solution)/shard_map/ppermute | solution.py:275
  44.0 4.6 %collective-permute-start.5 = (f16[144,256]{1,0:T(8,128)(2,1)S(1)}, f16[144,256]{1,0:T(8,128)(2,1)S(1)}, u32[]{:S(2)}, u32[]{:S(2)}) collective-permute-start(f16[144,256]{1,0:T(8,128)(2,1)S(1)} %convert_element_type.39), channel_id=1, source_target_pairs={{0,4},{4,0},{8,12},{12,8},{16,20},{20,16},{24,28},{28,24},{1,5},{5... | collective-permute-start | bytes 221192 | tf_op jit(solution)/shard_map/ppermute | solution.py:275
  45.2 6.2 %collective-permute-start.10 = (f16[256,256]{1,0:T(8,128)(2,1)S(1)}, f16[256,256]{1,0:T(8,128)(2,1)S(1)}, u32[]{:S(2)}, u32[]{:S(2)}) collective-permute-start(f16[256,256]{1,0:T(8,128)(2,1)S(1)} %convert_element_type.44), channel_id=1, source_target_pairs={{0,16},{4,20},{8,24},{12,28},{16,0},{20,4},{24,8},{28,12},{1,17},{... | collective-permute-start | bytes 393224 | tf_op jit(solution)/shard_map/ppermute | solution.py:275
  48.6 1.2 %collective-permute-start.8 = (f32[16,128]{1,0:T(8,128)S(1)}, f32[16,128]{1,0:T(8,128)S(1)}, u32[]{:S(2)}, u32[]{:S(2)}) collective-permute-start(f32[16,128]{1,0:T(8,128)S(1)} %fusion.2), channel_id=1, source_target_pairs={{0,1},{1,0},{2,3},{3,2},{4,5},{5,4},{6,7},{7,6},{8,9},{9,8},{10,11... | collective-permute-start | bytes 24584 | tf_op jit(solution)/shard_map/ppermute | solution.py:381
  49.9 3.7 %collective-permute-start.9 = (f32[16,128]{1,0:T(8,128)S(1)}, f32[16,128]{1,0:T(8,128)S(1)}, u32[]{:S(2)}, u32[]{:S(2)}) collective-permute-start(f32[16,128]{1,0:T(8,128)S(1)} %add.44), channel_id=1, source_target_pairs={{0,2},{1,3},{2,0},{3,1},{4,6},{5,7},{6,4},{7,5},{8,10},{9,11},{10,... | collective-permute-start | bytes 24584 | tf_op jit(solution)/shard_map/ppermute | solution.py:381

commit v7 on v6

--- a/solution.py
+++ b/solution.py
@@ -18,7 +18,7 @@
 BACK_BLOCK = 16
 RIDE_ROWS = 16
 LANES = 128
-STUDENT_FLOPS = 64 * 10**8
+STUDENT_FLOPS = 30*10**8
 VMEM_LIMIT = 8 * 1024 * 1024
 
 F32 = jnp.float32
@@ -92,14 +92,41 @@
     return parts[0] if len(parts) == 1 else jnp.concatenate(parts, axis=0)
 
 
-def student_kernel(row_parts, key_parts, heads, *refs):
-    key_s, query_s, refs = refs[:key_parts], refs[key_parts : key_parts + row_parts], refs[key_parts + row_parts :]
-    lift_hi, lift_lo, lifted, exp_l, stu_hi, stu_lo, top, lse = refs
-    keys, rows = stu_hi.shape[1:]
+def share_kernel(count, *refs):
+    sources, targets, semaphores = refs[:count], refs[count : 2 * count], refs[-1]
+    size = targets[0].shape[1]
+    start = pl.multiple_of(lax.axis_index("head") * size, size)
+    moves = [
+        pltpu.make_async_copy(source.at[:, pl.ds(start, size), :], target, semaphores.at[i])
+        for i, (source, target) in enumerate(zip(sources, targets))
+    ]
+    for move in moves:
+        move.start()
+    for move in moves:
+        move.wait()
+
+
+def by_head(shards, pieces, side):
+    place = lax.axis_index("head")
+    own, *others = pieces
+    part = own.shape[1]
     for index in range(HEADS_S):
         columns = slice(index * HD_S, (index + 1) * HD_S)
-        student = dot(stacked(key_s, columns), stacked(query_s, columns), ((1,), (1,)))
-        stu_hi[index], stu_lo[index] = split(student)
+        side[index, :part] = own[0, :, columns]
+        for i, piece in enumerate(others):
+            size = piece.shape[1]
+            first = (i // shards + 1) * part + lax.rem(place + shards - i % shards, shards) * size
+            side[index, pl.ds(pl.multiple_of(first, size), size), :] = piece[0, :, columns]
+
+
+def student_kernel(counts, shards, heads, *refs):
+    key_s, query_s, refs = refs[: counts[0]], refs[counts[0] : sum(counts)], refs[sum(counts) :]
+    lift_hi, lift_lo, lifted, exp_l, stu_hi, stu_lo, top, lse, key_side, query_side = refs
+    keys, rows = stu_hi.shape[1:]
+    by_head(shards, key_s, key_side)
+    by_head(shards, query_s, query_side)
+    for index in range(HEADS_S):
+        stu_hi[index], stu_lo[index] = split(dot(key_side[index], query_side[index], ((1,), (1,))))
     for start in range(0, keys, LIFT_BLOCK):
         block = slice(start, start + LIFT_BLOCK)
         high = stu_hi[:, block, :].reshape(HEADS_S * LIFT_BLOCK, rows)
@@ -148,12 +175,11 @@
 
 def back_kernel(row_parts, key_parts, shards, blocks, heads, factors, *refs):
     refs = list(refs)
-    query_s = [refs.pop(0) for _ in range(row_parts)]
-    key_s = [refs.pop(0) for _ in range(key_parts)]
+    row_side, key_side = refs.pop(0), refs.pop(0)
     lse = [refs.pop(0) for _ in range(row_parts)]
     back_both, exp_l, stu_hi, stu_lo, top_l = refs[:5]
     maps = [refs[5 + 3 * i : 8 + 3 * i] for i in range(blocks)]
-    *outs, scale_t, scale_l, back, row_side, key_side, mix_acc = refs[5 + 3 * blocks :]
+    *outs, scale_t, scale_l, back, mix_acc = refs[5 + 3 * blocks :]
     keys, rows = back.shape[1:]
     part, size = rows // row_parts, keys // key_parts
     sums, pieces = outs[0], outs[1:]
@@ -213,10 +239,6 @@
     packed = jnp.transpose(packed)[:RIDE_ROWS]
     sums[...] = packed
 
-    for index in range(HEADS_S):
-        columns = slice(index * HD_S, (index + 1) * HD_S)
-        row_side[index] = stacked(query_s, columns)
-        key_side[index] = stacked(key_s, columns)
     place = lax.axis_index("head")
     per = HEADS_S // shards
     count = row_parts + key_parts - 1
@@ -277,8 +299,23 @@
     own = (teacher_key, teacher_query, student_key, student_query)
     key_t = [fetch(teacher_key, along_keys, d) for d in range(1, key_parts)]
     query_t = [fetch(teacher_query, along_rows, d) for d in range(1, row_parts)]
-    key_s = [fetch(student_key, along_keys, d) for d in range(1, key_parts)]
-    query_s = [fetch(student_query, along_rows, d) for d in range(1, row_parts)]
+    share = pltpu.VMEM((1, shard_rows // shards, HEADS_S * HD_S), BF16)
+    shares = pl.pallas_call(
+        functools.partial(share_kernel, 2),
+        out_shape=(share, share),
+        in_specs=[pl.BlockSpec(memory_space=pl.ANY)] * 2,
+        scratch_shapes=[pltpu.SemaphoreType.DMA((2,))],
+        compiler_params=pltpu.CompilerParams(vmem_limit_bytes=VMEM_LIMIT // 4),
+        name="share",
+    )(*[pltpu.with_memory_space_constraint(array, pltpu.HBM) for array in (student_key, student_query)])
+
+    def fetch_student(value, target, step):
+        value = fetch(value, target, step)
+        turns = [[(h, (h + turn) % shards) for h in range(shards)] for turn in range(1, shards)]
+        return [value] + [lax.ppermute(value, "head", pairs) for pairs in turns]
+
+    key_s = [piece for d in range(1, key_parts) for piece in fetch_student(shares[0], along_keys, d)]
+    query_s = [piece for d in range(1, row_parts) for piece in fetch_student(shares[1], along_rows, d)]
     *own, lift_hi, lift_lo, back_both = prepare(head_mix, own)
     key_t, query_t, key_s, query_s = [[mine, *rest] for mine, rest in zip(own, (key_t, query_t, key_s, query_s))]
 
@@ -286,9 +323,10 @@
     student = pltpu.VMEM((HEADS_S, keys, rows), BF16)
     stats = pltpu.VMEM((heads, rows), F32)
     both = pltpu.VMEM((2, heads, rows), F32)
-    lifted, exp_l, stu_hi, stu_lo, top_l, lse_l = pl.pallas_call(
-        functools.partial(student_kernel, row_parts, key_parts, heads),
-        out_shape=(exponents, exponents, student, student, stats, stats),
+    sides = [pltpu.VMEM((HEADS_S, size, HD_S), BF16) for size in (keys, rows)]
+    lifted, exp_l, stu_hi, stu_lo, top_l, lse_l, key_side, row_side = pl.pallas_call(
+        functools.partial(student_kernel, (len(key_s), len(query_s)), shards, heads),
+        out_shape=(exponents, exponents, student, student, stats, stats, *sides),
         compiler_params=pltpu.CompilerParams(vmem_limit_bytes=VMEM_LIMIT),
         cost_estimate=pl.CostEstimate(flops=STUDENT_FLOPS, bytes_accessed=1, transcendentals=1),
         name="student",
@@ -338,14 +376,12 @@
             pltpu.VMEM((heads, rows), F32),
             pltpu.VMEM((heads, rows), F32),
             pltpu.VMEM((HEADS_S, keys, rows), BF16),
-            pltpu.VMEM((HEADS_S, rows, HD_S), BF16),
-            pltpu.VMEM((HEADS_S, keys, HD_S), BF16),
             pltpu.VMEM((heads * LIFT_BLOCK, HEADS_S * LIFT_BLOCK), F32),
         ],
         compiler_params=pltpu.CompilerParams(vmem_limit_bytes=VMEM_LIMIT),
         name="back",
     )(
-        *query_s, *key_s, *lse_parts, back_both, exp_l, stu_hi, stu_lo, top_l,
+        row_side, key_side, *lse_parts, back_both, exp_l, stu_hi, stu_lo, top_l,
         *[ref for block in done for ref in block],
     )
 

time: 54.4 us -> 55.6 us (1.022)
  starting transfers between devices: 17.4 us -> 21 us
  waiting for transfers between devices: 20.7 us -> 17.2 us
  Pallas kernels: 9.16 us -> 10.2 us
    ppermute x6, waiting for transfers between devices: 16.4 us -> 12 us  [fetch(): lax.ppermute(value, 'seq', [(target(i, step), i) for i in range(length)])]
    ppermute x0 -> x2, starting transfers between devices: none -> 3.4 us  [fetch_student(): return [value] + [lax.ppermute(value, 'head', pairs) for pairs in turns]]
    pallas_call x1 -> x2, Pallas kernels: 2.19 us -> 3.21 us  [the longest x1 2.31 us: body(): pl.pallas_call(functools.partial(student_kernel, (len(key_s), len(query_s...]
    ppermute x5, starting transfers between devices: 7.43 us -> 8.24 us  [deliver(): return lax.ppermute(value, ('head', 'seq'), pairs)]
    ppermute x5, waiting for transfers between devices: 1.84 us -> 2.64 us  [deliver(): return lax.ppermute(value, ('head', 'seq'), pairs)]
    ppermute x6, starting transfers between devices: 8.42 us -> 7.82 us  [fetch(): lax.ppermute(value, 'seq', [(target(i, step), i) for i in range(length)])]
  transfers between devices with their start and end apart: 13 -> 15, of which waited for: 7 -> 6; matrix products, arithmetic and copies ran while one was open for 3% -> 3% of each run, Pallas kernels for 9% -> 9%
where the time goes in v7:
time: 55.6 us; the launch traced here: 55.2 us
  starting transfers between devices  21 us (38%)
  waiting for transfers between devices  17.2 us (31%)
  Pallas kernels  10.2 us (18%)
  local copies, waits for them, and re-layouts  5.25 us (9%)
  other arithmetic  0.86 us (2%)
  between operations  0.75 us (1%)
    ppermute x6, waiting for transfers between devices, fetch(): lax.ppermute(value, 'seq', [(target(i, step), i) for i in range(length)])  12 us
    ppermute x5, starting transfers between devices, deliver(): return lax.ppermute(value, ('head', 'seq'), pairs)  8.24 us
    ppermute x6, starting transfers between devices, fetch(): lax.ppermute(value, 'seq', [(target(i, step), i) for i in range(length)])  7.82 us
    unnamed x11, local copies, waits for them, and re-layouts  5.25 us
    ppermute x2, starting transfers between devices, fetch_student(): return [value] + [lax.ppermute(value, 'head', pairs) for pairs in turns]  3.4 us
    pallas_call x1, Pallas kernels, body(): pl.pallas_call(functools.partial(back_kernel, row_parts, key_parts, shard...  3.04 us
    ppermute x5, waiting for transfers between devices, deliver(): return lax.ppermute(value, ('head', 'seq'), pairs)  2.64 us
    ppermute x2, waiting for transfers between devices, body(): last = lax.ppermute(total, 'dp', [(i, i ^ 1 << bit) for i in range(copies)])  2.52 us
  transfers between devices with their start and end apart: 15, of which 6 were waited for; matrix products, arithmetic and copies ran while one was open for 3% of the time, Pallas kernels for 9%

profile of v7, /device:TPU:0, one launch (start us, length us, event | category | flops | bytes accessed | tf_op | source)
XLA Modules:
  0.0 55.2 jit_solution(9439166325709323549)
XLA Ops:
  1.5 4.1 %collective-permute-start = (bf16[1,64,512]{2,1,0:T(8,128)(2,1)S(1)}, bf16[1,64,512]{2,1,0:T(8,128)(2,1)S(1)}, u32[]{:S(2)}, u32[]{:S(2)}) collective-permute-start(bf16[1,64,512]{2,1,0:T(8,128)(2,1)S(1)} %get-tuple-element.43), channel_id=1, source_target_pairs={{8,0},{12,4},{0,8},{4,12},{9,1},{13,5},{1,9},{5,13},{10,2},{14,6},... | collective-permute-start | bytes 196616 | tf_op jit(solution)/shard_map/ppermute | solution.py:289
  5.6 1.6 %collective-permute-start.2 = (bf16[1,64,512]{2,1,0:T(8,128)(2,1)S(1)}, bf16[1,64,512]{2,1,0:T(8,128)(2,1)S(1)}, u32[]{:S(2)}, u32[]{:S(2)}) collective-permute-start(bf16[1,64,512]{2,1,0:T(8,128)(2,1)S(1)} %get-tuple-element.45), channel_id=1, source_target_pairs={{4,0},{0,4},{12,8},{8,12},{5,1},{1,5},{13,9},{9,13},{6,2},{2,6},{1... | collective-permute-start | bytes 196616 | tf_op jit(solution)/shard_map/ppermute | solution.py:289
  7.7 0.9 %collective-permute-done.refs_1_ = bf16[1,64,512]{2,1,0:T(8,128)(2,1)S(1)} collective-permute-done((bf16[1,64,512]{2,1,0:T(8,128)(2,1)S(1)}, bf16[1,64,512]{2,1,0:T(8,128)(2,1)S(1)}, u32[]{:S(2)}, u32[]{:S(2)}) %collective-permute-start) | collective-permute-done | bytes 65568 | tf_op jit(solution)/shard_map/ppermute | solution.py:289
  8.7 1.9 %collective-permute-start.1 = (bf16[1,64,512]{2,1,0:T(8,128)(2,1)S(1)}, bf16[1,64,512]{2,1,0:T(8,128)(2,1)S(1)}, u32[]{:S(2)}, u32[]{:S(2)}) collective-permute-start(bf16[1,64,512]{2,1,0:T(8,128)(2,1)S(1)} %collective-permute-done.refs_1_), channel_id=1, source_target_pairs={{0,16},{16,0},{1,17},{17,1},{2,18},{18,2},{3,19},{19,3},{4,20},{20... | collective-permute-start | bytes 196616 | tf_op jit(solution)/shard_map/ppermute | solution.py:315
  10.6 7.2 %collective-permute-done.2.refs_4_ = bf16[1,64,512]{2,1,0:T(8,128)(2,1)S(1)} collective-permute-done((bf16[1,64,512]{2,1,0:T(8,128)(2,1)S(1)}, bf16[1,64,512]{2,1,0:T(8,128)(2,1)S(1)}, u32[]{:S(2)}, u32[]{:S(2)}) %collective-permute-start.2) | collective-permute-done | bytes 65568 | tf_op jit(solution)/shard_map/ppermute | solution.py:289
  17.7 1.5 %collective-permute-start.3 = (bf16[1,64,512]{2,1,0:T(8,128)(2,1)S(1)}, bf16[1,64,512]{2,1,0:T(8,128)(2,1)S(1)}, u32[]{:S(2)}, u32[]{:S(2)}) collective-permute-start(bf16[1,64,512]{2,1,0:T(8,128)(2,1)S(1)} %collective-permute-done.2.refs_4_), channel_id=1, source_target_pairs={{0,16},{16,0},{1,17},{17,1},{2,18},{18,2},{3,19},{19,3},{4,20},{20... | collective-permute-start | bytes 196616 | tf_op jit(solution)/shard_map/ppermute | solution.py:315
  20.0 0.9 %copy-done = bf16[1,128,512]{2,1,0:T(8,128)(2,1)S(1)} copy-done((bf16[1,128,512]{2,1,0:T(8,128)(2,1)S(1)}, bf16[1,128,512]{2,1,0:T(8,128)(2,1)}, u32[]{:S(2)}) %copy-start) | copy-done | bytes 131096
  20.9 0.9 %copy-done.1 = bf16[1,128,512]{2,1,0:T(8,128)(2,1)S(1)} copy-done((bf16[1,128,512]{2,1,0:T(8,128)(2,1)S(1)}, bf16[1,128,512]{2,1,0:T(8,128)(2,1)}, u32[]{:S(2)}) %copy-start.1) | copy-done | bytes 131096
  21.8 1.0 %copy-done.2 = bf16[1,128,1536]{2,1,0:T(8,128)(2,1)S(1)} copy-done((bf16[1,128,1536]{2,1,0:T(8,128)(2,1)S(1)}, bf16[1,128,1536]{2,1,0:T(8,128)(2,1)}, u32[]{:S(2)}) %copy-start.2) | copy-done | bytes 393240
  22.8 1.0 %copy-done.3 = bf16[1,128,1536]{2,1,0:T(8,128)(2,1)S(1)} copy-done((bf16[1,128,1536]{2,1,0:T(8,128)(2,1)S(1)}, bf16[1,128,1536]{2,1,0:T(8,128)(2,1)}, u32[]{:S(2)}) %copy-start.3) | copy-done | bytes 393240
  24.5 1.0 %prepare.1 = (bf16[1,128,1536]{2,1,0:T(8,128)(2,1)S(1)}, bf16[1,128,1536]{2,1,0:T(8,128)(2,1)S(1)}, bf16[1,128,512]{2,1,0:T(8,128)(2,1)S(1)}, bf16[1,128,512]{2,...) custom-call(f32[12,8]{1,0:T(8,128)S(1)} %copy.9.mix_ref, ...), custom_call_target="tpu_custom_call" | custom-call | tf_op jit(solution)/shard_map/prepare/pallas_call | solution.py:80
  25.5 2.3 %student.1 = (f32[12,256,256]{2,1,0:T(8,128)S(1)}, f32[12,256,256]{2,1,0:T(8,128)S(1)}, bf16[8,256,256]{2,1,0:T(8,128)(2,1)S(1)}, bf16[8,256,256]{2,1,0:T(8,128)...) custom-call(bf16[1,128,512]{2,1,0:T(8,128)(2,1)S(1)} %get-tuple-elem, ...), custom_call_target="tpu_custom_call" | custom-call | flops 3000000000 | bytes 1 | tf_op jit(solution)/shard_map/student/pallas_call | solution.py:327
  27.8 1.5 %teacher.2 = (f32[12,128,256]{2,1,0:T(8,128)S(1)}, f32[12,256]{1,0:T(8,128)S(1)}, f32[12,256]{1,0:T(8,128)S(1)}, f32[2,12,256]{2,1,0:T(8,128)S(1)}, f32[2,12,256]{2,1,0:T(8,128)}) custom-call(bf16[1,128,1536]{2,1,0:T(8,128)(2,1)S(1)} %get-tuple-element.53.refs_0_, bf16[1,128,1536]{2,1,0:T(8,128)(2,1)S(1)} %get-tuple-element.50.refs_1_, ...), custom_call_target="tpu_custom_call" | custom-call | tf_op jit(solution)/shard_map/teacher/pallas_call | solution.py:337
  30.3 3.9 %collective-permute-done.6.refs_3_ = f32[2,12,256]{2,1,0:T(8,128)S(1)} collective-permute-done((f32[2,12,256]{2,1,0:T(8,128)S(1)}, f32[2,12,256]{2,1,0:T(8,128)S(1)}, u32[]{:S(2)}, u32[]{:S(2)}) %collective-permute-start.6) | collective-permute-done | bytes 24608 | tf_op jit(solution)/shard_map/ppermute | solution.py:289
  34.2 3.0 %back.1 = (f32[16,128]{1,0:T(8,128)S(1)}, f32[256,256]{1,0:T(8,128)S(1)}, f32[144,256]{1,0:T(8,128)S(1)}, f32[144,256]{1,0:T(8,128)S(1)}, f32[256,256]{1,0:T(8,1...) custom-call(bf16[8,256,64]{2,1,0:T(8,128)(2,1)S(1)} %get-tuple-element.48.refs_0_, ...), custom_call_target="tpu_custom_call" | custom-call | tf_op jit(solution)/shard_map/back/pallas_call | solution.py:364
  37.2 2.7 %collective-permute-start.8 = (f16[144,256]{1,0:T(8,128)(2,1)S(1)}, f16[144,256]{1,0:T(8,128)(2,1)S(1)}, u32[]{:S(2)}, u32[]{:S(2)}) collective-permute-start(f16[144,256]{1,0:T(8,128)(2,1)S(1)} %convert_element_type.41), channel_id=1, source_target_pairs={{0,8},{4,12},{8,0},{12,4},{16,24},{20,28},{24,16},{28,20},{1,9},{5... | collective-permute-start | bytes 221192 | tf_op jit(solution)/shard_map/ppermute | solution.py:297
  39.9 1.5 %collective-permute-start.9 = (f32[16,128]{1,0:T(8,128)S(1)}, f32[16,128]{1,0:T(8,128)S(1)}, u32[]{:S(2)}, u32[]{:S(2)}) collective-permute-start(f32[16,128]{1,0:T(8,128)S(1)} %get-tuple-element.68), channel_id=1, source_target_pairs={{12,0},{8,4},{4,8},{0,12},{13,1},{9,5},{5,9},{1,13},{14,2},{10,6},... | collective-permute-start | bytes 24584 | tf_op jit(solution)/shard_map/ppermute | solution.py:289
  41.5 2.0 %collective-permute-start.14 = (f16[128,256]{1,0:T(8,128)(2,1)S(1)}, f16[128,256]{1,0:T(8,128)(2,1)S(1)}, u32[]{:S(2)}, u32[]{:S(2)}) collective-permute-start(f16[128,256]{1,0:T(8,128)(2,1)S(1)} %convert_element_type.50), channel_id=1, source_target_pairs={{0,24},{4,28},{8,16},{12,20},{16,8},{20,12},{24,0},{28,4},{1,25},{... | collective-permute-start | bytes 196616 | tf_op jit(solution)/shard_map/ppermute | solution.py:297
  43.5 1.9 %collective-permute-start.13 = (f16[128,256]{1,0:T(8,128)(2,1)S(1)}, f16[128,256]{1,0:T(8,128)(2,1)S(1)}, u32[]{:S(2)}, u32[]{:S(2)}) collective-permute-start(f16[128,256]{1,0:T(8,128)(2,1)S(1)} %convert_element_type.46), channel_id=1, source_target_pairs={{0,20},{4,16},{8,28},{12,24},{16,4},{20,0},{24,12},{28,8},{1,21},{... | collective-permute-start | bytes 196616 | tf_op jit(solution)/shard_map/ppermute | solution.py:297
  45.4 1.1 %collective-permute-start.7 = (f16[144,256]{1,0:T(8,128)(2,1)S(1)}, f16[144,256]{1,0:T(8,128)(2,1)S(1)}, u32[]{:S(2)}, u32[]{:S(2)}) collective-permute-start(f16[144,256]{1,0:T(8,128)(2,1)S(1)} %convert_element_type.39), channel_id=1, source_target_pairs={{0,4},{4,0},{8,12},{12,8},{16,20},{20,16},{24,28},{28,24},{1,5},{5... | collective-permute-start | bytes 221192 | tf_op jit(solution)/shard_map/ppermute | solution.py:297
  47.1 2.6 %collective-permute-done.7 = f16[144,256]{1,0:T(8,128)(2,1)S(1)} collective-permute-done((f16[144,256]{1,0:T(8,128)(2,1)S(1)}, f16[144,256]{1,0:T(8,128)(2,1)S(1)}, u32[]{:S(2)}, u32[]{:S(2)}) %collective-permute-start.7) | collective-permute-done | bytes 73760 | tf_op jit(solution)/shard_map/ppermute | solution.py:297
  49.8 1.2 %collective-permute-done.10 = f32[16,128]{1,0:T(8,128)S(1)} collective-permute-done((f32[16,128]{1,0:T(8,128)S(1)}, f32[16,128]{1,0:T(8,128)S(1)}, u32[]{:S(2)}, u32[]{:S(2)}) %collective-permute-start.10) | collective-permute-done | bytes 8224 | tf_op jit(solution)/shard_map/ppermute | solution.py:417
  51.0 1.5 %collective-permute-start.11 = (f32[16,128]{1,0:T(8,128)S(1)}, f32[16,128]{1,0:T(8,128)S(1)}, u32[]{:S(2)}, u32[]{:S(2)}) collective-permute-start(f32[16,128]{1,0:T(8,128)S(1)} %add.44), channel_id=1, source_target_pairs={{0,2},{1,3},{2,0},{3,1},{4,6},{5,7},{6,4},{7,5},{8,10},{9,11},{10,... | collective-permute-start | bytes 24584 | tf_op jit(solution)/shard_map/ppermute | solution.py:417
  53.3 1.4 %collective-permute-done.11 = f32[16,128]{1,0:T(8,128)S(1)} collective-permute-done((f32[16,128]{1,0:T(8,128)S(1)}, f32[16,128]{1,0:T(8,128)S(1)}, u32[]{:S(2)}, u32[]{:S(2)}) %collective-permute-start.11) | collective-permute-done | bytes 8224 | tf_op jit(solution)/shard_map/ppermute | solution.py:417
  (35 shorter events, 6.0 us)
Async XLA Ops:
  1.5 7.2 %collective-permute-start = (bf16[1,64,512]{2,1,0:T(8,128)(2,1)S(1)}, bf16[1,64,512]{2,1,0:T(8,128)(2,1)S(1)}, u32[]{:S(2)}, u32[]{:S(2)}) collective-permute-start(bf16[1,64,512]{2,1,0:T(8,128)(2,1)S(1)} %get-tuple-element.43), channel_id=1, source_target_pairs={{8,0},{12,4},{0,8},{4,12},{9,1},{13,5},{1,9},{5,13},{10,2},{14,6},... | collective-permute-start | bytes 196616 | tf_op jit(solution)/shard_map/ppermute | solution.py:289
  5.6 12.1 %collective-permute-start.2 = (bf16[1,64,512]{2,1,0:T(8,128)(2,1)S(1)}, bf16[1,64,512]{2,1,0:T(8,128)(2,1)S(1)}, u32[]{:S(2)}, u32[]{:S(2)}) collective-permute-start(bf16[1,64,512]{2,1,0:T(8,128)(2,1)S(1)} %get-tuple-element.45), channel_id=1, source_target_pairs={{4,0},{0,4},{12,8},{8,12},{5,1},{1,5},{13,9},{9,13},{6,2},{2,6},{1... | collective-permute-start | bytes 196616 | tf_op jit(solution)/shard_map/ppermute | solution.py:289
  7.2 20.6 %collective-permute-start.5 = (bf16[1,128,1536]{2,1,0:T(8,128)(2,1)}, bf16[1,128,1536]{2,1,0:T(8,128)(2,1)S(1)}, u32[]{:S(2)}, u32[]{:S(2)}) collective-permute-start(bf16[1,128,1536]{2,1,0:T(8,128)(2,1)} %refs_1_.2), channel_id=1, source_target_pairs={{4,0},{0,4},{12,8},{8,12},{5,1},{1,5},{13,9},{9,13},{6,2},{2,6},{1... | collective-permute-start | bytes 1179656 | tf_op jit(solution)/shard_map/ppermute | solution.py:289
  7.7 21.6 %collective-permute-start.4 = (bf16[1,128,1536]{2,1,0:T(8,128)(2,1)}, bf16[1,128,1536]{2,1,0:T(8,128)(2,1)S(1)}, u32[]{:S(2)}, u32[]{:S(2)}) collective-permute-start(bf16[1,128,1536]{2,1,0:T(8,128)(2,1)} %refs_0_.2), channel_id=1, source_target_pairs={{8,0},{12,4},{0,8},{4,12},{9,1},{13,5},{1,9},{5,13},{10,2},{14,6},... | collective-permute-start | bytes 1179656 | tf_op jit(solution)/shard_map/ppermute | solution.py:289
  8.7 16.8 %collective-permute-start.1 = (bf16[1,64,512]{2,1,0:T(8,128)(2,1)S(1)}, bf16[1,64,512]{2,1,0:T(8,128)(2,1)S(1)}, u32[]{:S(2)}, u32[]{:S(2)}) collective-permute-start(bf16[1,64,512]{2,1,0:T(8,128)(2,1)S(1)} %collective-permute-done.refs_1_), channel_id=1, source_target_pairs={{0,16},{16,0},{1,17},{17,1},{2,18},{18,2},{3,19},{19,3},{4,20},{20... | collective-permute-start | bytes 196616 | tf_op jit(solution)/shard_map/ppermute | solution.py:315
  17.7 7.8 %collective-permute-start.3 = (bf16[1,64,512]{2,1,0:T(8,128)(2,1)S(1)}, bf16[1,64,512]{2,1,0:T(8,128)(2,1)S(1)}, u32[]{:S(2)}, u32[]{:S(2)}) collective-permute-start(bf16[1,64,512]{2,1,0:T(8,128)(2,1)S(1)} %collective-permute-done.2.refs_4_), channel_id=1, source_target_pairs={{0,16},{16,0},{1,17},{17,1},{2,18},{18,2},{3,19},{19,3},{4,20},{20... | collective-permute-start | bytes 196616 | tf_op jit(solution)/shard_map/ppermute | solution.py:315
  20.0 0.9 %copy-start = (bf16[1,128,512]{2,1,0:T(8,128)(2,1)S(1)}, bf16[1,128,512]{2,1,0:T(8,128)(2,1)}, u32[]{:S(2)}) copy-start(bf16[1,128,512]{2,1,0:T(8,128)(2,1)} %refs_0_.3) | copy-start | bytes 393220
  20.9 0.9 %copy-start.1 = (bf16[1,128,512]{2,1,0:T(8,128)(2,1)S(1)}, bf16[1,128,512]{2,1,0:T(8,128)(2,1)}, u32[]{:S(2)}) copy-start(bf16[1,128,512]{2,1,0:T(8,128)(2,1)} %refs_1_.3) | copy-start | bytes 393220
  21.8 1.0 %copy-start.2 = (bf16[1,128,1536]{2,1,0:T(8,128)(2,1)S(1)}, bf16[1,128,1536]{2,1,0:T(8,128)(2,1)}, u32[]{:S(2)}) copy-start(bf16[1,128,1536]{2,1,0:T(8,128)(2,1)} %refs_1_.2) | copy-start | bytes 1179652
  22.8 1.0 %copy-start.3 = (bf16[1,128,1536]{2,1,0:T(8,128)(2,1)S(1)}, bf16[1,128,1536]{2,1,0:T(8,128)(2,1)}, u32[]{:S(2)}) copy-start(bf16[1,128,1536]{2,1,0:T(8,128)(2,1)} %refs_0_.2) | copy-start | bytes 1179652
  23.8 0.7 %copy-start.4 = (f32[12,8]{0,1:T(8,128)S(1)}, f32[12,8]{0,1:T(8,128)}, u32[]{:S(2)}) copy-start(f32[12,8]{0,1:T(8,128)} %param.9) | copy-start | bytes 1156
  30.2 4.0 %collective-permute-start.6 = (f32[2,12,256]{2,1,0:T(8,128)S(1)}, f32[2,12,256]{2,1,0:T(8,128)S(1)}, u32[]{:S(2)}, u32[]{:S(2)}) collective-permute-start(f32[2,12,256]{2,1,0:T(8,128)S(1)} %get-tuple-element.56), channel_id=1, source_target_pairs={{4,0},{0,4},{12,8},{8,12},{5,1},{1,5},{13,9},{9,13},{6,2},{2,6},{1... | collective-permute-start | bytes 73736 | tf_op jit(solution)/shard_map/ppermute | solution.py:289
  37.2 9.3 %collective-permute-start.8 = (f16[144,256]{1,0:T(8,128)(2,1)S(1)}, f16[144,256]{1,0:T(8,128)(2,1)S(1)}, u32[]{:S(2)}, u32[]{:S(2)}) collective-permute-start(f16[144,256]{1,0:T(8,128)(2,1)S(1)} %convert_element_type.41), channel_id=1, source_target_pairs={{0,8},{4,12},{8,0},{12,4},{16,24},{20,28},{24,16},{28,20},{1,9},{5... | collective-permute-start | bytes 221192 | tf_op jit(solution)/shard_map/ppermute | solution.py:297
  39.9 9.8 %collective-permute-start.9 = (f32[16,128]{1,0:T(8,128)S(1)}, f32[16,128]{1,0:T(8,128)S(1)}, u32[]{:S(2)}, u32[]{:S(2)}) collective-permute-start(f32[16,128]{1,0:T(8,128)S(1)} %get-tuple-element.68), channel_id=1, source_target_pairs={{12,0},{8,4},{4,8},{0,12},{13,1},{9,5},{5,9},{1,13},{14,2},{10,6},... | collective-permute-start | bytes 24584 | tf_op jit(solution)/shard_map/ppermute | solution.py:289
  41.5 11.0 %collective-permute-start.14 = (f16[128,256]{1,0:T(8,128)(2,1)S(1)}, f16[128,256]{1,0:T(8,128)(2,1)S(1)}, u32[]{:S(2)}, u32[]{:S(2)}) collective-permute-start(f16[128,256]{1,0:T(8,128)(2,1)S(1)} %convert_element_type.50), channel_id=1, source_target_pairs={{0,24},{4,28},{8,16},{12,20},{16,8},{20,12},{24,0},{28,4},{1,25},{... | collective-permute-start | bytes 196616 | tf_op jit(solution)/shard_map/ppermute | solution.py:297
  43.5 9.0 %collective-permute-start.13 = (f16[128,256]{1,0:T(8,128)(2,1)S(1)}, f16[128,256]{1,0:T(8,128)(2,1)S(1)}, u32[]{:S(2)}, u32[]{:S(2)}) collective-permute-start(f16[128,256]{1,0:T(8,128)(2,1)S(1)} %convert_element_type.46), channel_id=1, source_target_pairs={{0,20},{4,16},{8,28},{12,24},{16,4},{20,0},{24,12},{28,8},{1,21},{... | collective-permute-start | bytes 196616 | tf_op jit(solution)/shard_map/ppermute | solution.py:297
  45.4 4.4 %collective-permute-start.7 = (f16[144,256]{1,0:T(8,128)(2,1)S(1)}, f16[144,256]{1,0:T(8,128)(2,1)S(1)}, u32[]{:S(2)}, u32[]{:S(2)}) collective-permute-start(f16[144,256]{1,0:T(8,128)(2,1)S(1)} %convert_element_type.39), channel_id=1, source_target_pairs={{0,4},{4,0},{8,12},{12,8},{16,20},{20,16},{24,28},{28,24},{1,5},{5... | collective-permute-start | bytes 221192 | tf_op jit(solution)/shard_map/ppermute | solution.py:297
  46.5 6.0 %collective-permute-start.12 = (f16[256,256]{1,0:T(8,128)(2,1)S(1)}, f16[256,256]{1,0:T(8,128)(2,1)S(1)}, u32[]{:S(2)}, u32[]{:S(2)}) collective-permute-start(f16[256,256]{1,0:T(8,128)(2,1)S(1)} %convert_element_type.44), channel_id=1, source_target_pairs={{0,16},{4,20},{8,24},{12,28},{16,0},{20,4},{24,8},{28,12},{1,17},{... | collective-permute-start | bytes 393224 | tf_op jit(solution)/shard_map/ppermute | solution.py:297
  49.7 1.2 %collective-permute-start.10 = (f32[16,128]{1,0:T(8,128)S(1)}, f32[16,128]{1,0:T(8,128)S(1)}, u32[]{:S(2)}, u32[]{:S(2)}) collective-permute-start(f32[16,128]{1,0:T(8,128)S(1)} %fusion.2), channel_id=1, source_target_pairs={{0,1},{1,0},{2,3},{3,2},{4,5},{5,4},{6,7},{7,6},{8,9},{9,8},{10,11... | collective-permute-start | bytes 24584 | tf_op jit(solution)/shard_map/ppermute | solution.py:417
  51.0 3.7 %collective-permute-start.11 = (f32[16,128]{1,0:T(8,128)S(1)}, f32[16,128]{1,0:T(8,128)S(1)}, u32[]{:S(2)}, u32[]{:S(2)}) collective-permute-start(f32[16,128]{1,0:T(8,128)S(1)} %add.44), channel_id=1, source_target_pairs={{0,2},{1,3},{2,0},{3,1},{4,6},{5,7},{6,4},{7,5},{8,10},{9,11},{10,... | collective-permute-start | bytes 24584 | tf_op jit(solution)/shard_map/ppermute | solution.py:417

commit v8 on v7

--- a/solution.py
+++ b/solution.py
@@ -84,7 +84,7 @@
         scratch_shapes=[pltpu.SemaphoreType.DMA((count,))],
         compiler_params=pltpu.CompilerParams(vmem_limit_bytes=VMEM_LIMIT // 2),
         name="prepare",
-    )(head_mix, head_mix.T, *arrays)
+    )(head_mix, head_mix.T, *[pltpu.with_memory_space_constraint(array, pltpu.HBM) for array in arrays])
 
 
 def stacked(refs, columns):

time: 55.6 us -> 52.6 us (0.946)
  local copies, waits for them, and re-layouts: 5.25 us -> 1.45 us
  waiting for transfers between devices: 17.2 us -> 18.8 us
  starting transfers between devices: 21 us -> 20.1 us
    unnamed x11 -> x3, local copies, waits for them, and re-layouts: 5.25 us -> 1.45 us
    ppermute x6, waiting for transfers between devices: 12 us -> 14.4 us  [fetch(): lax.ppermute(value, 'seq', [(target(i, step), i) for i in range(length)])]
    ppermute x5, starting transfers between devices: 8.24 us -> 7.41 us  [deliver(): return lax.ppermute(value, ('head', 'seq'), pairs)]
    ppermute x5, waiting for transfers between devices: 2.64 us -> 1.85 us  [deliver(): return lax.ppermute(value, ('head', 'seq'), pairs)]
  transfers between devices with their start and end apart: 15 -> 15, of which waited for: 6 -> 8; matrix products, arithmetic and copies ran while one was open for 3% -> 3% of each run, Pallas kernels for 9% -> 10%
where the time goes in v8:
time: 52.6 us; the launch traced here: 52.4 us
  starting transfers between devices  20.1 us (38%)
  waiting for transfers between devices  18.8 us (36%)
  Pallas kernels  10.4 us (20%)
  local copies, waits for them, and re-layouts  1.45 us (3%)
  other arithmetic  0.86 us (2%)
  between operations  0.73 us (1%)
    ppermute x6, waiting for transfers between devices, fetch(): lax.ppermute(value, 'seq', [(target(i, step), i) for i in range(length)])  14.4 us
    ppermute x6, starting transfers between devices, fetch(): lax.ppermute(value, 'seq', [(target(i, step), i) for i in range(length)])  7.77 us
    ppermute x5, starting transfers between devices, deliver(): return lax.ppermute(value, ('head', 'seq'), pairs)  7.41 us
    ppermute x2, starting transfers between devices, fetch_student(): return [value] + [lax.ppermute(value, 'head', pairs) for pairs in turns]  3.4 us
    pallas_call x1, Pallas kernels, body(): pl.pallas_call(functools.partial(back_kernel, row_parts, key_parts, shard...  3.04 us
    ppermute x2, waiting for transfers between devices, body(): last = lax.ppermute(total, 'dp', [(i, i ^ 1 << bit) for i in range(copies)])  2.53 us
    pallas_call x2, Pallas kernels, teacher(): pl.pallas_call(functools.partial(teacher_kernel, row_parts, len(block_t),...  2.35 us
    pallas_call x1, Pallas kernels, body(): pl.pallas_call(functools.partial(student_kernel, (len(key_s), len(query_s...  2.31 us
  transfers between devices with their start and end apart: 15, of which 8 were waited for; matrix products, arithmetic and copies ran while one was open for 3% of the time, Pallas kernels for 10%

profile of v8, /device:TPU:0, one launch (start us, length us, event | category | flops | bytes accessed | tf_op | source)
XLA Modules:
  0.0 52.4 jit_solution(4826733478110541856)
XLA Ops:
  0.6 0.9 %share.1 = (bf16[1,64,512]{2,1,0:T(8,128)(2,1)S(1)}, bf16[1,64,512]{2,1,0:T(8,128)(2,1)S(1)}) custom-call(bf16[1,128,512]{2,1,0:T(8,128)(2,1)} %refs_0_.3, bf16[1,128,512]{2,1,0:T(8,128)(2,1)} %refs_1_.3), custom_call_target="tpu_custom_call" | custom-call | tf_op jit(solution)/shard_map/share/pallas_call | solution.py:303
  1.5 4.1 %collective-permute-start = (bf16[1,64,512]{2,1,0:T(8,128)(2,1)S(1)}, bf16[1,64,512]{2,1,0:T(8,128)(2,1)S(1)}, u32[]{:S(2)}, u32[]{:S(2)}) collective-permute-start(bf16[1,64,512]{2,1,0:T(8,128)(2,1)S(1)} %get-tuple-element.43), channel_id=1, source_target_pairs={{8,0},{12,4},{0,8},{4,12},{9,1},{13,5},{1,9},{5,13},{10,2},{14,6},... | collective-permute-start | bytes 196616 | tf_op jit(solution)/shard_map/ppermute | solution.py:289
  5.6 1.6 %collective-permute-start.2 = (bf16[1,64,512]{2,1,0:T(8,128)(2,1)S(1)}, bf16[1,64,512]{2,1,0:T(8,128)(2,1)S(1)}, u32[]{:S(2)}, u32[]{:S(2)}) collective-permute-start(bf16[1,64,512]{2,1,0:T(8,128)(2,1)S(1)} %get-tuple-element.45), channel_id=1, source_target_pairs={{4,0},{0,4},{12,8},{8,12},{5,1},{1,5},{13,9},{9,13},{6,2},{2,6},{1... | collective-permute-start | bytes 196616 | tf_op jit(solution)/shard_map/ppermute | solution.py:289
  7.7 0.9 %collective-permute-done.refs_1_ = bf16[1,64,512]{2,1,0:T(8,128)(2,1)S(1)} collective-permute-done((bf16[1,64,512]{2,1,0:T(8,128)(2,1)S(1)}, bf16[1,64,512]{2,1,0:T(8,128)(2,1)S(1)}, u32[]{:S(2)}, u32[]{:S(2)}) %collective-permute-start) | collective-permute-done | bytes 65568 | tf_op jit(solution)/shard_map/ppermute | solution.py:289
  8.7 1.9 %collective-permute-start.1 = (bf16[1,64,512]{2,1,0:T(8,128)(2,1)S(1)}, bf16[1,64,512]{2,1,0:T(8,128)(2,1)S(1)}, u32[]{:S(2)}, u32[]{:S(2)}) collective-permute-start(bf16[1,64,512]{2,1,0:T(8,128)(2,1)S(1)} %collective-permute-done.refs_1_), channel_id=1, source_target_pairs={{0,16},{16,0},{1,17},{17,1},{2,18},{18,2},{3,19},{19,3},{4,20},{20... | collective-permute-start | bytes 196616 | tf_op jit(solution)/shard_map/ppermute | solution.py:315
  10.6 7.2 %collective-permute-done.2.refs_4_ = bf16[1,64,512]{2,1,0:T(8,128)(2,1)S(1)} collective-permute-done((bf16[1,64,512]{2,1,0:T(8,128)(2,1)S(1)}, bf16[1,64,512]{2,1,0:T(8,128)(2,1)S(1)}, u32[]{:S(2)}, u32[]{:S(2)}) %collective-permute-start.2) | collective-permute-done | bytes 65568 | tf_op jit(solution)/shard_map/ppermute | solution.py:289
  17.7 1.5 %collective-permute-start.3 = (bf16[1,64,512]{2,1,0:T(8,128)(2,1)S(1)}, bf16[1,64,512]{2,1,0:T(8,128)(2,1)S(1)}, u32[]{:S(2)}, u32[]{:S(2)}) collective-permute-start(bf16[1,64,512]{2,1,0:T(8,128)(2,1)S(1)} %collective-permute-done.2.refs_4_), channel_id=1, source_target_pairs={{0,16},{16,0},{1,17},{17,1},{2,18},{18,2},{3,19},{19,3},{4,20},{20... | collective-permute-start | bytes 196616 | tf_op jit(solution)/shard_map/ppermute | solution.py:315
  20.7 1.2 %prepare.1 = (bf16[1,128,1536]{2,1,0:T(8,128)(2,1)S(1)}, bf16[1,128,1536]{2,1,0:T(8,128)(2,1)S(1)}, bf16[1,128,512]{2,1,0:T(8,128)(2,1)S(1)}, bf16[1,128,512]{2,...) custom-call(f32[12,8]{1,0:T(8,128)S(1)} %copy.9.mix_ref, ...), custom_call_target="tpu_custom_call" | custom-call | tf_op jit(solution)/shard_map/prepare/pallas_call | solution.py:80
  22.0 2.3 %student.1 = (f32[12,256,256]{2,1,0:T(8,128)S(1)}, f32[12,256,256]{2,1,0:T(8,128)S(1)}, bf16[8,256,256]{2,1,0:T(8,128)(2,1)S(1)}, bf16[8,256,256]{2,1,0:T(8,128)...) custom-call(bf16[1,128,512]{2,1,0:T(8,128)(2,1)S(1)} %get-tuple-elem, ...), custom_call_target="tpu_custom_call" | custom-call | flops 3000000000 | bytes 1 | tf_op jit(solution)/shard_map/student/pallas_call | solution.py:327
  24.3 2.3 %collective-permute-done.5.refs_2_ = bf16[1,128,1536]{2,1,0:T(8,128)(2,1)S(1)} collective-permute-done((bf16[1,128,1536]{2,1,0:T(8,128)(2,1)}, bf16[1,128,1536]{2,1,0:T(8,128)(2,1)S(1)}, u32[]{:S(2)}, u32[]{:S(2)}) %collective-permute-start.5) | collective-permute-done | bytes 393248 | tf_op jit(solution)/shard_map/ppermute | solution.py:289
  26.6 1.5 %teacher.2 = (f32[12,128,256]{2,1,0:T(8,128)S(1)}, f32[12,256]{1,0:T(8,128)S(1)}, f32[12,256]{1,0:T(8,128)S(1)}, f32[2,12,256]{2,1,0:T(8,128)S(1)}, f32[2,12,256]{2,1,0:T(8,128)}) custom-call(bf16[1,128,1536]{2,1,0:T(8,128)(2,1)S(1)} %get-tuple-element.53.refs_0_, bf16[1,128,1536]{2,1,0:T(8,128)(2,1)S(1)} %get-tuple-element.50.refs_1_, ...), custom_call_target="tpu_custom_call" | custom-call | tf_op jit(solution)/shard_map/teacher/pallas_call | solution.py:337
  28.1 0.9 %teacher.3 = (f32[12,128,256]{2,1,0:T(8,128)S(1)}, f32[12,256]{1,0:T(8,128)S(1)}, f32[12,256]{1,0:T(8,128)S(1)}, f32[2,12,256]{2,1,0:T(8,128)S(1)}, f32[2,12,256]{2,1,0:T(8,128)S(1)}) custom-call(bf16[1,128,1536]{2,1,0:T(8,128)(2,1)S(1)} %collective-permute-done.4.refs_0_, bf16[1,128,1536]{2,1,0:T(8,128)(2,1)S(1)} %get-tuple-element.50.refs_1_, ...), custom_call_target="tpu_custom_call" | custom-call | tf_op jit(solution)/shard_map/teacher/pallas_call | solution.py:337
  29.1 3.9 %collective-permute-done.6.refs_3_ = f32[2,12,256]{2,1,0:T(8,128)S(1)} collective-permute-done((f32[2,12,256]{2,1,0:T(8,128)S(1)}, f32[2,12,256]{2,1,0:T(8,128)S(1)}, u32[]{:S(2)}, u32[]{:S(2)}) %collective-permute-start.6) | collective-permute-done | bytes 24608 | tf_op jit(solution)/shard_map/ppermute | solution.py:289
  33.0 3.0 %back.1 = (f32[16,128]{1,0:T(8,128)S(1)}, f32[256,256]{1,0:T(8,128)S(1)}, f32[144,256]{1,0:T(8,128)S(1)}, f32[144,256]{1,0:T(8,128)S(1)}, f32[256,256]{1,0:T(8,1...) custom-call(bf16[8,256,64]{2,1,0:T(8,128)(2,1)S(1)} %get-tuple-element.48.refs_0_, ...), custom_call_target="tpu_custom_call" | custom-call | tf_op jit(solution)/shard_map/back/pallas_call | solution.py:364
  36.0 1.0 %collective-permute-start.8 = (f16[144,256]{1,0:T(8,128)(2,1)S(1)}, f16[144,256]{1,0:T(8,128)(2,1)S(1)}, u32[]{:S(2)}, u32[]{:S(2)}) collective-permute-start(f16[144,256]{1,0:T(8,128)(2,1)S(1)} %convert_element_type.41), channel_id=1, source_target_pairs={{0,8},{4,12},{8,0},{12,4},{16,24},{20,28},{24,16},{28,20},{1,9},{5... | collective-permute-start | bytes 221192 | tf_op jit(solution)/shard_map/ppermute | solution.py:297
  37.1 1.5 %collective-permute-start.9 = (f32[16,128]{1,0:T(8,128)S(1)}, f32[16,128]{1,0:T(8,128)S(1)}, u32[]{:S(2)}, u32[]{:S(2)}) collective-permute-start(f32[16,128]{1,0:T(8,128)S(1)} %get-tuple-element.68), channel_id=1, source_target_pairs={{12,0},{8,4},{4,8},{0,12},{13,1},{9,5},{5,9},{1,13},{14,2},{10,6},... | collective-permute-start | bytes 24584 | tf_op jit(solution)/shard_map/ppermute | solution.py:289
  38.6 2.8 %collective-permute-start.14 = (f16[128,256]{1,0:T(8,128)(2,1)S(1)}, f16[128,256]{1,0:T(8,128)(2,1)S(1)}, u32[]{:S(2)}, u32[]{:S(2)}) collective-permute-start(f16[128,256]{1,0:T(8,128)(2,1)S(1)} %convert_element_type.50), channel_id=1, source_target_pairs={{0,24},{4,28},{8,16},{12,20},{16,8},{20,12},{24,0},{28,4},{1,25},{... | collective-permute-start | bytes 196616 | tf_op jit(solution)/shard_map/ppermute | solution.py:297
  41.4 1.1 %collective-permute-start.13 = (f16[128,256]{1,0:T(8,128)(2,1)S(1)}, f16[128,256]{1,0:T(8,128)(2,1)S(1)}, u32[]{:S(2)}, u32[]{:S(2)}) collective-permute-start(f16[128,256]{1,0:T(8,128)(2,1)S(1)} %convert_element_type.46), channel_id=1, source_target_pairs={{0,20},{4,16},{8,28},{12,24},{16,4},{20,0},{24,12},{28,8},{1,21},{... | collective-permute-start | bytes 196616 | tf_op jit(solution)/shard_map/ppermute | solution.py:297
  42.5 0.9 %collective-permute-start.7 = (f16[144,256]{1,0:T(8,128)(2,1)S(1)}, f16[144,256]{1,0:T(8,128)(2,1)S(1)}, u32[]{:S(2)}, u32[]{:S(2)}) collective-permute-start(f16[144,256]{1,0:T(8,128)(2,1)S(1)} %convert_element_type.39), channel_id=1, source_target_pairs={{0,4},{4,0},{8,12},{12,8},{16,20},{20,16},{24,28},{28,24},{1,5},{5... | collective-permute-start | bytes 221192 | tf_op jit(solution)/shard_map/ppermute | solution.py:297
  43.4 1.6 %collective-permute-start.12 = (f16[256,256]{1,0:T(8,128)(2,1)S(1)}, f16[256,256]{1,0:T(8,128)(2,1)S(1)}, u32[]{:S(2)}, u32[]{:S(2)}) collective-permute-start(f16[256,256]{1,0:T(8,128)(2,1)S(1)} %convert_element_type.44), channel_id=1, source_target_pairs={{0,16},{4,20},{8,24},{12,28},{16,0},{20,4},{24,8},{28,12},{1,17},{... | collective-permute-start | bytes 393224 | tf_op jit(solution)/shard_map/ppermute | solution.py:297
  45.0 1.8 %collective-permute-done.7 = f16[144,256]{1,0:T(8,128)(2,1)S(1)} collective-permute-done((f16[144,256]{1,0:T(8,128)(2,1)S(1)}, f16[144,256]{1,0:T(8,128)(2,1)S(1)}, u32[]{:S(2)}, u32[]{:S(2)}) %collective-permute-start.7) | collective-permute-done | bytes 73760 | tf_op jit(solution)/shard_map/ppermute | solution.py:297
  47.0 1.2 %collective-permute-done.10 = f32[16,128]{1,0:T(8,128)S(1)} collective-permute-done((f32[16,128]{1,0:T(8,128)S(1)}, f32[16,128]{1,0:T(8,128)S(1)}, u32[]{:S(2)}, u32[]{:S(2)}) %collective-permute-start.10) | collective-permute-done | bytes 8224 | tf_op jit(solution)/shard_map/ppermute | solution.py:417
  48.1 1.5 %collective-permute-start.11 = (f32[16,128]{1,0:T(8,128)S(1)}, f32[16,128]{1,0:T(8,128)S(1)}, u32[]{:S(2)}, u32[]{:S(2)}) collective-permute-start(f32[16,128]{1,0:T(8,128)S(1)} %add.44), channel_id=1, source_target_pairs={{0,2},{1,3},{2,0},{3,1},{4,6},{5,7},{6,4},{7,5},{8,10},{9,11},{10,... | collective-permute-start | bytes 24584 | tf_op jit(solution)/shard_map/ppermute | solution.py:417
  50.4 1.4 %collective-permute-done.11 = f32[16,128]{1,0:T(8,128)S(1)} collective-permute-done((f32[16,128]{1,0:T(8,128)S(1)}, f32[16,128]{1,0:T(8,128)S(1)}, u32[]{:S(2)}, u32[]{:S(2)}) %collective-permute-start.11) | collective-permute-done | bytes 8224 | tf_op jit(solution)/shard_map/ppermute | solution.py:417
  (27 shorter events, 3.7 us)
Async XLA Ops:
  1.5 7.2 %collective-permute-start = (bf16[1,64,512]{2,1,0:T(8,128)(2,1)S(1)}, bf16[1,64,512]{2,1,0:T(8,128)(2,1)S(1)}, u32[]{:S(2)}, u32[]{:S(2)}) collective-permute-start(bf16[1,64,512]{2,1,0:T(8,128)(2,1)S(1)} %get-tuple-element.43), channel_id=1, source_target_pairs={{8,0},{12,4},{0,8},{4,12},{9,1},{13,5},{1,9},{5,13},{10,2},{14,6},... | collective-permute-start | bytes 196616 | tf_op jit(solution)/shard_map/ppermute | solution.py:289
  5.6 12.1 %collective-permute-start.2 = (bf16[1,64,512]{2,1,0:T(8,128)(2,1)S(1)}, bf16[1,64,512]{2,1,0:T(8,128)(2,1)S(1)}, u32[]{:S(2)}, u32[]{:S(2)}) collective-permute-start(bf16[1,64,512]{2,1,0:T(8,128)(2,1)S(1)} %get-tuple-element.45), channel_id=1, source_target_pairs={{4,0},{0,4},{12,8},{8,12},{5,1},{1,5},{13,9},{9,13},{6,2},{2,6},{1... | collective-permute-start | bytes 196616 | tf_op jit(solution)/shard_map/ppermute | solution.py:289
  7.2 19.4 %collective-permute-start.5 = (bf16[1,128,1536]{2,1,0:T(8,128)(2,1)}, bf16[1,128,1536]{2,1,0:T(8,128)(2,1)S(1)}, u32[]{:S(2)}, u32[]{:S(2)}) collective-permute-start(bf16[1,128,1536]{2,1,0:T(8,128)(2,1)} %refs_1_.2), channel_id=1, source_target_pairs={{4,0},{0,4},{12,8},{8,12},{5,1},{1,5},{13,9},{9,13},{6,2},{2,6},{1... | collective-permute-start | bytes 1179656 | tf_op jit(solution)/shard_map/ppermute | solution.py:289
  7.7 20.5 %collective-permute-start.4 = (bf16[1,128,1536]{2,1,0:T(8,128)(2,1)}, bf16[1,128,1536]{2,1,0:T(8,128)(2,1)S(1)}, u32[]{:S(2)}, u32[]{:S(2)}) collective-permute-start(bf16[1,128,1536]{2,1,0:T(8,128)(2,1)} %refs_0_.2), channel_id=1, source_target_pairs={{8,0},{12,4},{0,8},{4,12},{9,1},{13,5},{1,9},{5,13},{10,2},{14,6},... | collective-permute-start | bytes 1179656 | tf_op jit(solution)/shard_map/ppermute | solution.py:289
  8.7 13.2 %collective-permute-start.1 = (bf16[1,64,512]{2,1,0:T(8,128)(2,1)S(1)}, bf16[1,64,512]{2,1,0:T(8,128)(2,1)S(1)}, u32[]{:S(2)}, u32[]{:S(2)}) collective-permute-start(bf16[1,64,512]{2,1,0:T(8,128)(2,1)S(1)} %collective-permute-done.refs_1_), channel_id=1, source_target_pairs={{0,16},{16,0},{1,17},{17,1},{2,18},{18,2},{3,19},{19,3},{4,20},{20... | collective-permute-start | bytes 196616 | tf_op jit(solution)/shard_map/ppermute | solution.py:315
  17.7 4.3 %collective-permute-start.3 = (bf16[1,64,512]{2,1,0:T(8,128)(2,1)S(1)}, bf16[1,64,512]{2,1,0:T(8,128)(2,1)S(1)}, u32[]{:S(2)}, u32[]{:S(2)}) collective-permute-start(bf16[1,64,512]{2,1,0:T(8,128)(2,1)S(1)} %collective-permute-done.2.refs_4_), channel_id=1, source_target_pairs={{0,16},{16,0},{1,17},{17,1},{2,18},{18,2},{3,19},{19,3},{4,20},{20... | collective-permute-start | bytes 196616 | tf_op jit(solution)/shard_map/ppermute | solution.py:315
  20.0 0.7 %copy-start = (f32[12,8]{0,1:T(8,128)S(1)}, f32[12,8]{0,1:T(8,128)}, u32[]{:S(2)}) copy-start(f32[12,8]{0,1:T(8,128)} %param.9) | copy-start | bytes 1156
  29.0 4.0 %collective-permute-start.6 = (f32[2,12,256]{2,1,0:T(8,128)S(1)}, f32[2,12,256]{2,1,0:T(8,128)S(1)}, u32[]{:S(2)}, u32[]{:S(2)}) collective-permute-start(f32[2,12,256]{2,1,0:T(8,128)S(1)} %get-tuple-element.56), channel_id=1, source_target_pairs={{4,0},{0,4},{12,8},{8,12},{5,1},{1,5},{13,9},{9,13},{6,2},{2,6},{1... | collective-permute-start | bytes 73736 | tf_op jit(solution)/shard_map/ppermute | solution.py:289
  36.0 7.4 %collective-permute-start.8 = (f16[144,256]{1,0:T(8,128)(2,1)S(1)}, f16[144,256]{1,0:T(8,128)(2,1)S(1)}, u32[]{:S(2)}, u32[]{:S(2)}) collective-permute-start(f16[144,256]{1,0:T(8,128)(2,1)S(1)} %convert_element_type.41), channel_id=1, source_target_pairs={{0,8},{4,12},{8,0},{12,4},{16,24},{20,28},{24,16},{28,20},{1,9},{5... | collective-permute-start | bytes 221192 | tf_op jit(solution)/shard_map/ppermute | solution.py:297
  37.1 9.8 %collective-permute-start.9 = (f32[16,128]{1,0:T(8,128)S(1)}, f32[16,128]{1,0:T(8,128)S(1)}, u32[]{:S(2)}, u32[]{:S(2)}) collective-permute-start(f32[16,128]{1,0:T(8,128)S(1)} %get-tuple-element.68), channel_id=1, source_target_pairs={{12,0},{8,4},{4,8},{0,12},{13,1},{9,5},{5,9},{1,13},{14,2},{10,6},... | collective-permute-start | bytes 24584 | tf_op jit(solution)/shard_map/ppermute | solution.py:289
  38.6 11.0 %collective-permute-start.14 = (f16[128,256]{1,0:T(8,128)(2,1)S(1)}, f16[128,256]{1,0:T(8,128)(2,1)S(1)}, u32[]{:S(2)}, u32[]{:S(2)}) collective-permute-start(f16[128,256]{1,0:T(8,128)(2,1)S(1)} %convert_element_type.50), channel_id=1, source_target_pairs={{0,24},{4,28},{8,16},{12,20},{16,8},{20,12},{24,0},{28,4},{1,25},{... | collective-permute-start | bytes 196616 | tf_op jit(solution)/shard_map/ppermute | solution.py:297
  41.4 8.2 %collective-permute-start.13 = (f16[128,256]{1,0:T(8,128)(2,1)S(1)}, f16[128,256]{1,0:T(8,128)(2,1)S(1)}, u32[]{:S(2)}, u32[]{:S(2)}) collective-permute-start(f16[128,256]{1,0:T(8,128)(2,1)S(1)} %convert_element_type.46), channel_id=1, source_target_pairs={{0,20},{4,16},{8,28},{12,24},{16,4},{20,0},{24,12},{28,8},{1,21},{... | collective-permute-start | bytes 196616 | tf_op jit(solution)/shard_map/ppermute | solution.py:297
  42.5 4.4 %collective-permute-start.7 = (f16[144,256]{1,0:T(8,128)(2,1)S(1)}, f16[144,256]{1,0:T(8,128)(2,1)S(1)}, u32[]{:S(2)}, u32[]{:S(2)}) collective-permute-start(f16[144,256]{1,0:T(8,128)(2,1)S(1)} %convert_element_type.39), channel_id=1, source_target_pairs={{0,4},{4,0},{8,12},{12,8},{16,20},{20,16},{24,28},{28,24},{1,5},{5... | collective-permute-start | bytes 221192 | tf_op jit(solution)/shard_map/ppermute | solution.py:297
  43.4 6.2 %collective-permute-start.12 = (f16[256,256]{1,0:T(8,128)(2,1)S(1)}, f16[256,256]{1,0:T(8,128)(2,1)S(1)}, u32[]{:S(2)}, u32[]{:S(2)}) collective-permute-start(f16[256,256]{1,0:T(8,128)(2,1)S(1)} %convert_element_type.44), channel_id=1, source_target_pairs={{0,16},{4,20},{8,24},{12,28},{16,0},{20,4},{24,8},{28,12},{1,17},{... | collective-permute-start | bytes 393224 | tf_op jit(solution)/shard_map/ppermute | solution.py:297
  46.9 1.2 %collective-permute-start.10 = (f32[16,128]{1,0:T(8,128)S(1)}, f32[16,128]{1,0:T(8,128)S(1)}, u32[]{:S(2)}, u32[]{:S(2)}) collective-permute-start(f32[16,128]{1,0:T(8,128)S(1)} %fusion.2), channel_id=1, source_target_pairs={{0,1},{1,0},{2,3},{3,2},{4,5},{5,4},{6,7},{7,6},{8,9},{9,8},{10,11... | collective-permute-start | bytes 24584 | tf_op jit(solution)/shard_map/ppermute | solution.py:417
  48.1 3.7 %collective-permute-start.11 = (f32[16,128]{1,0:T(8,128)S(1)}, f32[16,128]{1,0:T(8,128)S(1)}, u32[]{:S(2)}, u32[]{:S(2)}) collective-permute-start(f32[16,128]{1,0:T(8,128)S(1)} %add.44), channel_id=1, source_target_pairs={{0,2},{1,3},{2,0},{3,1},{4,6},{5,7},{6,4},{7,5},{8,10},{9,11},{10,... | collective-permute-start | bytes 24584 | tf_op jit(solution)/shard_map/ppermute | solution.py:417

commit v9 on v8

--- a/solution.py
+++ b/solution.py
@@ -332,11 +332,11 @@
         name="student",
     )(*key_s, *query_s, lift_hi, lift_lo)
 
-    def teacher(block_t, offset, before):
+    def teacher(block_t, offset, before, extra):
         size = len(block_t) * shard_rows
         return pl.pallas_call(
             functools.partial(teacher_kernel, row_parts, len(block_t), heads, offset, bool(before)),
-            out_shape=(pltpu.VMEM((heads, size, rows), F32), stats, stats, both) + (both,) * (row_parts - 1),
+            out_shape=(pltpu.VMEM((heads, size, rows), F32), stats, stats, both) + (both,) * extra,
             compiler_params=pltpu.CompilerParams(vmem_limit_bytes=VMEM_LIMIT),
             name="teacher",
         )(*block_t, *query_t, lifted, lse_l, *before)
@@ -344,7 +344,8 @@
     done, before = [], []
     for first, block in ((0, key_t[:1]), (1, key_t[1:])):
         if block:
-            results = teacher(block, first * shard_rows, before)
+            extra = row_parts - 1 if first or key_parts == 1 else 0
+            results = teacher(block, first * shard_rows, before, extra)
             done.append(results[:3])
             before, turned = results[3:4], results[4:]
     lse_parts = [*before] + [fetch(turned[step - 1], along_rows, row_parts - step) for step in range(1, row_parts)]

time: 52.6 us -> 52.6 us (level)
  Pallas kernels: 10.4 us -> 9.78 us
    pallas_call x2, Pallas kernels: 2.35 us -> 1.72 us  [teacher(): pl.pallas_call(functools.partial(teacher_kernel, row_parts, len(block_t),...]
    ppermute x5, waiting for transfers between devices: 1.85 us -> 2.47 us  [deliver(): return lax.ppermute(value, ('head', 'seq'), pairs)]
  transfers between devices with their start and end apart: 15 -> 15, of which waited for: 8 -> 8; matrix products, arithmetic and copies ran while one was open for 3% -> 3% of each run, Pallas kernels for 10% -> 8%
where the time goes in v9:
time: 52.6 us; the launch traced here: 52.4 us
  starting transfers between devices  20.3 us (39%)
  waiting for transfers between devices  19.2 us (37%)
  Pallas kernels  9.78 us (19%)
  local copies, waits for them, and re-layouts  1.45 us (3%)
  other arithmetic  0.85 us (2%)
  between operations  0.73 us (1%)
    ppermute x6, waiting for transfers between devices, fetch(): lax.ppermute(value, 'seq', [(target(i, step), i) for i in range(length)])  14.1 us
    ppermute x5, starting transfers between devices, deliver(): return lax.ppermute(value, ('head', 'seq'), pairs)  7.82 us
    ppermute x6, starting transfers between devices, fetch(): lax.ppermute(value, 'seq', [(target(i, step), i) for i in range(length)])  7.57 us
    ppermute x2, starting transfers between devices, fetch_student(): return [value] + [lax.ppermute(value, 'head', pairs) for pairs in turns]  3.4 us
    pallas_call x1, Pallas kernels, body(): pl.pallas_call(functools.partial(back_kernel, row_parts, key_parts, shard...  3.04 us
    ppermute x2, waiting for transfers between devices, body(): last = lax.ppermute(total, 'dp', [(i, i ^ 1 << bit) for i in range(copies)])  2.54 us
    ppermute x5, waiting for transfers between devices, deliver(): return lax.ppermute(value, ('head', 'seq'), pairs)  2.47 us
    pallas_call x1, Pallas kernels, body(): pl.pallas_call(functools.partial(student_kernel, (len(key_s), len(query_s...  2.31 us
  transfers between devices with their start and end apart: 15, of which 8 were waited for; matrix products, arithmetic and copies ran while one was open for 3% of the time, Pallas kernels for 8%

profile of v9, /device:TPU:0, one launch (start us, length us, event | category | flops | bytes accessed | tf_op | source)
XLA Modules:
  0.0 52.4 jit_solution(10043969525472830491)
XLA Ops:
  0.6 0.9 %share.1 = (bf16[1,64,512]{2,1,0:T(8,128)(2,1)S(1)}, bf16[1,64,512]{2,1,0:T(8,128)(2,1)S(1)}) custom-call(bf16[1,128,512]{2,1,0:T(8,128)(2,1)} %refs_0_.3, bf16[1,128,512]{2,1,0:T(8,128)(2,1)} %refs_1_.3), custom_call_target="tpu_custom_call" | custom-call | tf_op jit(solution)/shard_map/share/pallas_call | solution.py:303
  1.5 4.1 %collective-permute-start = (bf16[1,64,512]{2,1,0:T(8,128)(2,1)S(1)}, bf16[1,64,512]{2,1,0:T(8,128)(2,1)S(1)}, u32[]{:S(2)}, u32[]{:S(2)}) collective-permute-start(bf16[1,64,512]{2,1,0:T(8,128)(2,1)S(1)} %get-tuple-element.43), channel_id=1, source_target_pairs={{8,0},{12,4},{0,8},{4,12},{9,1},{13,5},{1,9},{5,13},{10,2},{14,6},... | collective-permute-start | bytes 196616 | tf_op jit(solution)/shard_map/ppermute | solution.py:289
  5.6 1.6 %collective-permute-start.2 = (bf16[1,64,512]{2,1,0:T(8,128)(2,1)S(1)}, bf16[1,64,512]{2,1,0:T(8,128)(2,1)S(1)}, u32[]{:S(2)}, u32[]{:S(2)}) collective-permute-start(bf16[1,64,512]{2,1,0:T(8,128)(2,1)S(1)} %get-tuple-element.45), channel_id=1, source_target_pairs={{4,0},{0,4},{12,8},{8,12},{5,1},{1,5},{13,9},{9,13},{6,2},{2,6},{1... | collective-permute-start | bytes 196616 | tf_op jit(solution)/shard_map/ppermute | solution.py:289
  7.7 0.9 %collective-permute-done.refs_1_ = bf16[1,64,512]{2,1,0:T(8,128)(2,1)S(1)} collective-permute-done((bf16[1,64,512]{2,1,0:T(8,128)(2,1)S(1)}, bf16[1,64,512]{2,1,0:T(8,128)(2,1)S(1)}, u32[]{:S(2)}, u32[]{:S(2)}) %collective-permute-start) | collective-permute-done | bytes 65568 | tf_op jit(solution)/shard_map/ppermute | solution.py:289
  8.7 1.9 %collective-permute-start.1 = (bf16[1,64,512]{2,1,0:T(8,128)(2,1)S(1)}, bf16[1,64,512]{2,1,0:T(8,128)(2,1)S(1)}, u32[]{:S(2)}, u32[]{:S(2)}) collective-permute-start(bf16[1,64,512]{2,1,0:T(8,128)(2,1)S(1)} %collective-permute-done.refs_1_), channel_id=1, source_target_pairs={{0,16},{16,0},{1,17},{17,1},{2,18},{18,2},{3,19},{19,3},{4,20},{20... | collective-permute-start | bytes 196616 | tf_op jit(solution)/shard_map/ppermute | solution.py:315
  10.6 7.2 %collective-permute-done.2.refs_4_ = bf16[1,64,512]{2,1,0:T(8,128)(2,1)S(1)} collective-permute-done((bf16[1,64,512]{2,1,0:T(8,128)(2,1)S(1)}, bf16[1,64,512]{2,1,0:T(8,128)(2,1)S(1)}, u32[]{:S(2)}, u32[]{:S(2)}) %collective-permute-start.2) | collective-permute-done | bytes 65568 | tf_op jit(solution)/shard_map/ppermute | solution.py:289
  17.7 1.5 %collective-permute-start.3 = (bf16[1,64,512]{2,1,0:T(8,128)(2,1)S(1)}, bf16[1,64,512]{2,1,0:T(8,128)(2,1)S(1)}, u32[]{:S(2)}, u32[]{:S(2)}) collective-permute-start(bf16[1,64,512]{2,1,0:T(8,128)(2,1)S(1)} %collective-permute-done.2.refs_4_), channel_id=1, source_target_pairs={{0,16},{16,0},{1,17},{17,1},{2,18},{18,2},{3,19},{19,3},{4,20},{20... | collective-permute-start | bytes 196616 | tf_op jit(solution)/shard_map/ppermute | solution.py:315
  19.2 0.8 %copy.9.mix_ref = f32[12,8]{1,0:T(8,128)S(1)} copy(f32[12,8]{0,1:T(8,128)} %param.9) | data formatting | bytes 768 | tf_op args[4]
  20.7 1.2 %prepare.1 = (bf16[1,128,1536]{2,1,0:T(8,128)(2,1)S(1)}, bf16[1,128,1536]{2,1,0:T(8,128)(2,1)S(1)}, bf16[1,128,512]{2,1,0:T(8,128)(2,1)S(1)}, bf16[1,128,512]{2,...) custom-call(f32[12,8]{1,0:T(8,128)S(1)} %copy.9.mix_ref, ...), custom_call_target="tpu_custom_call" | custom-call | tf_op jit(solution)/shard_map/prepare/pallas_call | solution.py:80
  22.0 2.3 %student.1 = (f32[12,256,256]{2,1,0:T(8,128)S(1)}, f32[12,256,256]{2,1,0:T(8,128)S(1)}, bf16[8,256,256]{2,1,0:T(8,128)(2,1)S(1)}, bf16[8,256,256]{2,1,0:T(8,128)...) custom-call(bf16[1,128,512]{2,1,0:T(8,128)(2,1)S(1)} %get-tuple-elem, ...), custom_call_target="tpu_custom_call" | custom-call | flops 3000000000 | bytes 1 | tf_op jit(solution)/shard_map/student/pallas_call | solution.py:327
  24.3 2.3 %collective-permute-done.5.refs_2_ = bf16[1,128,1536]{2,1,0:T(8,128)(2,1)S(1)} collective-permute-done((bf16[1,128,1536]{2,1,0:T(8,128)(2,1)}, bf16[1,128,1536]{2,1,0:T(8,128)(2,1)S(1)}, u32[]{:S(2)}, u32[]{:S(2)}) %collective-permute-start.5) | collective-permute-done | bytes 393248 | tf_op jit(solution)/shard_map/ppermute | solution.py:289
  26.6 0.8 %teacher.2 = (f32[12,128,256]{2,1,0:T(8,128)S(1)}, f32[12,256]{1,0:T(8,128)S(1)}, f32[12,256]{1,0:T(8,128)S(1)}, f32[2,12,256]{2,1,0:T(8,128)S(1)}) custom-call(bf16[1,128,1536]{2,1,0:T(8,128)(2,1)S(1)} %get-tuple-element.53.refs_0_, bf16[1,128,1536]{2,1,0:T(8,128)(2,1)S(1)} %get-tuple-element.50.refs_1_, ...), custom_call_target="tpu_custom_call" | custom-call | tf_op jit(solution)/shard_map/teacher/pallas_call | solution.py:337
  27.5 0.9 %teacher.3 = (f32[12,128,256]{2,1,0:T(8,128)S(1)}, f32[12,256]{1,0:T(8,128)S(1)}, f32[12,256]{1,0:T(8,128)S(1)}, f32[2,12,256]{2,1,0:T(8,128)S(1)}, f32[2,12,256]{2,1,0:T(8,128)S(1)}) custom-call(bf16[1,128,1536]{2,1,0:T(8,128)(2,1)S(1)} %collective-permute-done.4.refs_0_, bf16[1,128,1536]{2,1,0:T(8,128)(2,1)S(1)} %get-tuple-element.50.refs_1_, ...), custom_call_target="tpu_custom_call" | custom-call | tf_op jit(solution)/shard_map/teacher/pallas_call | solution.py:337
  28.7 3.7 %collective-permute-done.6.refs_3_ = f32[2,12,256]{2,1,0:T(8,128)S(1)} collective-permute-done((f32[2,12,256]{2,1,0:T(8,128)S(1)}, f32[2,12,256]{2,1,0:T(8,128)S(1)}, u32[]{:S(2)}, u32[]{:S(2)}) %collective-permute-start.6) | collective-permute-done | bytes 24608 | tf_op jit(solution)/shard_map/ppermute | solution.py:289
  32.4 3.0 %back.1 = (f32[16,128]{1,0:T(8,128)S(1)}, f32[256,256]{1,0:T(8,128)S(1)}, f32[144,256]{1,0:T(8,128)S(1)}, f32[144,256]{1,0:T(8,128)S(1)}, f32[256,256]{1,0:T(8,1...) custom-call(bf16[8,256,64]{2,1,0:T(8,128)(2,1)S(1)} %get-tuple-element.48.refs_0_, ...), custom_call_target="tpu_custom_call" | custom-call | tf_op jit(solution)/shard_map/back/pallas_call | solution.py:365
  35.4 1.6 %collective-permute-start.8 = (f16[144,256]{1,0:T(8,128)(2,1)S(1)}, f16[144,256]{1,0:T(8,128)(2,1)S(1)}, u32[]{:S(2)}, u32[]{:S(2)}) collective-permute-start(f16[144,256]{1,0:T(8,128)(2,1)S(1)} %convert_element_type.41), channel_id=1, source_target_pairs={{0,8},{4,12},{8,0},{12,4},{16,24},{20,28},{24,16},{28,20},{1,9},{5... | collective-permute-start | bytes 221192 | tf_op jit(solution)/shard_map/ppermute | solution.py:297
  37.1 1.1 %collective-permute-start.9 = (f32[16,128]{1,0:T(8,128)S(1)}, f32[16,128]{1,0:T(8,128)S(1)}, u32[]{:S(2)}, u32[]{:S(2)}) collective-permute-start(f32[16,128]{1,0:T(8,128)S(1)} %get-tuple-element.68), channel_id=1, source_target_pairs={{12,0},{8,4},{4,8},{0,12},{13,1},{9,5},{5,9},{1,13},{14,2},{10,6},... | collective-permute-start | bytes 24584 | tf_op jit(solution)/shard_map/ppermute | solution.py:289
  38.2 2.6 %collective-permute-start.14 = (f16[128,256]{1,0:T(8,128)(2,1)S(1)}, f16[128,256]{1,0:T(8,128)(2,1)S(1)}, u32[]{:S(2)}, u32[]{:S(2)}) collective-permute-start(f16[128,256]{1,0:T(8,128)(2,1)S(1)} %convert_element_type.50), channel_id=1, source_target_pairs={{0,24},{4,28},{8,16},{12,20},{16,8},{20,12},{24,0},{28,4},{1,25},{... | collective-permute-start | bytes 196616 | tf_op jit(solution)/shard_map/ppermute | solution.py:297
  40.8 1.7 %collective-permute-start.13 = (f16[128,256]{1,0:T(8,128)(2,1)S(1)}, f16[128,256]{1,0:T(8,128)(2,1)S(1)}, u32[]{:S(2)}, u32[]{:S(2)}) collective-permute-start(f16[128,256]{1,0:T(8,128)(2,1)S(1)} %convert_element_type.46), channel_id=1, source_target_pairs={{0,20},{4,16},{8,28},{12,24},{16,4},{20,0},{24,12},{28,8},{1,21},{... | collective-permute-start | bytes 196616 | tf_op jit(solution)/shard_map/ppermute | solution.py:297
  42.8 1.6 %collective-permute-start.12 = (f16[256,256]{1,0:T(8,128)(2,1)S(1)}, f16[256,256]{1,0:T(8,128)(2,1)S(1)}, u32[]{:S(2)}, u32[]{:S(2)}) collective-permute-start(f16[256,256]{1,0:T(8,128)(2,1)S(1)} %convert_element_type.44), channel_id=1, source_target_pairs={{0,16},{4,20},{8,24},{12,28},{16,0},{20,4},{24,8},{28,12},{1,17},{... | collective-permute-start | bytes 393224 | tf_op jit(solution)/shard_map/ppermute | solution.py:297
  44.4 2.5 %collective-permute-done.7 = f16[144,256]{1,0:T(8,128)(2,1)S(1)} collective-permute-done((f16[144,256]{1,0:T(8,128)(2,1)S(1)}, f16[144,256]{1,0:T(8,128)(2,1)S(1)}, u32[]{:S(2)}, u32[]{:S(2)}) %collective-permute-start.7) | collective-permute-done | bytes 73760 | tf_op jit(solution)/shard_map/ppermute | solution.py:297
  47.0 1.2 %collective-permute-done.10 = f32[16,128]{1,0:T(8,128)S(1)} collective-permute-done((f32[16,128]{1,0:T(8,128)S(1)}, f32[16,128]{1,0:T(8,128)S(1)}, u32[]{:S(2)}, u32[]{:S(2)}) %collective-permute-start.10) | collective-permute-done | bytes 8224 | tf_op jit(solution)/shard_map/ppermute | solution.py:418
  48.1 1.5 %collective-permute-start.11 = (f32[16,128]{1,0:T(8,128)S(1)}, f32[16,128]{1,0:T(8,128)S(1)}, u32[]{:S(2)}, u32[]{:S(2)}) collective-permute-start(f32[16,128]{1,0:T(8,128)S(1)} %add.44), channel_id=1, source_target_pairs={{0,2},{1,3},{2,0},{3,1},{4,6},{5,7},{6,4},{7,5},{8,10},{9,11},{10,... | collective-permute-start | bytes 24584 | tf_op jit(solution)/shard_map/ppermute | solution.py:418
  50.4 1.4 %collective-permute-done.11 = f32[16,128]{1,0:T(8,128)S(1)} collective-permute-done((f32[16,128]{1,0:T(8,128)S(1)}, f32[16,128]{1,0:T(8,128)S(1)}, u32[]{:S(2)}, u32[]{:S(2)}) %collective-permute-start.11) | collective-permute-done | bytes 8224 | tf_op jit(solution)/shard_map/ppermute | solution.py:418
  (27 shorter events, 3.4 us)
Async XLA Ops:
  1.5 7.2 %collective-permute-start = (bf16[1,64,512]{2,1,0:T(8,128)(2,1)S(1)}, bf16[1,64,512]{2,1,0:T(8,128)(2,1)S(1)}, u32[]{:S(2)}, u32[]{:S(2)}) collective-permute-start(bf16[1,64,512]{2,1,0:T(8,128)(2,1)S(1)} %get-tuple-element.43), channel_id=1, source_target_pairs={{8,0},{12,4},{0,8},{4,12},{9,1},{13,5},{1,9},{5,13},{10,2},{14,6},... | collective-permute-start | bytes 196616 | tf_op jit(solution)/shard_map/ppermute | solution.py:289
  5.6 12.1 %collective-permute-start.2 = (bf16[1,64,512]{2,1,0:T(8,128)(2,1)S(1)}, bf16[1,64,512]{2,1,0:T(8,128)(2,1)S(1)}, u32[]{:S(2)}, u32[]{:S(2)}) collective-permute-start(bf16[1,64,512]{2,1,0:T(8,128)(2,1)S(1)} %get-tuple-element.45), channel_id=1, source_target_pairs={{4,0},{0,4},{12,8},{8,12},{5,1},{1,5},{13,9},{9,13},{6,2},{2,6},{1... | collective-permute-start | bytes 196616 | tf_op jit(solution)/shard_map/ppermute | solution.py:289
  7.2 19.4 %collective-permute-start.5 = (bf16[1,128,1536]{2,1,0:T(8,128)(2,1)}, bf16[1,128,1536]{2,1,0:T(8,128)(2,1)S(1)}, u32[]{:S(2)}, u32[]{:S(2)}) collective-permute-start(bf16[1,128,1536]{2,1,0:T(8,128)(2,1)} %refs_1_.2), channel_id=1, source_target_pairs={{4,0},{0,4},{12,8},{8,12},{5,1},{1,5},{13,9},{9,13},{6,2},{2,6},{1... | collective-permute-start | bytes 1179656 | tf_op jit(solution)/shard_map/ppermute | solution.py:289
  7.7 19.8 %collective-permute-start.4 = (bf16[1,128,1536]{2,1,0:T(8,128)(2,1)}, bf16[1,128,1536]{2,1,0:T(8,128)(2,1)S(1)}, u32[]{:S(2)}, u32[]{:S(2)}) collective-permute-start(bf16[1,128,1536]{2,1,0:T(8,128)(2,1)} %refs_0_.2), channel_id=1, source_target_pairs={{8,0},{12,4},{0,8},{4,12},{9,1},{13,5},{1,9},{5,13},{10,2},{14,6},... | collective-permute-start | bytes 1179656 | tf_op jit(solution)/shard_map/ppermute | solution.py:289
  8.7 13.2 %collective-permute-start.1 = (bf16[1,64,512]{2,1,0:T(8,128)(2,1)S(1)}, bf16[1,64,512]{2,1,0:T(8,128)(2,1)S(1)}, u32[]{:S(2)}, u32[]{:S(2)}) collective-permute-start(bf16[1,64,512]{2,1,0:T(8,128)(2,1)S(1)} %collective-permute-done.refs_1_), channel_id=1, source_target_pairs={{0,16},{16,0},{1,17},{17,1},{2,18},{18,2},{3,19},{19,3},{4,20},{20... | collective-permute-start | bytes 196616 | tf_op jit(solution)/shard_map/ppermute | solution.py:315
  17.7 4.3 %collective-permute-start.3 = (bf16[1,64,512]{2,1,0:T(8,128)(2,1)S(1)}, bf16[1,64,512]{2,1,0:T(8,128)(2,1)S(1)}, u32[]{:S(2)}, u32[]{:S(2)}) collective-permute-start(bf16[1,64,512]{2,1,0:T(8,128)(2,1)S(1)} %collective-permute-done.2.refs_4_), channel_id=1, source_target_pairs={{0,16},{16,0},{1,17},{17,1},{2,18},{18,2},{3,19},{19,3},{4,20},{20... | collective-permute-start | bytes 196616 | tf_op jit(solution)/shard_map/ppermute | solution.py:315
  20.0 0.7 %copy-start = (f32[12,8]{0,1:T(8,128)S(1)}, f32[12,8]{0,1:T(8,128)}, u32[]{:S(2)}) copy-start(f32[12,8]{0,1:T(8,128)} %param.9) | copy-start | bytes 1156
  28.4 4.0 %collective-permute-start.6 = (f32[2,12,256]{2,1,0:T(8,128)S(1)}, f32[2,12,256]{2,1,0:T(8,128)S(1)}, u32[]{:S(2)}, u32[]{:S(2)}) collective-permute-start(f32[2,12,256]{2,1,0:T(8,128)S(1)} %get-tuple-element.56), channel_id=1, source_target_pairs={{4,0},{0,4},{12,8},{8,12},{5,1},{1,5},{13,9},{9,13},{6,2},{2,6},{1... | collective-permute-start | bytes 73736 | tf_op jit(solution)/shard_map/ppermute | solution.py:289
  35.4 7.4 %collective-permute-start.8 = (f16[144,256]{1,0:T(8,128)(2,1)S(1)}, f16[144,256]{1,0:T(8,128)(2,1)S(1)}, u32[]{:S(2)}, u32[]{:S(2)}) collective-permute-start(f16[144,256]{1,0:T(8,128)(2,1)S(1)} %convert_element_type.41), channel_id=1, source_target_pairs={{0,8},{4,12},{8,0},{12,4},{16,24},{20,28},{24,16},{28,20},{1,9},{5... | collective-permute-start | bytes 221192 | tf_op jit(solution)/shard_map/ppermute | solution.py:297
  37.1 9.8 %collective-permute-start.9 = (f32[16,128]{1,0:T(8,128)S(1)}, f32[16,128]{1,0:T(8,128)S(1)}, u32[]{:S(2)}, u32[]{:S(2)}) collective-permute-start(f32[16,128]{1,0:T(8,128)S(1)} %get-tuple-element.68), channel_id=1, source_target_pairs={{12,0},{8,4},{4,8},{0,12},{13,1},{9,5},{5,9},{1,13},{14,2},{10,6},... | collective-permute-start | bytes 24584 | tf_op jit(solution)/shard_map/ppermute | solution.py:289
  38.2 11.4 %collective-permute-start.14 = (f16[128,256]{1,0:T(8,128)(2,1)S(1)}, f16[128,256]{1,0:T(8,128)(2,1)S(1)}, u32[]{:S(2)}, u32[]{:S(2)}) collective-permute-start(f16[128,256]{1,0:T(8,128)(2,1)S(1)} %convert_element_type.50), channel_id=1, source_target_pairs={{0,24},{4,28},{8,16},{12,20},{16,8},{20,12},{24,0},{28,4},{1,25},{... | collective-permute-start | bytes 196616 | tf_op jit(solution)/shard_map/ppermute | solution.py:297
  40.8 8.8 %collective-permute-start.13 = (f16[128,256]{1,0:T(8,128)(2,1)S(1)}, f16[128,256]{1,0:T(8,128)(2,1)S(1)}, u32[]{:S(2)}, u32[]{:S(2)}) collective-permute-start(f16[128,256]{1,0:T(8,128)(2,1)S(1)} %convert_element_type.46), channel_id=1, source_target_pairs={{0,20},{4,16},{8,28},{12,24},{16,4},{20,0},{24,12},{28,8},{1,21},{... | collective-permute-start | bytes 196616 | tf_op jit(solution)/shard_map/ppermute | solution.py:297
  42.5 4.4 %collective-permute-start.7 = (f16[144,256]{1,0:T(8,128)(2,1)S(1)}, f16[144,256]{1,0:T(8,128)(2,1)S(1)}, u32[]{:S(2)}, u32[]{:S(2)}) collective-permute-start(f16[144,256]{1,0:T(8,128)(2,1)S(1)} %convert_element_type.39), channel_id=1, source_target_pairs={{0,4},{4,0},{8,12},{12,8},{16,20},{20,16},{24,28},{28,24},{1,5},{5... | collective-permute-start | bytes 221192 | tf_op jit(solution)/shard_map/ppermute | solution.py:297
  42.8 6.8 %collective-permute-start.12 = (f16[256,256]{1,0:T(8,128)(2,1)S(1)}, f16[256,256]{1,0:T(8,128)(2,1)S(1)}, u32[]{:S(2)}, u32[]{:S(2)}) collective-permute-start(f16[256,256]{1,0:T(8,128)(2,1)S(1)} %convert_element_type.44), channel_id=1, source_target_pairs={{0,16},{4,20},{8,24},{12,28},{16,0},{20,4},{24,8},{28,12},{1,17},{... | collective-permute-start | bytes 393224 | tf_op jit(solution)/shard_map/ppermute | solution.py:297
  46.9 1.2 %collective-permute-start.10 = (f32[16,128]{1,0:T(8,128)S(1)}, f32[16,128]{1,0:T(8,128)S(1)}, u32[]{:S(2)}, u32[]{:S(2)}) collective-permute-start(f32[16,128]{1,0:T(8,128)S(1)} %fusion.2), channel_id=1, source_target_pairs={{0,1},{1,0},{2,3},{3,2},{4,5},{5,4},{6,7},{7,6},{8,9},{9,8},{10,11... | collective-permute-start | bytes 24584 | tf_op jit(solution)/shard_map/ppermute | solution.py:418
  48.1 3.7 %collective-permute-start.11 = (f32[16,128]{1,0:T(8,128)S(1)}, f32[16,128]{1,0:T(8,128)S(1)}, u32[]{:S(2)}, u32[]{:S(2)}) collective-permute-start(f32[16,128]{1,0:T(8,128)S(1)} %add.44), channel_id=1, source_target_pairs={{0,2},{1,3},{2,0},{3,1},{4,6},{5,7},{6,4},{7,5},{8,10},{9,11},{10,... | collective-permute-start | bytes 24584 | tf_op jit(solution)/shard_map/ppermute | solution.py:418

commit v10 on v9

--- a/solution.py
+++ b/solution.py
@@ -263,8 +263,9 @@
                 ref[part:, LANES:] = low.astype(F32)
 
 
-def close_kernel(mix_scale, loss_scale, total, grad_mix, head_loss):
+def close_kernel(mix_scale, loss_scale, mine, other, grad_mix, head_loss):
     heads = grad_mix.shape[1]
+    total = mine[...] + other[...]
     grad_mix[...] = total[:HEADS_S, :heads] * mix_scale
     head_loss[...] = total[HEADS_S : HEADS_S + 1, :heads] * loss_scale
 
@@ -411,7 +412,7 @@
     ]
     grad_query = (sum(for_query[1:], for_query[0]) * (1.0 / room_query))[None]
     grad_key = (sum(for_key[1:], for_key[0]) * (1.0 / room_key))[None]
-    last = total
+    last = jnp.zeros_like(total)
     if copies > 1 and copies & (copies - 1) == 0:
         for bit in range(copies.bit_length() - 1):
             total = total if bit == 0 else total + last
@@ -422,13 +423,12 @@
             jnp.zeros_like(total),
         )
     last, grad_query, grad_key = lax.optimization_barrier((last, grad_query, grad_key))
-    total = total + last
     samples = copies * teacher_query.shape[0] * shard_rows * length
     grad_mix, head_loss = small(
         functools.partial(close_kernel, HD_S ** (-0.5) * weight / samples, 1.0 / samples),
         out_shape=(jax.ShapeDtypeStruct((HEADS_S, heads), F32), jax.ShapeDtypeStruct((1, heads), F32)),
         name="close",
-    )(total)
+    )(total, last)
     return (grad_query, grad_key, grad_mix.T, head_loss[0])
 
 

time: 52.6 us -> 52.6 us (level)
  no operation moved by 1% of the time
where the time goes in v10:
time: 52.6 us; the launch traced here: 52.4 us
  starting transfers between devices  20.3 us (39%)
  waiting for transfers between devices  19.2 us (37%)
  Pallas kernels  9.78 us (19%)
  local copies, waits for them, and re-layouts  1.45 us (3%)
  other arithmetic  0.84 us (2%)
  between operations  0.73 us (1%)
    ppermute x6, waiting for transfers between devices, fetch(): lax.ppermute(value, 'seq', [(target(i, step), i) for i in range(length)])  14.1 us
    ppermute x5, starting transfers between devices, deliver(): return lax.ppermute(value, ('head', 'seq'), pairs)  7.82 us
    ppermute x6, starting transfers between devices, fetch(): lax.ppermute(value, 'seq', [(target(i, step), i) for i in range(length)])  7.57 us
    ppermute x2, starting transfers between devices, fetch_student(): return [value] + [lax.ppermute(value, 'head', pairs) for pairs in turns]  3.4 us
    pallas_call x1, Pallas kernels, body(): pl.pallas_call(functools.partial(back_kernel, row_parts, key_parts, shard...  3.04 us
    ppermute x2, waiting for transfers between devices, body(): last = lax.ppermute(total, 'dp', [(i, i ^ 1 << bit) for i in range(copies)])  2.54 us
    ppermute x5, waiting for transfers between devices, deliver(): return lax.ppermute(value, ('head', 'seq'), pairs)  2.47 us
    pallas_call x1, Pallas kernels, body(): pl.pallas_call(functools.partial(student_kernel, (len(key_s), len(query_s...  2.31 us
  transfers between devices with their start and end apart: 15, of which 8 were waited for; matrix products, arithmetic and copies ran while one was open for 3% of the time, Pallas kernels for 8%

profile of v10, /device:TPU:0, one launch (start us, length us, event | category | flops | bytes accessed | tf_op | source)
XLA Modules:
  0.0 52.4 jit_solution(5340210288040176697)
XLA Ops:
  0.6 0.9 %share.1 = (bf16[1,64,512]{2,1,0:T(8,128)(2,1)S(1)}, bf16[1,64,512]{2,1,0:T(8,128)(2,1)S(1)}) custom-call(bf16[1,128,512]{2,1,0:T(8,128)(2,1)} %refs_0_.3, bf16[1,128,512]{2,1,0:T(8,128)(2,1)} %refs_1_.3), custom_call_target="tpu_custom_call" | custom-call | tf_op jit(solution)/shard_map/share/pallas_call | solution.py:304
  1.5 4.1 %collective-permute-start = (bf16[1,64,512]{2,1,0:T(8,128)(2,1)S(1)}, bf16[1,64,512]{2,1,0:T(8,128)(2,1)S(1)}, u32[]{:S(2)}, u32[]{:S(2)}) collective-permute-start(bf16[1,64,512]{2,1,0:T(8,128)(2,1)S(1)} %get-tuple-element.43), channel_id=1, source_target_pairs={{8,0},{12,4},{0,8},{4,12},{9,1},{13,5},{1,9},{5,13},{10,2},{14,6},... | collective-permute-start | bytes 196616 | tf_op jit(solution)/shard_map/ppermute | solution.py:290
  5.6 1.6 %collective-permute-start.2 = (bf16[1,64,512]{2,1,0:T(8,128)(2,1)S(1)}, bf16[1,64,512]{2,1,0:T(8,128)(2,1)S(1)}, u32[]{:S(2)}, u32[]{:S(2)}) collective-permute-start(bf16[1,64,512]{2,1,0:T(8,128)(2,1)S(1)} %get-tuple-element.45), channel_id=1, source_target_pairs={{4,0},{0,4},{12,8},{8,12},{5,1},{1,5},{13,9},{9,13},{6,2},{2,6},{1... | collective-permute-start | bytes 196616 | tf_op jit(solution)/shard_map/ppermute | solution.py:290
  7.7 0.9 %collective-permute-done.refs_1_ = bf16[1,64,512]{2,1,0:T(8,128)(2,1)S(1)} collective-permute-done((bf16[1,64,512]{2,1,0:T(8,128)(2,1)S(1)}, bf16[1,64,512]{2,1,0:T(8,128)(2,1)S(1)}, u32[]{:S(2)}, u32[]{:S(2)}) %collective-permute-start) | collective-permute-done | bytes 65568 | tf_op jit(solution)/shard_map/ppermute | solution.py:290
  8.7 1.9 %collective-permute-start.1 = (bf16[1,64,512]{2,1,0:T(8,128)(2,1)S(1)}, bf16[1,64,512]{2,1,0:T(8,128)(2,1)S(1)}, u32[]{:S(2)}, u32[]{:S(2)}) collective-permute-start(bf16[1,64,512]{2,1,0:T(8,128)(2,1)S(1)} %collective-permute-done.refs_1_), channel_id=1, source_target_pairs={{0,16},{16,0},{1,17},{17,1},{2,18},{18,2},{3,19},{19,3},{4,20},{20... | collective-permute-start | bytes 196616 | tf_op jit(solution)/shard_map/ppermute | solution.py:316
  10.6 7.2 %collective-permute-done.2.refs_4_ = bf16[1,64,512]{2,1,0:T(8,128)(2,1)S(1)} collective-permute-done((bf16[1,64,512]{2,1,0:T(8,128)(2,1)S(1)}, bf16[1,64,512]{2,1,0:T(8,128)(2,1)S(1)}, u32[]{:S(2)}, u32[]{:S(2)}) %collective-permute-start.2) | collective-permute-done | bytes 65568 | tf_op jit(solution)/shard_map/ppermute | solution.py:290
  17.7 1.5 %collective-permute-start.3 = (bf16[1,64,512]{2,1,0:T(8,128)(2,1)S(1)}, bf16[1,64,512]{2,1,0:T(8,128)(2,1)S(1)}, u32[]{:S(2)}, u32[]{:S(2)}) collective-permute-start(bf16[1,64,512]{2,1,0:T(8,128)(2,1)S(1)} %collective-permute-done.2.refs_4_), channel_id=1, source_target_pairs={{0,16},{16,0},{1,17},{17,1},{2,18},{18,2},{3,19},{19,3},{4,20},{20... | collective-permute-start | bytes 196616 | tf_op jit(solution)/shard_map/ppermute | solution.py:316
  19.2 0.8 %copy.9.mix_ref = f32[12,8]{1,0:T(8,128)S(1)} copy(f32[12,8]{0,1:T(8,128)} %param.9) | data formatting | bytes 768 | tf_op args[4]
  20.7 1.2 %prepare.1 = (bf16[1,128,1536]{2,1,0:T(8,128)(2,1)S(1)}, bf16[1,128,1536]{2,1,0:T(8,128)(2,1)S(1)}, bf16[1,128,512]{2,1,0:T(8,128)(2,1)S(1)}, bf16[1,128,512]{2,...) custom-call(f32[12,8]{1,0:T(8,128)S(1)} %copy.9.mix_ref, ...), custom_call_target="tpu_custom_call" | custom-call | tf_op jit(solution)/shard_map/prepare/pallas_call | solution.py:80
  22.0 2.3 %student.1 = (f32[12,256,256]{2,1,0:T(8,128)S(1)}, f32[12,256,256]{2,1,0:T(8,128)S(1)}, bf16[8,256,256]{2,1,0:T(8,128)(2,1)S(1)}, bf16[8,256,256]{2,1,0:T(8,128)...) custom-call(bf16[1,128,512]{2,1,0:T(8,128)(2,1)S(1)} %get-tuple-elem, ...), custom_call_target="tpu_custom_call" | custom-call | flops 3000000000 | bytes 1 | tf_op jit(solution)/shard_map/student/pallas_call | solution.py:328
  24.3 2.3 %collective-permute-done.5.refs_2_ = bf16[1,128,1536]{2,1,0:T(8,128)(2,1)S(1)} collective-permute-done((bf16[1,128,1536]{2,1,0:T(8,128)(2,1)}, bf16[1,128,1536]{2,1,0:T(8,128)(2,1)S(1)}, u32[]{:S(2)}, u32[]{:S(2)}) %collective-permute-start.5) | collective-permute-done | bytes 393248 | tf_op jit(solution)/shard_map/ppermute | solution.py:290
  26.6 0.8 %teacher.2 = (f32[12,128,256]{2,1,0:T(8,128)S(1)}, f32[12,256]{1,0:T(8,128)S(1)}, f32[12,256]{1,0:T(8,128)S(1)}, f32[2,12,256]{2,1,0:T(8,128)S(1)}) custom-call(bf16[1,128,1536]{2,1,0:T(8,128)(2,1)S(1)} %get-tuple-element.53.refs_0_, bf16[1,128,1536]{2,1,0:T(8,128)(2,1)S(1)} %get-tuple-element.50.refs_1_, ...), custom_call_target="tpu_custom_call" | custom-call | tf_op jit(solution)/shard_map/teacher/pallas_call | solution.py:338
  27.5 0.9 %teacher.3 = (f32[12,128,256]{2,1,0:T(8,128)S(1)}, f32[12,256]{1,0:T(8,128)S(1)}, f32[12,256]{1,0:T(8,128)S(1)}, f32[2,12,256]{2,1,0:T(8,128)S(1)}, f32[2,12,256]{2,1,0:T(8,128)S(1)}) custom-call(bf16[1,128,1536]{2,1,0:T(8,128)(2,1)S(1)} %collective-permute-done.4.refs_0_, bf16[1,128,1536]{2,1,0:T(8,128)(2,1)S(1)} %get-tuple-element.50.refs_1_, ...), custom_call_target="tpu_custom_call" | custom-call | tf_op jit(solution)/shard_map/teacher/pallas_call | solution.py:338
  28.7 3.7 %collective-permute-done.6.refs_3_ = f32[2,12,256]{2,1,0:T(8,128)S(1)} collective-permute-done((f32[2,12,256]{2,1,0:T(8,128)S(1)}, f32[2,12,256]{2,1,0:T(8,128)S(1)}, u32[]{:S(2)}, u32[]{:S(2)}) %collective-permute-start.6) | collective-permute-done | bytes 24608 | tf_op jit(solution)/shard_map/ppermute | solution.py:290
  32.4 3.0 %back.1 = (f32[16,128]{1,0:T(8,128)S(1)}, f32[256,256]{1,0:T(8,128)S(1)}, f32[144,256]{1,0:T(8,128)S(1)}, f32[144,256]{1,0:T(8,128)S(1)}, f32[256,256]{1,0:T(8,1...) custom-call(bf16[8,256,64]{2,1,0:T(8,128)(2,1)S(1)} %get-tuple-element.48.refs_0_, ...), custom_call_target="tpu_custom_call" | custom-call | tf_op jit(solution)/shard_map/back/pallas_call | solution.py:366
  35.4 1.6 %collective-permute-start.8 = (f16[144,256]{1,0:T(8,128)(2,1)S(1)}, f16[144,256]{1,0:T(8,128)(2,1)S(1)}, u32[]{:S(2)}, u32[]{:S(2)}) collective-permute-start(f16[144,256]{1,0:T(8,128)(2,1)S(1)} %convert_element_type.41), channel_id=1, source_target_pairs={{0,8},{4,12},{8,0},{12,4},{16,24},{20,28},{24,16},{28,20},{1,9},{5... | collective-permute-start | bytes 221192 | tf_op jit(solution)/shard_map/ppermute | solution.py:298
  37.1 1.1 %collective-permute-start.9 = (f32[16,128]{1,0:T(8,128)S(1)}, f32[16,128]{1,0:T(8,128)S(1)}, u32[]{:S(2)}, u32[]{:S(2)}) collective-permute-start(f32[16,128]{1,0:T(8,128)S(1)} %get-tuple-element.68), channel_id=1, source_target_pairs={{12,0},{8,4},{4,8},{0,12},{13,1},{9,5},{5,9},{1,13},{14,2},{10,6},... | collective-permute-start | bytes 24584 | tf_op jit(solution)/shard_map/ppermute | solution.py:290
  38.2 2.6 %collective-permute-start.14 = (f16[128,256]{1,0:T(8,128)(2,1)S(1)}, f16[128,256]{1,0:T(8,128)(2,1)S(1)}, u32[]{:S(2)}, u32[]{:S(2)}) collective-permute-start(f16[128,256]{1,0:T(8,128)(2,1)S(1)} %convert_element_type.50), channel_id=1, source_target_pairs={{0,24},{4,28},{8,16},{12,20},{16,8},{20,12},{24,0},{28,4},{1,25},{... | collective-permute-start | bytes 196616 | tf_op jit(solution)/shard_map/ppermute | solution.py:298
  40.8 1.7 %collective-permute-start.13 = (f16[128,256]{1,0:T(8,128)(2,1)S(1)}, f16[128,256]{1,0:T(8,128)(2,1)S(1)}, u32[]{:S(2)}, u32[]{:S(2)}) collective-permute-start(f16[128,256]{1,0:T(8,128)(2,1)S(1)} %convert_element_type.46), channel_id=1, source_target_pairs={{0,20},{4,16},{8,28},{12,24},{16,4},{20,0},{24,12},{28,8},{1,21},{... | collective-permute-start | bytes 196616 | tf_op jit(solution)/shard_map/ppermute | solution.py:298
  42.8 1.6 %collective-permute-start.12 = (f16[256,256]{1,0:T(8,128)(2,1)S(1)}, f16[256,256]{1,0:T(8,128)(2,1)S(1)}, u32[]{:S(2)}, u32[]{:S(2)}) collective-permute-start(f16[256,256]{1,0:T(8,128)(2,1)S(1)} %convert_element_type.44), channel_id=1, source_target_pairs={{0,16},{4,20},{8,24},{12,28},{16,0},{20,4},{24,8},{28,12},{1,17},{... | collective-permute-start | bytes 393224 | tf_op jit(solution)/shard_map/ppermute | solution.py:298
  44.4 2.5 %collective-permute-done.7 = f16[144,256]{1,0:T(8,128)(2,1)S(1)} collective-permute-done((f16[144,256]{1,0:T(8,128)(2,1)S(1)}, f16[144,256]{1,0:T(8,128)(2,1)S(1)}, u32[]{:S(2)}, u32[]{:S(2)}) %collective-permute-start.7) | collective-permute-done | bytes 73760 | tf_op jit(solution)/shard_map/ppermute | solution.py:298
  47.0 1.2 %collective-permute-done.10 = f32[16,128]{1,0:T(8,128)S(1)} collective-permute-done((f32[16,128]{1,0:T(8,128)S(1)}, f32[16,128]{1,0:T(8,128)S(1)}, u32[]{:S(2)}, u32[]{:S(2)}) %collective-permute-start.10) | collective-permute-done | bytes 8224 | tf_op jit(solution)/shard_map/ppermute | solution.py:419
  48.1 1.5 %collective-permute-start.11 = (f32[16,128]{1,0:T(8,128)S(1)}, f32[16,128]{1,0:T(8,128)S(1)}, u32[]{:S(2)}, u32[]{:S(2)}) collective-permute-start(f32[16,128]{1,0:T(8,128)S(1)} %add.41.mine), channel_id=1, source_target_pairs={{0,2},{1,3},{2,0},{3,1},{4,6},{5,7},{6,4},{7,5},{8,10},{9,11},{10,... | collective-permute-start | bytes 24584 | tf_op jit(solution)/shard_map/ppermute | solution.py:419
  50.4 1.4 %collective-permute-done.11.other = f32[16,128]{1,0:T(8,128)S(1)} collective-permute-done((f32[16,128]{1,0:T(8,128)S(1)}, f32[16,128]{1,0:T(8,128)S(1)}, u32[]{:S(2)}, u32[]{:S(2)}) %collective-permute-start.11) | collective-permute-done | bytes 8224 | tf_op jit(solution)/shard_map/ppermute | solution.py:419
  (26 shorter events, 3.4 us)
Async XLA Ops:
  1.5 7.2 %collective-permute-start = (bf16[1,64,512]{2,1,0:T(8,128)(2,1)S(1)}, bf16[1,64,512]{2,1,0:T(8,128)(2,1)S(1)}, u32[]{:S(2)}, u32[]{:S(2)}) collective-permute-start(bf16[1,64,512]{2,1,0:T(8,128)(2,1)S(1)} %get-tuple-element.43), channel_id=1, source_target_pairs={{8,0},{12,4},{0,8},{4,12},{9,1},{13,5},{1,9},{5,13},{10,2},{14,6},... | collective-permute-start | bytes 196616 | tf_op jit(solution)/shard_map/ppermute | solution.py:290
  5.6 12.1 %collective-permute-start.2 = (bf16[1,64,512]{2,1,0:T(8,128)(2,1)S(1)}, bf16[1,64,512]{2,1,0:T(8,128)(2,1)S(1)}, u32[]{:S(2)}, u32[]{:S(2)}) collective-permute-start(bf16[1,64,512]{2,1,0:T(8,128)(2,1)S(1)} %get-tuple-element.45), channel_id=1, source_target_pairs={{4,0},{0,4},{12,8},{8,12},{5,1},{1,5},{13,9},{9,13},{6,2},{2,6},{1... | collective-permute-start | bytes 196616 | tf_op jit(solution)/shard_map/ppermute | solution.py:290
  7.2 19.4 %collective-permute-start.5 = (bf16[1,128,1536]{2,1,0:T(8,128)(2,1)}, bf16[1,128,1536]{2,1,0:T(8,128)(2,1)S(1)}, u32[]{:S(2)}, u32[]{:S(2)}) collective-permute-start(bf16[1,128,1536]{2,1,0:T(8,128)(2,1)} %refs_1_.2), channel_id=1, source_target_pairs={{4,0},{0,4},{12,8},{8,12},{5,1},{1,5},{13,9},{9,13},{6,2},{2,6},{1... | collective-permute-start | bytes 1179656 | tf_op jit(solution)/shard_map/ppermute | solution.py:290
  7.7 19.8 %collective-permute-start.4 = (bf16[1,128,1536]{2,1,0:T(8,128)(2,1)}, bf16[1,128,1536]{2,1,0:T(8,128)(2,1)S(1)}, u32[]{:S(2)}, u32[]{:S(2)}) collective-permute-start(bf16[1,128,1536]{2,1,0:T(8,128)(2,1)} %refs_0_.2), channel_id=1, source_target_pairs={{8,0},{12,4},{0,8},{4,12},{9,1},{13,5},{1,9},{5,13},{10,2},{14,6},... | collective-permute-start | bytes 1179656 | tf_op jit(solution)/shard_map/ppermute | solution.py:290
  8.7 13.2 %collective-permute-start.1 = (bf16[1,64,512]{2,1,0:T(8,128)(2,1)S(1)}, bf16[1,64,512]{2,1,0:T(8,128)(2,1)S(1)}, u32[]{:S(2)}, u32[]{:S(2)}) collective-permute-start(bf16[1,64,512]{2,1,0:T(8,128)(2,1)S(1)} %collective-permute-done.refs_1_), channel_id=1, source_target_pairs={{0,16},{16,0},{1,17},{17,1},{2,18},{18,2},{3,19},{19,3},{4,20},{20... | collective-permute-start | bytes 196616 | tf_op jit(solution)/shard_map/ppermute | solution.py:316
  17.7 4.3 %collective-permute-start.3 = (bf16[1,64,512]{2,1,0:T(8,128)(2,1)S(1)}, bf16[1,64,512]{2,1,0:T(8,128)(2,1)S(1)}, u32[]{:S(2)}, u32[]{:S(2)}) collective-permute-start(bf16[1,64,512]{2,1,0:T(8,128)(2,1)S(1)} %collective-permute-done.2.refs_4_), channel_id=1, source_target_pairs={{0,16},{16,0},{1,17},{17,1},{2,18},{18,2},{3,19},{19,3},{4,20},{20... | collective-permute-start | bytes 196616 | tf_op jit(solution)/shard_map/ppermute | solution.py:316
  20.0 0.7 %copy-start = (f32[12,8]{0,1:T(8,128)S(1)}, f32[12,8]{0,1:T(8,128)}, u32[]{:S(2)}) copy-start(f32[12,8]{0,1:T(8,128)} %param.9) | copy-start | bytes 1156
  28.4 4.0 %collective-permute-start.6 = (f32[2,12,256]{2,1,0:T(8,128)S(1)}, f32[2,12,256]{2,1,0:T(8,128)S(1)}, u32[]{:S(2)}, u32[]{:S(2)}) collective-permute-start(f32[2,12,256]{2,1,0:T(8,128)S(1)} %get-tuple-element.56), channel_id=1, source_target_pairs={{4,0},{0,4},{12,8},{8,12},{5,1},{1,5},{13,9},{9,13},{6,2},{2,6},{1... | collective-permute-start | bytes 73736 | tf_op jit(solution)/shard_map/ppermute | solution.py:290
  35.4 7.4 %collective-permute-start.8 = (f16[144,256]{1,0:T(8,128)(2,1)S(1)}, f16[144,256]{1,0:T(8,128)(2,1)S(1)}, u32[]{:S(2)}, u32[]{:S(2)}) collective-permute-start(f16[144,256]{1,0:T(8,128)(2,1)S(1)} %convert_element_type.41), channel_id=1, source_target_pairs={{0,8},{4,12},{8,0},{12,4},{16,24},{20,28},{24,16},{28,20},{1,9},{5... | collective-permute-start | bytes 221192 | tf_op jit(solution)/shard_map/ppermute | solution.py:298
  37.1 9.8 %collective-permute-start.9 = (f32[16,128]{1,0:T(8,128)S(1)}, f32[16,128]{1,0:T(8,128)S(1)}, u32[]{:S(2)}, u32[]{:S(2)}) collective-permute-start(f32[16,128]{1,0:T(8,128)S(1)} %get-tuple-element.68), channel_id=1, source_target_pairs={{12,0},{8,4},{4,8},{0,12},{13,1},{9,5},{5,9},{1,13},{14,2},{10,6},... | collective-permute-start | bytes 24584 | tf_op jit(solution)/shard_map/ppermute | solution.py:290
  38.2 11.4 %collective-permute-start.14 = (f16[128,256]{1,0:T(8,128)(2,1)S(1)}, f16[128,256]{1,0:T(8,128)(2,1)S(1)}, u32[]{:S(2)}, u32[]{:S(2)}) collective-permute-start(f16[128,256]{1,0:T(8,128)(2,1)S(1)} %convert_element_type.50), channel_id=1, source_target_pairs={{0,24},{4,28},{8,16},{12,20},{16,8},{20,12},{24,0},{28,4},{1,25},{... | collective-permute-start | bytes 196616 | tf_op jit(solution)/shard_map/ppermute | solution.py:298
  40.8 8.8 %collective-permute-start.13 = (f16[128,256]{1,0:T(8,128)(2,1)S(1)}, f16[128,256]{1,0:T(8,128)(2,1)S(1)}, u32[]{:S(2)}, u32[]{:S(2)}) collective-permute-start(f16[128,256]{1,0:T(8,128)(2,1)S(1)} %convert_element_type.46), channel_id=1, source_target_pairs={{0,20},{4,16},{8,28},{12,24},{16,4},{20,0},{24,12},{28,8},{1,21},{... | collective-permute-start | bytes 196616 | tf_op jit(solution)/shard_map/ppermute | solution.py:298
  42.5 4.4 %collective-permute-start.7 = (f16[144,256]{1,0:T(8,128)(2,1)S(1)}, f16[144,256]{1,0:T(8,128)(2,1)S(1)}, u32[]{:S(2)}, u32[]{:S(2)}) collective-permute-start(f16[144,256]{1,0:T(8,128)(2,1)S(1)} %convert_element_type.39), channel_id=1, source_target_pairs={{0,4},{4,0},{8,12},{12,8},{16,20},{20,16},{24,28},{28,24},{1,5},{5... | collective-permute-start | bytes 221192 | tf_op jit(solution)/shard_map/ppermute | solution.py:298
  42.8 6.8 %collective-permute-start.12 = (f16[256,256]{1,0:T(8,128)(2,1)S(1)}, f16[256,256]{1,0:T(8,128)(2,1)S(1)}, u32[]{:S(2)}, u32[]{:S(2)}) collective-permute-start(f16[256,256]{1,0:T(8,128)(2,1)S(1)} %convert_element_type.44), channel_id=1, source_target_pairs={{0,16},{4,20},{8,24},{12,28},{16,0},{20,4},{24,8},{28,12},{1,17},{... | collective-permute-start | bytes 393224 | tf_op jit(solution)/shard_map/ppermute | solution.py:298
  46.9 1.2 %collective-permute-start.10 = (f32[16,128]{1,0:T(8,128)S(1)}, f32[16,128]{1,0:T(8,128)S(1)}, u32[]{:S(2)}, u32[]{:S(2)}) collective-permute-start(f32[16,128]{1,0:T(8,128)S(1)} %fusion.2), channel_id=1, source_target_pairs={{0,1},{1,0},{2,3},{3,2},{4,5},{5,4},{6,7},{7,6},{8,9},{9,8},{10,11... | collective-permute-start | bytes 24584 | tf_op jit(solution)/shard_map/ppermute | solution.py:419
  48.1 3.7 %collective-permute-start.11 = (f32[16,128]{1,0:T(8,128)S(1)}, f32[16,128]{1,0:T(8,128)S(1)}, u32[]{:S(2)}, u32[]{:S(2)}) collective-permute-start(f32[16,128]{1,0:T(8,128)S(1)} %add.41.mine), channel_id=1, source_target_pairs={{0,2},{1,3},{2,0},{3,1},{4,6},{5,7},{6,4},{7,5},{8,10},{9,11},{10,... | collective-permute-start | bytes 24584 | tf_op jit(solution)/shard_map/ppermute | solution.py:419

commit v11 on v10

--- a/solution.py
+++ b/solution.py
@@ -422,7 +422,7 @@
             [lax.ppermute(total, "dp", [(i, (i + step) % copies) for i in range(copies)]) for step in range(1, copies)],
             jnp.zeros_like(total),
         )
-    last, grad_query, grad_key = lax.optimization_barrier((last, grad_query, grad_key))
+    last, grad_key, grad_query = lax.optimization_barrier((last, grad_key, grad_query))
     samples = copies * teacher_query.shape[0] * shard_rows * length
     grad_mix, head_loss = small(
         functools.partial(close_kernel, HD_S ** (-0.5) * weight / samples, 1.0 / samples),

time: 52.6 us -> 52.6 us (level)
  no operation moved by 1% of the time
where the time goes in v11:
time: 52.6 us; the launch traced here: 52.4 us
  starting transfers between devices  20.3 us (39%)
  waiting for transfers between devices  19.2 us (37%)
  Pallas kernels  9.78 us (19%)
  local copies, waits for them, and re-layouts  1.45 us (3%)
  other arithmetic  0.85 us (2%)
  between operations  0.73 us (1%)
    ppermute x6, waiting for transfers between devices, fetch(): lax.ppermute(value, 'seq', [(target(i, step), i) for i in range(length)])  14.1 us
    ppermute x5, starting transfers between devices, deliver(): return lax.ppermute(value, ('head', 'seq'), pairs)  7.82 us
    ppermute x6, starting transfers between devices, fetch(): lax.ppermute(value, 'seq', [(target(i, step), i) for i in range(length)])  7.57 us
    ppermute x2, starting transfers between devices, fetch_student(): return [value] + [lax.ppermute(value, 'head', pairs) for pairs in turns]  3.4 us
    pallas_call x1, Pallas kernels, body(): pl.pallas_call(functools.partial(back_kernel, row_parts, key_parts, shard...  3.04 us
    ppermute x2, waiting for transfers between devices, body(): last = lax.ppermute(total, 'dp', [(i, i ^ 1 << bit) for i in range(copies)])  2.54 us
    ppermute x5, waiting for transfers between devices, deliver(): return lax.ppermute(value, ('head', 'seq'), pairs)  2.47 us
    pallas_call x1, Pallas kernels, body(): pl.pallas_call(functools.partial(student_kernel, (len(key_s), len(query_s...  2.31 us
  transfers between devices with their start and end apart: 15, of which 8 were waited for; matrix products, arithmetic and copies ran while one was open for 3% of the time, Pallas kernels for 8%

profile of v11, /device:TPU:0, one launch (start us, length us, event | category | flops | bytes accessed | tf_op | source)
XLA Modules:
  0.0 52.4 jit_solution(17628612277193326308)
XLA Ops:
  0.6 0.9 %share.1 = (bf16[1,64,512]{2,1,0:T(8,128)(2,1)S(1)}, bf16[1,64,512]{2,1,0:T(8,128)(2,1)S(1)}) custom-call(bf16[1,128,512]{2,1,0:T(8,128)(2,1)} %refs_0_.3, bf16[1,128,512]{2,1,0:T(8,128)(2,1)} %refs_1_.3), custom_call_target="tpu_custom_call" | custom-call | tf_op jit(solution)/shard_map/share/pallas_call | solution.py:304
  1.5 4.1 %collective-permute-start = (bf16[1,64,512]{2,1,0:T(8,128)(2,1)S(1)}, bf16[1,64,512]{2,1,0:T(8,128)(2,1)S(1)}, u32[]{:S(2)}, u32[]{:S(2)}) collective-permute-start(bf16[1,64,512]{2,1,0:T(8,128)(2,1)S(1)} %get-tuple-element.43), channel_id=1, source_target_pairs={{8,0},{12,4},{0,8},{4,12},{9,1},{13,5},{1,9},{5,13},{10,2},{14,6},... | collective-permute-start | bytes 196616 | tf_op jit(solution)/shard_map/ppermute | solution.py:290
  5.6 1.6 %collective-permute-start.2 = (bf16[1,64,512]{2,1,0:T(8,128)(2,1)S(1)}, bf16[1,64,512]{2,1,0:T(8,128)(2,1)S(1)}, u32[]{:S(2)}, u32[]{:S(2)}) collective-permute-start(bf16[1,64,512]{2,1,0:T(8,128)(2,1)S(1)} %get-tuple-element.45), channel_id=1, source_target_pairs={{4,0},{0,4},{12,8},{8,12},{5,1},{1,5},{13,9},{9,13},{6,2},{2,6},{1... | collective-permute-start | bytes 196616 | tf_op jit(solution)/shard_map/ppermute | solution.py:290
  7.7 0.9 %collective-permute-done.refs_1_ = bf16[1,64,512]{2,1,0:T(8,128)(2,1)S(1)} collective-permute-done((bf16[1,64,512]{2,1,0:T(8,128)(2,1)S(1)}, bf16[1,64,512]{2,1,0:T(8,128)(2,1)S(1)}, u32[]{:S(2)}, u32[]{:S(2)}) %collective-permute-start) | collective-permute-done | bytes 65568 | tf_op jit(solution)/shard_map/ppermute | solution.py:290
  8.7 1.9 %collective-permute-start.1 = (bf16[1,64,512]{2,1,0:T(8,128)(2,1)S(1)}, bf16[1,64,512]{2,1,0:T(8,128)(2,1)S(1)}, u32[]{:S(2)}, u32[]{:S(2)}) collective-permute-start(bf16[1,64,512]{2,1,0:T(8,128)(2,1)S(1)} %collective-permute-done.refs_1_), channel_id=1, source_target_pairs={{0,16},{16,0},{1,17},{17,1},{2,18},{18,2},{3,19},{19,3},{4,20},{20... | collective-permute-start | bytes 196616 | tf_op jit(solution)/shard_map/ppermute | solution.py:316
  10.6 7.2 %collective-permute-done.2.refs_4_ = bf16[1,64,512]{2,1,0:T(8,128)(2,1)S(1)} collective-permute-done((bf16[1,64,512]{2,1,0:T(8,128)(2,1)S(1)}, bf16[1,64,512]{2,1,0:T(8,128)(2,1)S(1)}, u32[]{:S(2)}, u32[]{:S(2)}) %collective-permute-start.2) | collective-permute-done | bytes 65568 | tf_op jit(solution)/shard_map/ppermute | solution.py:290
  17.7 1.5 %collective-permute-start.3 = (bf16[1,64,512]{2,1,0:T(8,128)(2,1)S(1)}, bf16[1,64,512]{2,1,0:T(8,128)(2,1)S(1)}, u32[]{:S(2)}, u32[]{:S(2)}) collective-permute-start(bf16[1,64,512]{2,1,0:T(8,128)(2,1)S(1)} %collective-permute-done.2.refs_4_), channel_id=1, source_target_pairs={{0,16},{16,0},{1,17},{17,1},{2,18},{18,2},{3,19},{19,3},{4,20},{20... | collective-permute-start | bytes 196616 | tf_op jit(solution)/shard_map/ppermute | solution.py:316
  20.7 1.2 %prepare.1 = (bf16[1,128,1536]{2,1,0:T(8,128)(2,1)S(1)}, bf16[1,128,1536]{2,1,0:T(8,128)(2,1)S(1)}, bf16[1,128,512]{2,1,0:T(8,128)(2,1)S(1)}, bf16[1,128,512]{2,...) custom-call(f32[12,8]{1,0:T(8,128)S(1)} %copy.9.mix_ref, ...), custom_call_target="tpu_custom_call" | custom-call | tf_op jit(solution)/shard_map/prepare/pallas_call | solution.py:80
  22.0 2.3 %student.1 = (f32[12,256,256]{2,1,0:T(8,128)S(1)}, f32[12,256,256]{2,1,0:T(8,128)S(1)}, bf16[8,256,256]{2,1,0:T(8,128)(2,1)S(1)}, bf16[8,256,256]{2,1,0:T(8,128)...) custom-call(bf16[1,128,512]{2,1,0:T(8,128)(2,1)S(1)} %get-tuple-elem, ...), custom_call_target="tpu_custom_call" | custom-call | flops 3000000000 | bytes 1 | tf_op jit(solution)/shard_map/student/pallas_call | solution.py:328
  24.3 2.3 %collective-permute-done.5.refs_2_ = bf16[1,128,1536]{2,1,0:T(8,128)(2,1)S(1)} collective-permute-done((bf16[1,128,1536]{2,1,0:T(8,128)(2,1)}, bf16[1,128,1536]{2,1,0:T(8,128)(2,1)S(1)}, u32[]{:S(2)}, u32[]{:S(2)}) %collective-permute-start.5) | collective-permute-done | bytes 393248 | tf_op jit(solution)/shard_map/ppermute | solution.py:290
  26.6 0.8 %teacher.2 = (f32[12,128,256]{2,1,0:T(8,128)S(1)}, f32[12,256]{1,0:T(8,128)S(1)}, f32[12,256]{1,0:T(8,128)S(1)}, f32[2,12,256]{2,1,0:T(8,128)S(1)}) custom-call(bf16[1,128,1536]{2,1,0:T(8,128)(2,1)S(1)} %get-tuple-element.53.refs_0_, bf16[1,128,1536]{2,1,0:T(8,128)(2,1)S(1)} %get-tuple-element.50.refs_1_, ...), custom_call_target="tpu_custom_call" | custom-call | tf_op jit(solution)/shard_map/teacher/pallas_call | solution.py:338
  27.5 0.9 %teacher.3 = (f32[12,128,256]{2,1,0:T(8,128)S(1)}, f32[12,256]{1,0:T(8,128)S(1)}, f32[12,256]{1,0:T(8,128)S(1)}, f32[2,12,256]{2,1,0:T(8,128)S(1)}, f32[2,12,256]{2,1,0:T(8,128)S(1)}) custom-call(bf16[1,128,1536]{2,1,0:T(8,128)(2,1)S(1)} %collective-permute-done.4.refs_0_, bf16[1,128,1536]{2,1,0:T(8,128)(2,1)S(1)} %get-tuple-element.50.refs_1_, ...), custom_call_target="tpu_custom_call" | custom-call | tf_op jit(solution)/shard_map/teacher/pallas_call | solution.py:338
  28.7 3.7 %collective-permute-done.6.refs_3_ = f32[2,12,256]{2,1,0:T(8,128)S(1)} collective-permute-done((f32[2,12,256]{2,1,0:T(8,128)S(1)}, f32[2,12,256]{2,1,0:T(8,128)S(1)}, u32[]{:S(2)}, u32[]{:S(2)}) %collective-permute-start.6) | collective-permute-done | bytes 24608 | tf_op jit(solution)/shard_map/ppermute | solution.py:290
  32.4 3.0 %back.1 = (f32[16,128]{1,0:T(8,128)S(1)}, f32[256,256]{1,0:T(8,128)S(1)}, f32[144,256]{1,0:T(8,128)S(1)}, f32[144,256]{1,0:T(8,128)S(1)}, f32[256,256]{1,0:T(8,1...) custom-call(bf16[8,256,64]{2,1,0:T(8,128)(2,1)S(1)} %get-tuple-element.48.refs_0_, ...), custom_call_target="tpu_custom_call" | custom-call | tf_op jit(solution)/shard_map/back/pallas_call | solution.py:366
  35.4 1.6 %collective-permute-start.8 = (f16[144,256]{1,0:T(8,128)(2,1)S(1)}, f16[144,256]{1,0:T(8,128)(2,1)S(1)}, u32[]{:S(2)}, u32[]{:S(2)}) collective-permute-start(f16[144,256]{1,0:T(8,128)(2,1)S(1)} %convert_element_type.41), channel_id=1, source_target_pairs={{0,8},{4,12},{8,0},{12,4},{16,24},{20,28},{24,16},{28,20},{1,9},{5... | collective-permute-start | bytes 221192 | tf_op jit(solution)/shard_map/ppermute | solution.py:298
  37.1 1.1 %collective-permute-start.9 = (f32[16,128]{1,0:T(8,128)S(1)}, f32[16,128]{1,0:T(8,128)S(1)}, u32[]{:S(2)}, u32[]{:S(2)}) collective-permute-start(f32[16,128]{1,0:T(8,128)S(1)} %get-tuple-element.68), channel_id=1, source_target_pairs={{12,0},{8,4},{4,8},{0,12},{13,1},{9,5},{5,9},{1,13},{14,2},{10,6},... | collective-permute-start | bytes 24584 | tf_op jit(solution)/shard_map/ppermute | solution.py:290
  38.2 1.9 %collective-permute-start.14 = (f16[128,256]{1,0:T(8,128)(2,1)S(1)}, f16[128,256]{1,0:T(8,128)(2,1)S(1)}, u32[]{:S(2)}, u32[]{:S(2)}) collective-permute-start(f16[128,256]{1,0:T(8,128)(2,1)S(1)} %convert_element_type.50), channel_id=1, source_target_pairs={{0,20},{4,16},{8,28},{12,24},{16,4},{20,0},{24,12},{28,8},{1,21},{... | collective-permute-start | bytes 196616 | tf_op jit(solution)/shard_map/ppermute | solution.py:298
  40.1 2.4 %collective-permute-start.13 = (f16[128,256]{1,0:T(8,128)(2,1)S(1)}, f16[128,256]{1,0:T(8,128)(2,1)S(1)}, u32[]{:S(2)}, u32[]{:S(2)}) collective-permute-start(f16[128,256]{1,0:T(8,128)(2,1)S(1)} %convert_element_type.46), channel_id=1, source_target_pairs={{0,24},{4,28},{8,16},{12,20},{16,8},{20,12},{24,0},{28,4},{1,25},{... | collective-permute-start | bytes 196616 | tf_op jit(solution)/shard_map/ppermute | solution.py:298
  42.8 1.6 %collective-permute-start.12 = (f16[256,256]{1,0:T(8,128)(2,1)S(1)}, f16[256,256]{1,0:T(8,128)(2,1)S(1)}, u32[]{:S(2)}, u32[]{:S(2)}) collective-permute-start(f16[256,256]{1,0:T(8,128)(2,1)S(1)} %convert_element_type.44), channel_id=1, source_target_pairs={{0,16},{4,20},{8,24},{12,28},{16,0},{20,4},{24,8},{28,12},{1,17},{... | collective-permute-start | bytes 393224 | tf_op jit(solution)/shard_map/ppermute | solution.py:298
  44.4 2.5 %collective-permute-done.7 = f16[144,256]{1,0:T(8,128)(2,1)S(1)} collective-permute-done((f16[144,256]{1,0:T(8,128)(2,1)S(1)}, f16[144,256]{1,0:T(8,128)(2,1)S(1)}, u32[]{:S(2)}, u32[]{:S(2)}) %collective-permute-start.7) | collective-permute-done | bytes 73760 | tf_op jit(solution)/shard_map/ppermute | solution.py:298
  47.0 1.2 %collective-permute-done.10 = f32[16,128]{1,0:T(8,128)S(1)} collective-permute-done((f32[16,128]{1,0:T(8,128)S(1)}, f32[16,128]{1,0:T(8,128)S(1)}, u32[]{:S(2)}, u32[]{:S(2)}) %collective-permute-start.10) | collective-permute-done | bytes 8224 | tf_op jit(solution)/shard_map/ppermute | solution.py:419
  48.1 1.5 %collective-permute-start.11 = (f32[16,128]{1,0:T(8,128)S(1)}, f32[16,128]{1,0:T(8,128)S(1)}, u32[]{:S(2)}, u32[]{:S(2)}) collective-permute-start(f32[16,128]{1,0:T(8,128)S(1)} %add.41.mine), channel_id=1, source_target_pairs={{0,2},{1,3},{2,0},{3,1},{4,6},{5,7},{6,4},{7,5},{8,10},{9,11},{10,... | collective-permute-start | bytes 24584 | tf_op jit(solution)/shard_map/ppermute | solution.py:419
  49.6 0.8 %multiply_bitcast_fusion = (f32[1,128,256]{2,1,0:T(8,128)}, f32[1,128,256]{2,1,0:T(8,128)}) fusion(f16[128,256]{1,0:T(8,128)(2,1)S(1)} %collective-permute-done.14, f32[256,256]{1,0:T(8,128)S(1)} %get-tuple-element.71, f16[256,256]{1,0:T(8,128)(2,1)S(1)} %collective-permute-done.12, f16[144,256]{1,0:T(8,128)(2,1)S(1)} %collective-permute-done.7, ...), kind=kLoop, calls=%fused_computation | loop fusion | flops 458752 | bytes 917504 | tf_op jit(solution)/shard_map/broadcast_in_dim | solution.py:413
  50.4 1.4 %collective-permute-done.11.other = f32[16,128]{1,0:T(8,128)S(1)} collective-permute-done((f32[16,128]{1,0:T(8,128)S(1)}, f32[16,128]{1,0:T(8,128)S(1)}, u32[]{:S(2)}, u32[]{:S(2)}) %collective-permute-start.11) | collective-permute-done | bytes 8224 | tf_op jit(solution)/shard_map/ppermute | solution.py:419
  (26 shorter events, 3.4 us)
Async XLA Ops:
  1.5 7.2 %collective-permute-start = (bf16[1,64,512]{2,1,0:T(8,128)(2,1)S(1)}, bf16[1,64,512]{2,1,0:T(8,128)(2,1)S(1)}, u32[]{:S(2)}, u32[]{:S(2)}) collective-permute-start(bf16[1,64,512]{2,1,0:T(8,128)(2,1)S(1)} %get-tuple-element.43), channel_id=1, source_target_pairs={{8,0},{12,4},{0,8},{4,12},{9,1},{13,5},{1,9},{5,13},{10,2},{14,6},... | collective-permute-start | bytes 196616 | tf_op jit(solution)/shard_map/ppermute | solution.py:290
  5.6 12.1 %collective-permute-start.2 = (bf16[1,64,512]{2,1,0:T(8,128)(2,1)S(1)}, bf16[1,64,512]{2,1,0:T(8,128)(2,1)S(1)}, u32[]{:S(2)}, u32[]{:S(2)}) collective-permute-start(bf16[1,64,512]{2,1,0:T(8,128)(2,1)S(1)} %get-tuple-element.45), channel_id=1, source_target_pairs={{4,0},{0,4},{12,8},{8,12},{5,1},{1,5},{13,9},{9,13},{6,2},{2,6},{1... | collective-permute-start | bytes 196616 | tf_op jit(solution)/shard_map/ppermute | solution.py:290
  7.2 19.4 %collective-permute-start.5 = (bf16[1,128,1536]{2,1,0:T(8,128)(2,1)}, bf16[1,128,1536]{2,1,0:T(8,128)(2,1)S(1)}, u32[]{:S(2)}, u32[]{:S(2)}) collective-permute-start(bf16[1,128,1536]{2,1,0:T(8,128)(2,1)} %refs_1_.2), channel_id=1, source_target_pairs={{4,0},{0,4},{12,8},{8,12},{5,1},{1,5},{13,9},{9,13},{6,2},{2,6},{1... | collective-permute-start | bytes 1179656 | tf_op jit(solution)/shard_map/ppermute | solution.py:290
  7.7 19.8 %collective-permute-start.4 = (bf16[1,128,1536]{2,1,0:T(8,128)(2,1)}, bf16[1,128,1536]{2,1,0:T(8,128)(2,1)S(1)}, u32[]{:S(2)}, u32[]{:S(2)}) collective-permute-start(bf16[1,128,1536]{2,1,0:T(8,128)(2,1)} %refs_0_.2), channel_id=1, source_target_pairs={{8,0},{12,4},{0,8},{4,12},{9,1},{13,5},{1,9},{5,13},{10,2},{14,6},... | collective-permute-start | bytes 1179656 | tf_op jit(solution)/shard_map/ppermute | solution.py:290
  8.7 13.2 %collective-permute-start.1 = (bf16[1,64,512]{2,1,0:T(8,128)(2,1)S(1)}, bf16[1,64,512]{2,1,0:T(8,128)(2,1)S(1)}, u32[]{:S(2)}, u32[]{:S(2)}) collective-permute-start(bf16[1,64,512]{2,1,0:T(8,128)(2,1)S(1)} %collective-permute-done.refs_1_), channel_id=1, source_target_pairs={{0,16},{16,0},{1,17},{17,1},{2,18},{18,2},{3,19},{19,3},{4,20},{20... | collective-permute-start | bytes 196616 | tf_op jit(solution)/shard_map/ppermute | solution.py:316
  17.7 4.3 %collective-permute-start.3 = (bf16[1,64,512]{2,1,0:T(8,128)(2,1)S(1)}, bf16[1,64,512]{2,1,0:T(8,128)(2,1)S(1)}, u32[]{:S(2)}, u32[]{:S(2)}) collective-permute-start(bf16[1,64,512]{2,1,0:T(8,128)(2,1)S(1)} %collective-permute-done.2.refs_4_), channel_id=1, source_target_pairs={{0,16},{16,0},{1,17},{17,1},{2,18},{18,2},{3,19},{19,3},{4,20},{20... | collective-permute-start | bytes 196616 | tf_op jit(solution)/shard_map/ppermute | solution.py:316
  20.0 0.7 %copy-start = (f32[12,8]{0,1:T(8,128)S(1)}, f32[12,8]{0,1:T(8,128)}, u32[]{:S(2)}) copy-start(f32[12,8]{0,1:T(8,128)} %param.9) | copy-start | bytes 1156
  28.4 4.0 %collective-permute-start.6 = (f32[2,12,256]{2,1,0:T(8,128)S(1)}, f32[2,12,256]{2,1,0:T(8,128)S(1)}, u32[]{:S(2)}, u32[]{:S(2)}) collective-permute-start(f32[2,12,256]{2,1,0:T(8,128)S(1)} %get-tuple-element.56), channel_id=1, source_target_pairs={{4,0},{0,4},{12,8},{8,12},{5,1},{1,5},{13,9},{9,13},{6,2},{2,6},{1... | collective-permute-start | bytes 73736 | tf_op jit(solution)/shard_map/ppermute | solution.py:290
  35.4 7.4 %collective-permute-start.8 = (f16[144,256]{1,0:T(8,128)(2,1)S(1)}, f16[144,256]{1,0:T(8,128)(2,1)S(1)}, u32[]{:S(2)}, u32[]{:S(2)}) collective-permute-start(f16[144,256]{1,0:T(8,128)(2,1)S(1)} %convert_element_type.41), channel_id=1, source_target_pairs={{0,8},{4,12},{8,0},{12,4},{16,24},{20,28},{24,16},{28,20},{1,9},{5... | collective-permute-start | bytes 221192 | tf_op jit(solution)/shard_map/ppermute | solution.py:298
  37.1 9.8 %collective-permute-start.9 = (f32[16,128]{1,0:T(8,128)S(1)}, f32[16,128]{1,0:T(8,128)S(1)}, u32[]{:S(2)}, u32[]{:S(2)}) collective-permute-start(f32[16,128]{1,0:T(8,128)S(1)} %get-tuple-element.68), channel_id=1, source_target_pairs={{12,0},{8,4},{4,8},{0,12},{13,1},{9,5},{5,9},{1,13},{14,2},{10,6},... | collective-permute-start | bytes 24584 | tf_op jit(solution)/shard_map/ppermute | solution.py:290
  38.2 11.4 %collective-permute-start.14 = (f16[128,256]{1,0:T(8,128)(2,1)S(1)}, f16[128,256]{1,0:T(8,128)(2,1)S(1)}, u32[]{:S(2)}, u32[]{:S(2)}) collective-permute-start(f16[128,256]{1,0:T(8,128)(2,1)S(1)} %convert_element_type.50), channel_id=1, source_target_pairs={{0,20},{4,16},{8,28},{12,24},{16,4},{20,0},{24,12},{28,8},{1,21},{... | collective-permute-start | bytes 196616 | tf_op jit(solution)/shard_map/ppermute | solution.py:298
  40.1 9.5 %collective-permute-start.13 = (f16[128,256]{1,0:T(8,128)(2,1)S(1)}, f16[128,256]{1,0:T(8,128)(2,1)S(1)}, u32[]{:S(2)}, u32[]{:S(2)}) collective-permute-start(f16[128,256]{1,0:T(8,128)(2,1)S(1)} %convert_element_type.46), channel_id=1, source_target_pairs={{0,24},{4,28},{8,16},{12,20},{16,8},{20,12},{24,0},{28,4},{1,25},{... | collective-permute-start | bytes 196616 | tf_op jit(solution)/shard_map/ppermute | solution.py:298
  42.5 4.4 %collective-permute-start.7 = (f16[144,256]{1,0:T(8,128)(2,1)S(1)}, f16[144,256]{1,0:T(8,128)(2,1)S(1)}, u32[]{:S(2)}, u32[]{:S(2)}) collective-permute-start(f16[144,256]{1,0:T(8,128)(2,1)S(1)} %convert_element_type.39), channel_id=1, source_target_pairs={{0,4},{4,0},{8,12},{12,8},{16,20},{20,16},{24,28},{28,24},{1,5},{5... | collective-permute-start | bytes 221192 | tf_op jit(solution)/shard_map/ppermute | solution.py:298
  42.8 6.8 %collective-permute-start.12 = (f16[256,256]{1,0:T(8,128)(2,1)S(1)}, f16[256,256]{1,0:T(8,128)(2,1)S(1)}, u32[]{:S(2)}, u32[]{:S(2)}) collective-permute-start(f16[256,256]{1,0:T(8,128)(2,1)S(1)} %convert_element_type.44), channel_id=1, source_target_pairs={{0,16},{4,20},{8,24},{12,28},{16,0},{20,4},{24,8},{28,12},{1,17},{... | collective-permute-start | bytes 393224 | tf_op jit(solution)/shard_map/ppermute | solution.py:298
  46.9 1.2 %collective-permute-start.10 = (f32[16,128]{1,0:T(8,128)S(1)}, f32[16,128]{1,0:T(8,128)S(1)}, u32[]{:S(2)}, u32[]{:S(2)}) collective-permute-start(f32[16,128]{1,0:T(8,128)S(1)} %fusion.2), channel_id=1, source_target_pairs={{0,1},{1,0},{2,3},{3,2},{4,5},{5,4},{6,7},{7,6},{8,9},{9,8},{10,11... | collective-permute-start | bytes 24584 | tf_op jit(solution)/shard_map/ppermute | solution.py:419
  48.1 3.7 %collective-permute-start.11 = (f32[16,128]{1,0:T(8,128)S(1)}, f32[16,128]{1,0:T(8,128)S(1)}, u32[]{:S(2)}, u32[]{:S(2)}) collective-permute-start(f32[16,128]{1,0:T(8,128)S(1)} %add.41.mine), channel_id=1, source_target_pairs={{0,2},{1,3},{2,0},{3,1},{4,6},{5,7},{6,4},{7,5},{8,10},{9,11},{10,... | collective-permute-start | bytes 24584 | tf_op jit(solution)/shard_map/ppermute | solution.py:419
